TPU v7x, 32 devices: a whole 2x2x4 slice. The times are simulated.
32 devices in a mesh: dp: 4 (over x, core), fsdp: 8 (over z, y).
Axes of the slice: x: 2, y: 2, z: 4, core: 2. Of those that a mesh axis runs over, the one named last changes fastest.
Arguments:
- layer_input: bfloat16 [376832, 512], P(('dp', 'fsdp')), may hold values from -6 to 6
- cotangent: bfloat16 [376832, 512], P(('dp', 'fsdp')), may hold values from -6 to 6
- shape_points: int32 [64], replicated, may hold values from 1 to 11776, 376832 in all
- shape_category: int32 [64], replicated, may hold values from 0 to 12
- category_counts: int32 [13], replicated, may hold values from 1 to 8
- dir_a: bfloat16 [512, 512], P(('dp', 'fsdp')), may hold values from -0.25 to 0.25
- gain_a: bfloat16 [512], P(('dp', 'fsdp')), may hold values from 0.5 to 1.5
- bias_a: bfloat16 [512], P(('dp', 'fsdp')), may hold values from -1.5 to 1.5
- dir_b: bfloat16 [512, 512], P(('dp', 'fsdp')), may hold values from -0.25 to 0.25
- gain_b: bfloat16 [512], P(('dp', 'fsdp')), may hold values from 0.5 to 1.5
- bias_b: bfloat16 [512], P(('dp', 'fsdp')), may hold values from -1.5 to 1.5
Outputs:
- layer_output: bfloat16 [376832, 512], P(('dp', 'fsdp'))
- input_grad: bfloat16 [376832, 512], P(('dp', 'fsdp'))
- dir_a_grad: float32 [512, 512], P(('dp', 'fsdp'))
- gain_a_grad: float32 [512], P(('dp', 'fsdp'))
- bias_a_grad: float32 [512], P(('dp', 'fsdp'))
- dir_b_grad: float32 [512, 512], P(('dp', 'fsdp'))
- gain_b_grad: float32 [512], P(('dp', 'fsdp'))
- bias_b_grad: float32 [512], P(('dp', 'fsdp'))
Inputs may be any that keep to these rules, and one draw needn't show every extreme that they name: `shape_points`: sums to 376832; the largest shape has exactly 11776 points.
All inputs are finite; a program needn't handle non-finite values.
Results may differ from a plain program's by a relative error of at most 0.0079.
Values may be sent and summed in bfloat16 or wider, within the bound.
No kernel may reach another device: no remote copies, remote signals or barrier semaphores. Data moves between devices by JAX's collectives and lax.ppermute only.
A program may use at most 256 MiB of HBM per device.

v0:
```python
import jax
import jax.numpy as jnp
from jax import lax
from jax.sharding import PartitionSpec as P

MICRO = 4


EPS = 1e-06


def prepare(pieces):
    direction, gain, bias = pieces
    dir_full = direction.astype(jnp.float32)
    gain_full = gain.astype(jnp.float32)
    norm_inv = lax.rsqrt(jnp.sum(dir_full * dir_full, axis=0) + EPS)
    weight = (gain_full * norm_inv * dir_full).astype(jnp.bfloat16)
    return (weight, norm_inv, bias.astype(jnp.float32), dir_full, gain_full)


def slope(value):
    sig = jax.nn.sigmoid(value)
    return sig * (1.0 + value * (1.0 - sig))


def outer_sum(left, right):
    return lax.dot_general(
        left, right, (((0,), (0,)), ((), ())), preferred_element_type=jnp.float32
    )


def back_dot(grad, weight):
    return lax.dot_general(
        grad, weight, (((1,), (1,)), ((), ())), preferred_element_type=jnp.float32
    )


def norm_back(grad_weight, layer):
    weight, norm_inv, bias, dir_full, gain_full = layer
    inner = jnp.sum(grad_weight * dir_full, axis=0)
    gain_grad = norm_inv * inner
    dir_grad = (
        gain_full * norm_inv * grad_weight
        - gain_full * norm_inv * norm_inv * norm_inv * inner * dir_full
    )
    return (dir_grad, gain_grad)


def run_forward(rows, layer_a, layer_b):
    pre_a = jnp.dot(rows, layer_a[0], preferred_element_type=jnp.float32) + layer_a[2]
    hidden = jax.nn.silu(pre_a).astype(jnp.bfloat16)
    pre_b = jnp.dot(hidden, layer_b[0], preferred_element_type=jnp.float32) + layer_b[2]
    return (pre_a, hidden, pre_b)


def body(
    layer_input,
    cotangent,
    shape_points,
    shape_category,
    category_counts,
    dir_a,
    gain_a,
    bias_a,
    dir_b,
    gain_b,
    bias_b,
):
    groups = lax.axis_size(("dp", "fsdp"))
    rows_dev = layer_input.shape[0]
    shapes = shape_points.shape[0]
    cats = category_counts.shape[0]
    average = groups * rows_dev // shapes
    picked = shape_category[:, None] == jnp.arange(cats, dtype=jnp.int32)[None, :]
    counts = jnp.sum(jnp.where(picked, category_counts[None, :], 0), axis=1).astype(jnp.float32)
    shape_weight = (
        counts * (average / 4.0) / jnp.maximum(shape_points, average // 2).astype(jnp.float32)
    )
    ends = jnp.cumsum(shape_points)
    starts = ends - shape_points
    offset = lax.axis_index(("dp", "fsdp")) * rows_dev
    rows = rows_dev // MICRO
    width = layer_input.shape[1]
    outputs = []
    for micro in range(MICRO):
        layer_a = prepare(
            (
                lax.all_gather(dir_a, ("dp", "fsdp"), axis=0, tiled=True),
                lax.all_gather(gain_a, ("dp", "fsdp"), axis=0, tiled=True),
                lax.all_gather(bias_a, ("dp", "fsdp"), axis=0, tiled=True),
            )
        )
        layer_b = prepare(
            (
                lax.all_gather(dir_b, ("dp", "fsdp"), axis=0, tiled=True),
                lax.all_gather(gain_b, ("dp", "fsdp"), axis=0, tiled=True),
                lax.all_gather(bias_b, ("dp", "fsdp"), axis=0, tiled=True),
            )
        )
        block = layer_input[micro * rows : (micro + 1) * rows]
        pre_a, hidden, pre_b = run_forward(block, layer_a, layer_b)
        outputs.append(jax.nn.silu(pre_b).astype(jnp.bfloat16))
    grad_wa = jnp.zeros((width, width), jnp.float32)
    grad_wb = jnp.zeros((width, width), jnp.float32)
    grad_ba = jnp.zeros((width,), jnp.float32)
    grad_bb = jnp.zeros((width,), jnp.float32)
    input_grads = []
    for micro in range(MICRO):
        both = (
            lax.all_gather(dir_a, ("dp", "fsdp"), axis=0, tiled=True),
            lax.all_gather(gain_a, ("dp", "fsdp"), axis=0, tiled=True),
            lax.all_gather(bias_a, ("dp", "fsdp"), axis=0, tiled=True),
            lax.all_gather(dir_b, ("dp", "fsdp"), axis=0, tiled=True),
            lax.all_gather(gain_b, ("dp", "fsdp"), axis=0, tiled=True),
            lax.all_gather(bias_b, ("dp", "fsdp"), axis=0, tiled=True),
        )
        layer_a = prepare(both[0:3])
        layer_b = prepare(both[3:6])
        block = layer_input[micro * rows : (micro + 1) * rows]
        pre_a, hidden, pre_b = run_forward(block, layer_a, layer_b)
        position = offset + micro * rows + jnp.arange(rows, dtype=jnp.int32)
        inside = (position[:, None] >= starts[None, :]) & (position[:, None] < ends[None, :])
        point_weight = jnp.sum(jnp.where(inside, shape_weight[None, :], 0.0), axis=1)
        weighted = (
            cotangent[micro * rows : (micro + 1) * rows].astype(jnp.float32) * point_weight[:, None]
        )
        grad_pre_b = (weighted * slope(pre_b)).astype(jnp.bfloat16)
        grad_wb = grad_wb + outer_sum(hidden, grad_pre_b)
        grad_bb = grad_bb + jnp.sum(grad_pre_b.astype(jnp.float32), axis=0)
        grad_hidden = back_dot(grad_pre_b, layer_b[0])
        grad_pre_a = (grad_hidden * slope(pre_a)).astype(jnp.bfloat16)
        input_grads.append(back_dot(grad_pre_a, layer_a[0]).astype(jnp.bfloat16))
        grad_wa = grad_wa + outer_sum(block, grad_pre_a)
        grad_ba = grad_ba + jnp.sum(grad_pre_a.astype(jnp.float32), axis=0)
    dir_grad_a, gain_grad_a = norm_back(grad_wa, layer_a)
    dir_grad_b, gain_grad_b = norm_back(grad_wb, layer_b)
    shares = (
        lax.psum_scatter(dir_grad_a, ("dp", "fsdp"), scatter_dimension=0, tiled=True),
        lax.psum_scatter(gain_grad_a, ("dp", "fsdp"), scatter_dimension=0, tiled=True),
        lax.psum_scatter(grad_ba, ("dp", "fsdp"), scatter_dimension=0, tiled=True),
        lax.psum_scatter(dir_grad_b, ("dp", "fsdp"), scatter_dimension=0, tiled=True),
        lax.psum_scatter(gain_grad_b, ("dp", "fsdp"), scatter_dimension=0, tiled=True),
        lax.psum_scatter(grad_bb, ("dp", "fsdp"), scatter_dimension=0, tiled=True),
    )
    layer_output = jnp.concatenate(outputs, axis=0)
    input_grad = jnp.concatenate(input_grads, axis=0)
    return (
        layer_output,
        input_grad,
        shares[0],
        shares[1],
        shares[2],
        shares[3],
        shares[4],
        shares[5],
    )


def solution(mesh):
    in_specs = (
        P(("dp", "fsdp"), None),
        P(("dp", "fsdp"), None),
        P(),
        P(),
        P(),
        P(("dp", "fsdp"), None),
        P(("dp", "fsdp")),
        P(("dp", "fsdp")),
        P(("dp", "fsdp"), None),
        P(("dp", "fsdp")),
        P(("dp", "fsdp")),
    )
    out_specs = (
        P(("dp", "fsdp"), None),
        P(("dp", "fsdp"), None),
        P(("dp", "fsdp"), None),
        P(("dp", "fsdp")),
        P(("dp", "fsdp")),
        P(("dp", "fsdp"), None),
        P(("dp", "fsdp")),
        P(("dp", "fsdp")),
    )
    return jax.shard_map(body, mesh=mesh, in_specs=in_specs, out_specs=out_specs, check_vma=False)
```

profile of v0, /device:TPU:0, one launch (start us, length us, event | category | flops | bytes accessed | tf_op | source)
XLA Modules:
  0.0 575.0 jit_solution(11885077633863281385)
XLA Ops:
  7.2 72.8 %all_gather.13 = bf16[512,512]{1,0:T(8,128)(2,1)S(1)} all-gather(bf16[16,512]{1,0:T(8,128)(2,1)} %param.16), channel_id=1, replica_groups=mesh['dp'=4,'fsdp'=8] {'dp','fsdp'}, dimensions={0}, use_global_device_ids=true | all-gather | bytes 540672 | tf_op jit(solution)/shard_map/all_gather | solution.py:88
  80.2 0.9 dynamic-update-slice
  81.9 0.8 dynamic-update-slice.2
  82.8 0.8 dynamic-update-slice.3
  83.6 36.9 %all-reduce.9 = (bf16[512]{0:T(512)(128)(2,1)S(1)}, bf16[512]{0:T(512)(128)(2,1)S(1)}, bf16[512]{0:T(512)(128)(2,1)S(1)}, bf16[512]{0:T(512)(128)(2,1)S(1)}) all-reduce(bf16[512]{0:T(512)(128)(2,1)S(1)} %dynamic-update-slice, bf16[512]{0:T(512)(128)(2,1)S(1)} %dynamic-update-slice.1, ...), channel_id=1, replica_groups=mesh['dp'=4,'fsdp'=8] {'dp','fsdp'}, use_global_device_ids=true, to_apply=%add | all-reduce | flops 2048 | bytes 8192
  120.5 6.3 %fusion.34 = f32[512,2944]{1,0:T(8,128)} fusion(bf16[11776,512]{1,0:T(8,128)(2,1)} %param.11, bf16[512,512]{1,0:T(8,128)(2,1)S(1)} %all_gather.13, f32[512]{0:T(512)S(1)} %convert_multiply_fusion.9), kind=kOutput, calls=%fused_computation.72 | convolution fusion | flops 1544290304 | bytes 9570304 | tf_op jit(solution)/shard_map/dot_general | solution.py:50
  126.9 6.3 %fusion.38 = f32[512,2944]{1,0:T(8,128)} fusion(bf16[11776,512]{1,0:T(8,128)(2,1)} %param.11, bf16[512,512]{1,0:T(8,128)(2,1)S(1)} %all_gather.13, f32[512]{0:T(512)S(1)} %convert_multiply_fusion.9), kind=kOutput, calls=%fused_computation.76 | convolution fusion | flops 1544290304 | bytes 9570304 | tf_op jit(solution)/shard_map/dot_general | solution.py:50
  133.2 3.7 fusion.42
  136.9 69.2 %all_gather.16 = bf16[512,512]{1,0:T(8,128)(2,1)S(1)} all-gather(bf16[16,512]{1,0:T(8,128)(2,1)S(1)} %copy-done.20), channel_id=1, replica_groups=mesh['dp'=4,'fsdp'=8] {'dp','fsdp'}, dimensions={0}, use_global_device_ids=true | all-gather | bytes 540672 | tf_op jit(solution)/shard_map/all_gather | solution.py:95
  206.3 15.5 %fusion.27 = (bf16[2944,512]{0,1:T(8,128)(2,1)}, bf16[2944,512]{0,1:T(8,128)(2,1)}, bf16[2944,512]{0,1:T(8,128)(2,1)}, bf16[2944,512]{0,1:T(8,128)(2,1)}, f32[512,2944]{1,0:T(8,128)}) fusion(f32[512]{0:T(512)S(1)} %convert_element_type.87, f32[512,2944]{1,0:T(8,128)S(1)} %fusion.42, f32[512,2944]{1,0:T(8,128)} %fusion.38, f32[512,2944]{1,0:T(8,128)} %fusion.34, ...), kind=kOutput, calls=%fused_computation.41 | convolution fusion | flops 1580466176 | bytes 39718912 | tf_op jit(solution)/shard_map/dot_general | solution.py:50
  221.8 6.4 %fusion.72 = f32[2944,512]{0,1:T(8,128)} fusion(bf16[2944,512]{0,1:T(8,128)(2,1)} %get-tuple-element.84, bf16[512,512]{1,0:T(8,128)(2,1)S(1)} %all_gather.16, f32[512]{0:T(512)S(1)} %convert_multiply_fusion.8), kind=kOutput, calls=%fused_computation.113 | convolution fusion | flops 1544290304 | bytes 9570304 | tf_op jit(solution)/shard_map/dot_general | solution.py:52
  228.2 4.4 fusion.74
  232.7 4.4 fusion.76
  239.8 8.3 %fusion.92 = (bf16[2944,512]{1,0:T(8,128)(2,1)}, bf16[2944,512]{1,0:T(8,128)(2,1)}, bf16[2944,512]{1,0:T(8,128)(2,1)}, bf16[2944,512]{1,0:T(8,128)(2,1)S(1)}) fusion(bf16[11776,512]{1,0:T(8,128)(2,1)} %param.12), kind=kLoop, calls=%fused_computation.136 | loop fusion | bytes 24117248 | tf_op jit(solution)/shard_map/slice | solution.py:125
  248.0 4.6 copy.83
  252.6 4.6 copy.84
  257.2 4.6 copy.85
  261.9 3.0 copy.86
  264.9 1.3 select_reduce_fusion.3
  266.3 22.9 %convert_reduce_fusion.3 = (f32[512]{0:T(512)}, bf16[2944,512]{0,1:T(8,128)(2,1)S(1)}, bf16[2944,512]{0,1:T(8,128)(2,1)S(1)}, bf16[2944,512]{0,1:T(8,128)(2,1)},...) fusion(f32[512]{0:T(512)} %convert_element_type.92, ...), kind=kOutput, calls=%fused_computation.49 | convolution fusion | flops 1640757248 | bytes 57862144 | tf_op jit(solution)/shard_map/dot_general | solution.py:52
  289.1 1.8 fusion.93
  291.0 2.3 copy-done.7
  293.2 1.8 convolution_add_fusion.2
  295.1 1.0 copy-done.5
  296.1 1.8 convolution_add_fusion.1
  297.9 1.8 fusion.66
  299.8 1.2 fusion.67
  301.1 6.7 %convert_reduce_fusion.4 = (f32[512]{0:T(512)}, bf16[2944,512]{0,1:T(8,128)(2,1)S(1)}) fusion(f32[512,2944]{1,0:T(8,128)} %fusion.34, f32[512]{0:T(512)S(1)} %copy-done.35, bf16[2944,512]{0,1:T(8,128)(2,1)} %copy-done.39, bf16[512,512]{1,0:T(8,128)(2,1)S(1)} %all_gather.16, f32[512]{0:T(512)S(1)} %convert_multiply_fusion.8), kind=kOutput, calls=%fused_computation.50 | convolution fusion | flops 1562377728 | bytes 12589056 | tf_op jit(solution)/shard_map/dot_general | solution.py:33
  307.9 6.8 %convert_reduce_fusion.5 = (f32[512]{0:T(512)}, bf16[2944,512]{0,1:T(8,128)(2,1)S(1)}) fusion(f32[512,2944]{1,0:T(8,128)} %fusion.38, f32[512]{0:T(512)S(1)} %copy-done.35, bf16[2944,512]{0,1:T(8,128)(2,1)S(1)} %copy-done.50, bf16[512,512]{1,0:T(8,128)(2,1)S(1)} %all_gather.16, f32[512]{0:T(512)S(1)} %convert_multiply_fusion.8), kind=kOutput, calls=%fused_computation.51 | convolution fusion | flops 1562377728 | bytes 12589056 | tf_op jit(solution)/shard_map/dot_general | solution.py:33
  314.7 6.8 %convert_reduce_fusion.6 = (f32[512]{0:T(512)}, bf16[2944,512]{0,1:T(8,128)(2,1)S(1)}) fusion(f32[512,2944]{1,0:T(8,128)} %copy-done.2, f32[512]{0:T(512)S(1)} %copy-done.35, bf16[2944,512]{0,1:T(8,128)(2,1)S(1)} %copy-done.48, bf16[512,512]{1,0:T(8,128)(2,1)S(1)} %all_gather.16, f32[512]{0:T(512)S(1)} %convert_multiply_fusion.8), kind=kOutput, calls=%fused_computation.52 | convolution fusion | flops 1562377728 | bytes 12589056 | tf_op jit(solution)/shard_map/dot_general | solution.py:33
  321.6 4.0 convert_reduce_fusion.7
  325.6 1.8 fusion.32
  327.5 1.8 fusion.36
  329.3 1.8 fusion.40
  331.2 2.0 fusion.62
  333.3 1.2 fusion.63
  334.5 5.4 convolution_convert_fusion.3
  340.0 3.5 convolution_convert_fusion
  343.5 3.6 convolution_convert_fusion.1
  347.1 1.1 copy-done.10
  348.2 8.9 %pad_maximum_fusion = bf16[11776,512]{0,1:T(8,128)(2,1)} fusion(bf16[2944,512]{0,1:T(8,128)(2,1)S(1)} %copy-done.10, bf16[2944,512]{0,1:T(8,128)(2,1)S(1)} %copy-done.9, bf16[2944,512]{0,1:T(8,128)(2,1)S(1)} %copy-done.8, bf16[2944,512]{0,1:T(8,128)(2,1)S(1)} %get-tuple-element.64), kind=kLoop, calls=%fused_computation | loop fusion | flops 48234496 | bytes 24117248 | tf_op jit(solution)/shard_map/concatenate | solution.py:145
  357.1 37.1 %all-reduce.8 = (f32[512]{0:T(512)S(1)}, f32[512]{0:T(512)S(1)}, f32[512]{0:T(512)S(1)}, f32[512]{0:T(512)S(1)}) all-reduce(f32[512]{0:T(512)S(1)} %get-tuple-element.70, f32[512]{0:T(512)S(1)} %add_add_fusion.1, f32[512]{0:T(512)S(1)} %get-tuple-element.69, ...), channel_id=3, replica_groups=mesh['dp'=4,'fsdp'=8] {'dp','fsdp'}, use_global_device_ids=true, to_apply=%region_10.11.clone | all-reduce | flops 2048 | bytes 16384
  396.6 16.5 %copy.74 = bf16[11776,512]{1,0:T(8,128)(2,1)} copy(bf16[11776,512]{0,1:T(8,128)(2,1)} %pad_maximum_fusion) | data formatting | bytes 24117248
  413.1 1.8 convolution_convert_fusion.2
  414.9 0.9 copy-done.12
  415.9 0.9 copy-done.13
  416.7 66.5 %pad_maximum_fusion.1 = bf16[11776,512]{1,0:T(8,128)(2,1)} fusion(bf16[2944,512]{1,0:T(8,128)(2,1)S(1)} %copy-done.12, bf16[2944,512]{1,0:T(8,128)(2,1)S(1)} %copy-done.13, bf16[2944,512]{1,0:T(8,128)(2,1)S(1)} %convolution_convert_fusion.2, bf16[2944,512]{1,0:T(8,128)(2,1)S(1)} %copy-done.11), kind=kLoop, calls=%fused_computation.1 | loop fusion | flops 48234496 | bytes 24117248 | tf_op jit(solution)/shard_map/concatenate | solution.py:146
  483.2 84.5 %reduce-scatter.3.cloned.1.call-done = f32[16,512]{1,0:T(8,128)} async-done(((f32[512,512]{1,0:T(8,128)}), f32[16,512]{1,0:T(8,128)}) %reduce-scatter.3.cloned.1.call-update) | async-done | bytes 32784 | tf_op jit(solution)/shard_map/reduce_scatter | solution.py:138
  (147 shorter events, 6.5 us)
Async XLA Ops:
  7.2 476.1 %reduce-scatter.5.cloned.1.call-start = ((), (), s32[]{:S(2)}) async-start(), calls=%async_computation.3 | async-start | bytes 1081344 | tf_op jit(solution)/shard_map/reduce_scatter | solution.py:141
  80.0 126.2 %copy-start = (bf16[512,512]{1,0:T(8,128)(2,1)}, bf16[512,512]{1,0:T(8,128)(2,1)S(1)}, u32[]{:S(2)}) copy-start(bf16[512,512]{1,0:T(8,128)(2,1)S(1)} %all_gather.13) | copy-start | bytes 1572868
  80.2 53.0 %copy-start.16 = (f32[512]{0:T(512)}, f32[512]{0:T(512)S(1)}, u32[]{:S(2)}) copy-start(f32[512]{0:T(512)S(1)} %fusion.60) | copy-start | bytes 6148
  120.5 12.7 %copy-start.21 = (bf16[512]{0:T(512)(128)(2,1)}, bf16[512]{0:T(512)(128)(2,1)S(1)}, u32[]{:S(2)}) copy-start(bf16[512]{0:T(512)(128)(2,1)S(1)} %get-tuple-element.48) | copy-start | bytes 3076
  120.5 85.7 %copy-start.23 = (bf16[512]{0:T(512)(128)(2,1)}, bf16[512]{0:T(512)(128)(2,1)S(1)}, u32[]{:S(2)}) copy-start(bf16[512]{0:T(512)(128)(2,1)S(1)} %get-tuple-element.50) | copy-start | bytes 3076
  120.5 85.8 %copy-start.14 = (f32[512]{0:T(512)}, f32[512]{0:T(512)S(1)}, u32[]{:S(2)}) copy-start(f32[512]{0:T(512)S(1)} %convert_multiply_fusion.9) | copy-start | bytes 6148
  133.2 3.7 copy-start.20
  136.9 84.9 %copy-start.2 = (f32[512,2944]{1,0:T(8,128)}, f32[512,2944]{1,0:T(8,128)S(1)}, u32[]{:S(2)}) copy-start(f32[512,2944]{1,0:T(8,128)S(1)} %fusion.42) | copy-start | bytes 18087940
  136.9 84.8 %copy-start.34 = (f32[512]{0:T(512)}, f32[512]{0:T(512)S(1)}, u32[]{:S(2)}) copy-start(f32[512]{0:T(512)S(1)} %convert_element_type.87) | copy-start | bytes 6148
  206.3 15.5 %copy-start.18 = (f32[512]{0:T(512)}, f32[512]{0:T(512)S(1)}, u32[]{:S(2)}) copy-start(f32[512]{0:T(512)S(1)} %fusion.64) | copy-start | bytes 6148
  221.8 6.5 %copy-start.4 = (bf16[2944,512]{0,1:T(8,128)(2,1)S(1)}, bf16[2944,512]{0,1:T(8,128)(2,1)}, u32[]{:S(2)}) copy-start(bf16[2944,512]{0,1:T(8,128)(2,1)} %get-tuple-element.83) | copy-start | bytes 9043972
  228.2 4.5 copy-start.6
  232.7 5.0 copy-start.36
  232.7 5.9 %copy-start.37 = (s32[13]{0:T(128)S(1)}, s32[13]{0:T(128)}, u32[]{:S(2)}) copy-start(s32[13]{0:T(128)} %param.15) | copy-start | bytes 160
  232.7 5.9 %copy-start.38 = (s32[64]{0:T(128)S(1)}, s32[64]{0:T(128)}, u32[]{:S(2)}) copy-start(s32[64]{0:T(128)} %param.14) | copy-start | bytes 772
  266.2 22.9 %copy-start.51 = (bf16[2944,512]{0,1:T(8,128)(2,1)S(1)}, bf16[2944,512]{0,1:T(8,128)(2,1)}, u32[]{:S(2)}) copy-start(bf16[2944,512]{0,1:T(8,128)(2,1)} %get-tuple-element.81) | copy-start | bytes 9043972
  289.1 5.9 %copy-start.47 = (bf16[2944,512]{0,1:T(8,128)(2,1)}, bf16[2944,512]{0,1:T(8,128)(2,1)S(1)}, u32[]{:S(2)}) copy-start(bf16[2944,512]{0,1:T(8,128)(2,1)S(1)} %get-tuple-element.74) | copy-start | bytes 9043972
  289.1 5.9 %copy-start.52 = (bf16[2944,512]{0,1:T(8,128)(2,1)}, bf16[2944,512]{0,1:T(8,128)(2,1)S(1)}, u32[]{:S(2)}) copy-start(bf16[2944,512]{0,1:T(8,128)(2,1)S(1)} %get-tuple-element.55) | copy-start | bytes 9043972
  289.1 6.0 %copy-start.49 = (bf16[2944,512]{0,1:T(8,128)(2,1)}, bf16[2944,512]{0,1:T(8,128)(2,1)S(1)}, u32[]{:S(2)}) copy-start(bf16[2944,512]{0,1:T(8,128)(2,1)S(1)} %get-tuple-element.77) | copy-start | bytes 9043972
  289.1 8.8 %copy-start.39 = (bf16[2944,512]{0,1:T(8,128)(2,1)}, bf16[2944,512]{0,1:T(8,128)(2,1)S(1)}, u32[]{:S(2)}) copy-start(bf16[2944,512]{0,1:T(8,128)(2,1)S(1)} %get-tuple-element.80) | copy-start | bytes 9043972
  289.1 4.1 copy-start.7
  291.0 5.1 copy-start.5
  301.1 266.7 %reduce-scatter.3.cloned.1.call-start = ((), (), s32[]{:S(2)}) async-start(), calls=%async_computation.2 | async-start | bytes 1081344 | tf_op jit(solution)/shard_map/reduce_scatter | solution.py:138
  301.1 6.7 %copy-start.50 = (bf16[2944,512]{0,1:T(8,128)(2,1)S(1)}, bf16[2944,512]{0,1:T(8,128)(2,1)}, u32[]{:S(2)}) copy-start(bf16[2944,512]{0,1:T(8,128)(2,1)} %copy-done.49) | copy-start | bytes 9043972
  307.9 17.7 %copy-start.42 = (bf16[2944,512]{0,1:T(8,128)(2,1)}, bf16[2944,512]{0,1:T(8,128)(2,1)S(1)}, u32[]{:S(2)}) copy-start(bf16[2944,512]{0,1:T(8,128)(2,1)S(1)} %get-tuple-element.89) | copy-start | bytes 9043972
  307.9 6.8 %copy-start.48 = (bf16[2944,512]{0,1:T(8,128)(2,1)S(1)}, bf16[2944,512]{0,1:T(8,128)(2,1)}, u32[]{:S(2)}) copy-start(bf16[2944,512]{0,1:T(8,128)(2,1)} %copy-done.47) | copy-start | bytes 9043972
  307.9 13.7 %slice-start.3 = ((s8[6029312]{0:T(1024)(128)(4,1)}), s8[4194304]{0:T(1024)(128)(4,1)S(1)}, s32[]{:S(2)}) async-start(s8[6029312]{0:T(1024)(128)(4,1)} %bitcast.126), calls=%async_computation.7 | async-start | bytes 8388608
  314.7 12.8 %copy-start.44 = (bf16[2944,512]{0,1:T(8,128)(2,1)}, bf16[2944,512]{0,1:T(8,128)(2,1)S(1)}, u32[]{:S(2)}) copy-start(bf16[2944,512]{0,1:T(8,128)(2,1)S(1)} %get-tuple-element.91) | copy-start | bytes 9043972
  314.7 6.8 %copy-start.53 = (bf16[2944,512]{0,1:T(8,128)(2,1)S(1)}, bf16[2944,512]{0,1:T(8,128)(2,1)}, u32[]{:S(2)}) copy-start(bf16[2944,512]{0,1:T(8,128)(2,1)} %copy-done.52) | copy-start | bytes 9043972
  314.7 6.8 %slice-start.4 = ((s8[6029312]{0:T(1024)(128)(4,1)}), s8[1835008]{0:T(1024)(128)(4,1)S(1)}, s32[]{:S(2)}) async-start(s8[6029312]{0:T(1024)(128)(4,1)} %bitcast.126), calls=%async_computation.8 | async-start | bytes 3670016
  314.7 10.9 %slice-start = ((s8[12058624]{0:T(1024)(128)(4,1)}), s8[4194304]{0:T(1024)(128)(4,1)S(1)}, s32[]{:S(2)}) async-start(s8[12058624]{0:T(1024)(128)(4,1)} %bitcast.123), calls=%async_computation.4 | async-start | bytes 8388608
  314.7 10.9 %slice-start.1 = ((s8[12058624]{0:T(1024)(128)(4,1)}), s8[4194304]{0:T(1024)(128)(4,1)S(1)}, s32[]{:S(2)}) async-start(s8[12058624]{0:T(1024)(128)(4,1)} %bitcast.123), calls=%async_computation.5 | async-start | bytes 8388608
  321.5 7.8 %copy-start.40 = (bf16[2944,512]{0,1:T(8,128)(2,1)}, bf16[2944,512]{0,1:T(8,128)(2,1)S(1)}, u32[]{:S(2)}) copy-start(bf16[2944,512]{0,1:T(8,128)(2,1)S(1)} %get-tuple-element.95) | copy-start | bytes 9043972
  321.5 4.1 slice-start.2
  325.6 5.6 copy-start.46
  334.5 5.5 copy-start.43
  343.4 3.7 copy-start.26
  343.4 3.7 copy-start.27
  343.4 3.7 copy-start.28
  343.4 3.7 copy-start.29
  343.5 3.7 copy-start.8
  343.5 3.7 copy-start.9
  343.5 4.8 copy-start.10
  348.2 8.9 %copy-start.30 = (f32[512]{0:T(512)S(1)}, f32[512]{0:T(512)}, u32[]{:S(2)}) copy-start(f32[512]{0:T(512)} %get-tuple-element.88) | copy-start | bytes 6148
  348.2 8.9 %copy-start.31 = (f32[512]{0:T(512)S(1)}, f32[512]{0:T(512)}, u32[]{:S(2)}) copy-start(f32[512]{0:T(512)} %get-tuple-element.90) | copy-start | bytes 6148
  348.2 8.9 %copy-start.32 = (f32[512]{0:T(512)S(1)}, f32[512]{0:T(512)}, u32[]{:S(2)}) copy-start(f32[512]{0:T(512)} %get-tuple-element.94) | copy-start | bytes 6148
  348.2 8.9 %copy-start.33 = (f32[512]{0:T(512)S(1)}, f32[512]{0:T(512)}, u32[]{:S(2)}) copy-start(f32[512]{0:T(512)} %get-tuple-element.92) | copy-start | bytes 6148
  396.6 16.5 %copy-start.41 = (bf16[2944,512]{0,1:T(8,128)(2,1)S(1)}, bf16[2944,512]{0,1:T(8,128)(2,1)}, u32[]{:S(2)}) copy-start(bf16[2944,512]{0,1:T(8,128)(2,1)} %copy-done.40) | copy-start | bytes 9043972
  (13 other events, 30.7 us)
Sparse Core Ops, SparseCore 0:
  301.2 131.9 reduce-scatter.4
  436.1 131.6 reduce-scatter.2
where the time goes:
time: 582 us; the launch traced here: 575 us
  blocking collectives  216 us (37%)
  matrix products  123 us (21%)
  waiting for transfers between devices  84.6 us (15%)
  other arithmetic  82 us (14%)
  local copies, waits for them, and re-layouts  53.8 us (9%)
  between operations  15.1 us (3%)
    reduce_scatter x1, waiting for transfers between devices, body(): lax.psum_scatter(dir_grad_a, ('dp', 'fsdp'), scatter_dimension=0, tiled=T...  84.5 us
    unnamed x2, blocking collectives  74 us
    all_gather x1, blocking collectives, body(): lax.all_gather(dir_a, ('dp', 'fsdp'), axis=0, tiled=True)  72.8 us
    all_gather x1, blocking collectives, body(): lax.all_gather(dir_b, ('dp', 'fsdp'), axis=0, tiled=True)  69.2 us
    concatenate x1, other arithmetic, body(): input_grad = jnp.concatenate(input_grads, axis=0)  66.5 us
    unnamed x135, local copies, waits for them, and re-layouts  45.5 us
    dot_general x8, matrix products, back_dot(): lax.dot_general(grad, weight, (((1,), (1,)), ((), ())), preferred_element...  38.7 us
    dot_general x4, matrix products, run_forward(): jnp.dot(hidden, layer_b[0], preferred_element_type=jnp.float32) + layer_b[2]  38.2 us
  transfers between devices with their start and end apart: 2, of which 1 were waited for; matrix products, arithmetic and copies ran while one was open for 25% of the time, Pallas kernels for 0%

commit v1 on v0

v1 whole, which is shorter than its diff:
```python
import functools

import jax
import jax.numpy as jnp
from jax import lax
from jax.experimental import pallas as pl
from jax.experimental.pallas import tpu as pltpu
from jax.sharding import PartitionSpec as P

AXES = ("dp", "fsdp")
EPS = 1e-06
SLOT = 16
LANES = 128
F32 = jnp.float32
BF16 = jnp.bfloat16
VMEM_BYTES = 60 << 20


def pick_tile(rows):
    for tile in (1472, 736, 512, 368, 256, 128, 64, 32, 16):
        if rows % tile == 0:
            return tile
    return rows


def dot(left, right):
    return jnp.dot(left, right, preferred_element_type=F32)


def point_weight_kernel(average, place_ref, counts_ref, points_ref, category_ref, out_ref, table):
    shapes = points_ref.shape[1]
    points = points_ref[...]
    lane = lax.broadcasted_iota(jnp.int32, points.shape, 1)
    ends = points
    shift = 1
    while shift < shapes:
        ends = ends + jnp.where(lane >= shift, pltpu.roll(ends, shift, 1), 0)
        shift *= 2
    starts = ends - points

    @pl.when(pl.program_id(0) == 0)
    def _():
        count = jnp.zeros(points.shape, jnp.int32)
        for cat in range(counts_ref.shape[0]):
            count = jnp.where(category_ref[...] == cat, counts_ref[cat], count)
        weight = (
            count.astype(F32) * (average / 4.0) / jnp.maximum(points, average // 2).astype(F32)
        )
        square = lax.broadcasted_iota(jnp.int32, (shapes, shapes), 0) == lax.broadcasted_iota(
            jnp.int32, (shapes, shapes), 1
        )
        column = jnp.sum(jnp.where(square, 0.5 * weight[0:1, :], 0.0), axis=1, keepdims=True)
        table[...] = jnp.broadcast_to(column, table.shape).astype(BF16)

    rows = out_ref.shape[0]
    first = place_ref[1] + pl.program_id(0) * rows
    position = first + lax.broadcasted_iota(jnp.int32, (rows, shapes), 0)
    inside = (position >= starts[0:1, :]) & (position < ends[0:1, :])
    out_ref[...] = dot(jnp.where(inside, 1.0, 0.0).astype(BF16), table[...]).astype(BF16)


def point_weights(place, shape_points, shape_category, category_counts, rows, average):
    shapes = shape_points.shape[0]
    padded = -(-shapes // LANES) * LANES
    wide = lambda v: jnp.broadcast_to(jnp.pad(v, (0, padded - shapes))[None, :], (8, padded))
    tile = pick_tile(rows)
    whole = pl.BlockSpec((8, padded), lambda i: (0, 0))
    return pl.pallas_call(
        functools.partial(point_weight_kernel, average),
        grid=(rows // tile,),
        in_specs=[
            pl.BlockSpec(memory_space=pltpu.SMEM),
            pl.BlockSpec(memory_space=pltpu.SMEM),
            whole,
            whole,
        ],
        out_specs=pl.BlockSpec((tile, LANES), lambda i: (i, 0)),
        out_shape=jax.ShapeDtypeStruct((rows, LANES), BF16),
        scratch_shapes=[pltpu.VMEM((padded, LANES), BF16)],
        compiler_params=pltpu.CompilerParams(vmem_limit_bytes=VMEM_BYTES),
        name="point_weight",
    )(place, category_counts, wide(shape_points), wide(shape_category))


def activate(half):
    one = jnp.asarray(1, BF16)
    half = half.astype(BF16)
    bent = jnp.tanh(half)
    lift = one + bent
    value = half * lift
    return value, lift + value * (one - bent)


def layers_kernel(masks, parts, *refs):
    gathered = refs[1:9]
    place_ref = refs[0]
    x_ref, cot_ref, pw_ref = refs[9:12]
    out_ref, in_grad_ref, keep_ref, send_ref = refs[12:16]
    dir_a, dir_b, w_a, w_b, wt_a, wt_b, gw_a, gw_b, vec, gsum = refs[16:26]
    step = pl.program_id(0)
    width = x_ref.shape[1]
    tile = x_ref.shape[0]
    sub = tile // parts

    def owner(slot):
        return place_ref[0] ^ masks[slot]

    @pl.when(step == 0)
    def _():
        lane = lax.broadcasted_iota(jnp.int32, (8, width), 1) // SLOT
        small = jnp.zeros((8, width), F32)
        for slot in range(len(masks)):
            home = owner(slot)
            rows = pl.ds(pl.multiple_of(home * SLOT, SLOT), SLOT)
            block = gathered[slot // 4][slot % 4]
            dir_a[rows, :] = block[:, 0:width]
            dir_b[rows, :] = block[:, width : 2 * width]
            extra = block[:, 2 * width :].astype(F32)[0:8]
            small = jnp.where(
                lane == home, jnp.concatenate([extra] * (width // LANES), axis=1), small
            )
        for k, (direction, w, wt) in enumerate(((dir_a, w_a, wt_a), (dir_b, w_b, wt_b))):
            full = direction[...].astype(F32)
            norm = lax.rsqrt(jnp.sum(full * full, axis=0, keepdims=True) + EPS)
            scale = small[2 * k : 2 * k + 1] * norm
            weight = (scale * full).astype(BF16)
            half = weight * jnp.asarray(0.5, BF16)
            w[...] = half
            wt[...] = (weight if k == 0 else half).T
            vec[3 * k : 3 * k + 1, :] = 0.5 * small[2 * k + 1 : 2 * k + 2]
            vec[3 * k + 1 : 3 * k + 2, :] = scale
            vec[3 * k + 2 : 3 * k + 3, :] = norm
        gw_a[...] = jnp.zeros_like(gw_a)
        gw_b[...] = jnp.zeros_like(gw_b)
        gsum[...] = jnp.zeros_like(gsum)

    spans = [pl.ds(k * sub, sub) for k in range(parts)]
    hidden, slope_a = zip(
        *[activate(dot(x_ref[s, :], w_a[...]) + vec[0:1, :]) for s in spans]
    )
    grads = []
    for s, h in zip(spans, hidden):
        value, slope_b = activate(dot(h, w_b[...]) + vec[3:4, :])
        out_ref[s, :] = value
        weight = jnp.concatenate([pw_ref[s, :]] * (width // LANES), axis=1)
        grads.append((cot_ref[s, :] * weight) * slope_b)
    grads_a = [dot(g, wt_b[...]).astype(BF16) * sa for g, sa in zip(grads, slope_a)]
    for s, g in zip(spans, grads_a):
        in_grad_ref[s, :] = dot(g, wt_a[...]).astype(BF16)
    ones = jnp.ones((SLOT, tile), BF16)
    join = lambda pieces: jnp.concatenate(pieces, axis=0)
    both = dot(join([join(hidden).T, ones]), join(grads))
    gw_b[...] += both[:width]
    gsum[8:16, :] += both[width : width + 8]
    both = dot(join([x_ref[...].T, ones]), join(grads_a))
    gw_a[...] += both[:width]
    gsum[0:8, :] += both[width : width + 8]

    @pl.when(step == pl.num_programs(0) - 1)
    def _():
        small = []
        for k, (direction, gw) in enumerate(((dir_a, gw_a), (dir_b, gw_b))):
            full = direction[...].astype(F32)
            grad = gw[...]
            scale, norm = vec[3 * k + 1 : 3 * k + 2, :], vec[3 * k + 2 : 3 * k + 3, :]
            inner = jnp.sum(grad * full, axis=0, keepdims=True)
            gw[...] = scale * grad - (scale * norm * norm * inner) * full
            small += [norm * inner, gsum[8 * k : 8 * k + 1, :]]
        gsum[0:8, :] = jnp.concatenate(small + [jnp.zeros((4, width), F32)], axis=0)
        for slot in range(len(masks)):
            home = owner(slot)
            rows = pl.ds(pl.multiple_of(home * SLOT, SLOT), SLOT)
            chunk = pl.ds(pl.multiple_of(home * SLOT // LANES * LANES, LANES), LANES)
            extra = pltpu.roll(gsum[0:8, chunk], LANES - home * SLOT % LANES, 1)
            extra = jnp.concatenate([extra, jnp.zeros((8, LANES), F32)], axis=0)
            block = jnp.concatenate([gw_a[rows, :], gw_b[rows, :], extra], axis=1)
            if slot < len(masks) // 2:
                keep_ref[slot] = block
            else:
                send_ref[slot - len(masks) // 2] = block.astype(BF16)


def layers(place, gathered, layer_input, cotangent, weights, masks):
    rows, width = layer_input.shape
    tile = pick_tile(rows)
    parts = 4 if tile % (4 * SLOT) == 0 else 1
    span = 2 * width + LANES
    half = len(masks) // 2
    by_row = lambda w: pl.BlockSpec((tile, w), lambda i: (i, 0))
    whole = lambda *dims: pl.BlockSpec(dims, lambda i: (0,) * len(dims))
    square = lambda dtype: pltpu.VMEM((width, width), dtype)
    return pl.pallas_call(
        functools.partial(layers_kernel, masks, parts),
        grid=(rows // tile,),
        in_specs=[pl.BlockSpec(memory_space=pltpu.SMEM)]
        + [whole(4, SLOT, span)] * 8
        + [by_row(width), by_row(width), by_row(LANES)],
        out_specs=[by_row(width), by_row(width), whole(half, SLOT, span), whole(half, SLOT, span)],
        out_shape=[
            jax.ShapeDtypeStruct((rows, width), BF16),
            jax.ShapeDtypeStruct((rows, width), BF16),
            jax.ShapeDtypeStruct((half, SLOT, span), F32),
            jax.ShapeDtypeStruct((half, SLOT, span), BF16),
        ],
        scratch_shapes=[square(BF16)] * 6
        + [square(F32)] * 2
        + [pltpu.VMEM((8, width), F32), pltpu.VMEM((16, width), F32)],
        compiler_params=pltpu.CompilerParams(vmem_limit_bytes=VMEM_BYTES),
        name="layers",
    )(place, *gathered, layer_input, cotangent, weights)


def swap(value, mask, groups):
    return lax.ppermute(value, AXES, [(k, k ^ mask) for k in range(groups)])


def body(
    layer_input,
    cotangent,
    shape_points,
    shape_category,
    category_counts,
    dir_a,
    gain_a,
    bias_a,
    dir_b,
    gain_b,
    bias_b,
):
    dp, fsdp = lax.axis_size("dp"), lax.axis_size("fsdp")
    groups = dp * fsdp
    rows, width = layer_input.shape
    share = dir_a.shape[0]
    slots = width // SLOT
    average = groups * rows // shape_points.shape[0]
    me = lax.axis_index(AXES).astype(jnp.int32)
    fast = share == SLOT and groups == 32 and fsdp == 8
    small = jnp.stack([gain_a, bias_a, gain_b, bias_b])
    place = jnp.stack([me if fast else jnp.zeros_like(me), me * rows])
    if fast:
        extra = jnp.pad(jnp.tile(small, (1, LANES // SLOT)), ((0, SLOT - 4), (0, 0)))
        mine = jnp.concatenate([dir_a, dir_b, extra], axis=1)[None]
        near = [mine] + [swap(mine, m, groups) for m in (2, 4, 6)]
        near = jnp.concatenate(near, axis=0)
        wide = [near] + [swap(near, m, groups) for m in (1, 16, 17)]
        gathered = wide + [swap(v, 8, groups) for v in wide]
        masks = [c ^ xy ^ z for c in (0, 8) for xy in (0, 1, 16, 17) for z in (0, 2, 4, 6)]
    else:
        full = [lax.all_gather(v, AXES, axis=0, tiled=True) for v in (dir_a, dir_b)]
        vectors = lax.all_gather(small, AXES, axis=1, tiled=True)
        extra = jnp.tile(vectors.reshape(4, slots, SLOT).transpose(1, 0, 2), (1, 1, LANES // SLOT))
        extra = jnp.pad(extra, ((0, 0), (0, SLOT - 4), (0, 0)))
        blocks = [v.reshape(slots, SLOT, width) for v in full] + [extra]
        blocks = jnp.concatenate(blocks, axis=2)
        gathered = [blocks[4 * k : 4 * k + 4] for k in range(8)]
        masks = list(range(slots))
    weights = point_weights(place, shape_points, shape_category, category_counts, rows, average)
    layer_output, input_grad, keep, send = layers(
        place, gathered, layer_input, cotangent, weights, masks
    )
    if fast:
        total = keep + swap(send, 8, groups).astype(F32)
        parts = [total[4 * k : 4 * k + 4] for k in range(4)]
        came = [swap(parts[k].astype(BF16), m, groups) for k, m in ((1, 1), (2, 16), (3, 17))]
        total = parts[0] + sum(v.astype(F32) for v in came)
        came = [swap(total[k].astype(BF16), m, groups) for k, m in ((1, 2), (2, 4), (3, 6))]
        total = total[0] + sum(v.astype(F32) for v in came)
        vectors = total[0:4, 2 * width : 2 * width + SLOT]
        grad_a, grad_b = total[:, :width], total[:, width : 2 * width]
    else:
        total = jnp.concatenate([keep, send.astype(F32)], axis=0)
        scatter = lambda v, d: lax.psum_scatter(v, AXES, scatter_dimension=d, tiled=True)
        square = total[:, :, : 2 * width].reshape(width, 2 * width)
        square = scatter(square, 0)
        grad_a, grad_b = square[:, :width], square[:, width:]
        vectors = total[:, 0:4, 2 * width : 2 * width + SLOT].transpose(1, 0, 2).reshape(4, width)
        vectors = scatter(vectors, 1)
    return (
        layer_output,
        input_grad,
        grad_a,
        vectors[0],
        vectors[1],
        grad_b,
        vectors[2],
        vectors[3],
    )


def solution(mesh):
    rows, row, none = P(AXES, None), P(AXES), P()
    in_specs = (rows, rows, none, none, none, rows, row, row, rows, row, row)
    out_specs = (rows, rows, rows, row, row, rows, row, row)
    return jax.shard_map(body, mesh=mesh, in_specs=in_specs, out_specs=out_specs, check_vma=False)
```

time: 582 us -> 105 us (0.18); the launches traced: 575 us -> 105 us
  blocking collectives: 216 us -> 0 us
  matrix products: 123 us -> 0 us
  other arithmetic: 82 us -> 3.59 us
  waiting for transfers between devices: 84.6 us -> 22.8 us
  Pallas kernels: 0 us -> 55.3 us
  local copies, waits for them, and re-layouts: 53.8 us -> 5.2 us
  starting transfers between devices: 0.08 us -> 17 us
  between operations: 15.1 us -> 0.78 us
    all_gather x2 -> x0, blocking collectives: 142 us -> none  [the longest x1 72.8 us: body(): lax.all_gather(dir_a, ('dp', 'fsdp'), axis=0, tiled=True)]
    dot_general x24 -> x0, matrix products: 123 us -> none  [the longest x8 38.7 us: back_dot(): lax.dot_general(grad, weight, (((1,), (1,)), ((), ())), preferred_element...]
    reduce_scatter x2 -> x0, waiting for transfers between devices: 84.5 us -> none  [the longest x1 84.5 us: body(): lax.psum_scatter(dir_grad_a, ('dp', 'fsdp'), scatter_dimension=0, tiled=T...]
    concatenate x2 -> x1, other arithmetic: 75.4 us -> 0.03 us  [body(): near = jnp.concatenate(near, axis=0)]
    unnamed x2 -> x0, blocking collectives: 74 us -> none
    pallas_call x0 -> x2, Pallas kernels: none -> 55.3 us  [the longest x1 47.6 us: layers(): pl.pallas_call(functools.partial(layers_kernel, masks, parts), grid=(rows...]
    unnamed x135 -> x16, local copies, waits for them, and re-layouts: 45.5 us -> 1.4 us
    ppermute x0 -> x17, waiting for transfers between devices: none -> 22.8 us  [swap(): return lax.ppermute(value, AXES, [(k, k ^ mask) for k in range(groups)])]
  transfers between devices with their start and end apart: 2 -> 17, of which waited for: 1 -> 10; matrix products, arithmetic and copies ran while one was open for 25% -> 3% of each run, Pallas kernels for 0% -> 7%
where the time goes in v1:
time: 105 us
  Pallas kernels  55.3 us (53%)
  waiting for transfers between devices  22.8 us (22%)
  starting transfers between devices  17 us (16%)
  local copies, waits for them, and re-layouts  5.2 us (5%)
  other arithmetic  3.59 us (3%)
    pallas_call x1, Pallas kernels, layers(): pl.pallas_call(functools.partial(layers_kernel, masks, parts), grid=(rows...  47.6 us
    ppermute x17, waiting for transfers between devices, swap(): return lax.ppermute(value, AXES, [(k, k ^ mask) for k in range(groups)])  22.8 us
    ppermute x17, starting transfers between devices, swap(): return lax.ppermute(value, AXES, [(k, k ^ mask) for k in range(groups)])  17 us
    pallas_call x1, Pallas kernels, point_weights(): pl.pallas_call(functools.partial(point_weight_kernel, average), grid=(row...  7.75 us
  transfers between devices with their start and end apart: 17, of which 10 were waited for; matrix products, arithmetic and copies ran while one was open for 3% of the time, Pallas kernels for 7%

profile of v1, /device:TPU:0, one launch (start us, length us, event | category | flops | bytes accessed | tf_op | source)
XLA Modules:
  0.0 104.7 jit_solution(4483992707145338027)
XLA Ops:
  0.6 0.7 pad_maximum_fusion.1
  1.4 0.1 tile.10
  1.5 0.7 fusion.3
  2.2 5.0 %collective-permute-start.2 = (bf16[1,16,1152]{2,1,0:T(8,128)(2,1)S(1)}, bf16[1,16,1152]{2,1,0:T(8,128)(2,1)S(1)}, u32[]{:S(2)}, u32[]{:S(2)}) collective-permute-start(bf16[1,16,1152]{2,1,0:T(8,128)(2,1)S(1)} %fusion.3), channel_id=1, source_target_pairs={{0,6},{1,7},{2,4},{3,5},{4,2},{5,3},{6,0},{7,1},{8,14},{9,15},{10,... | collective-permute-start | bytes 110600 | tf_op jit(solution)/shard_map/ppermute | solution.py:214
  7.2 0.0 collective-permute-start.1
  7.2 0.6 collective-permute-start
  7.9 1.3 %collective-permute-done.2 = bf16[1,16,1152]{2,1,0:T(8,128)(2,1)S(1)} collective-permute-done((bf16[1,16,1152]{2,1,0:T(8,128)(2,1)S(1)}, bf16[1,16,1152]{2,1,0:T(8,128)(2,1)S(1)}, u32[]{:S(2)}, u32[]{:S(2)}) %collective-permute-start.2) | collective-permute-done | bytes 36896 | tf_op jit(solution)/shard_map/ppermute | solution.py:214
  9.2 2.9 %collective-permute-done.1 = bf16[1,16,1152]{2,1,0:T(8,128)(2,1)S(1)} collective-permute-done((bf16[1,16,1152]{2,1,0:T(8,128)(2,1)S(1)}, bf16[1,16,1152]{2,1,0:T(8,128)(2,1)S(1)}, u32[]{:S(2)}, u32[]{:S(2)}) %collective-permute-start.1) | collective-permute-done | bytes 36896 | tf_op jit(solution)/shard_map/ppermute | solution.py:214
  12.1 2.5 %collective-permute-start.5 = (bf16[4,16,1152]{2,1,0:T(8,128)(2,1)S(1)}, bf16[4,16,1152]{2,1,0:T(8,128)(2,1)S(1)}, u32[]{:S(2)}, u32[]{:S(2)}) collective-permute-start(bf16[4,16,1152]{2,1,0:T(8,128)(2,1)S(1)} %pad_maximum_fusion.refs_1_), channel_id=1, source_target_pairs={{0,17},{1,16},{2,19},{3,18},{4,21},{5,20},{6,23},{7,22},{8,25},{9,... | collective-permute-start | bytes 442376 | tf_op jit(solution)/shard_map/ppermute | solution.py:214
  14.7 0.5 collective-permute-start.4
  15.2 0.5 collective-permute-start.3
  15.7 3.1 %collective-permute-done.5.refs_4_ = bf16[4,16,1152]{2,1,0:T(8,128)(2,1)S(1)} collective-permute-done((bf16[4,16,1152]{2,1,0:T(8,128)(2,1)S(1)}, bf16[4,16,1152]{2,1,0:T(8,128)(2,1)S(1)}, u32[]{:S(2)}, u32[]{:S(2)}) %collective-permute-start.5) | collective-permute-done | bytes 147488 | tf_op jit(solution)/shard_map/ppermute | solution.py:214
  18.9 0.0 collective-permute-start.9
  18.9 1.6 %collective-permute-done.4.refs_3_ = bf16[4,16,1152]{2,1,0:T(8,128)(2,1)S(1)} collective-permute-done((bf16[4,16,1152]{2,1,0:T(8,128)(2,1)S(1)}, bf16[4,16,1152]{2,1,0:T(8,128)(2,1)S(1)}, u32[]{:S(2)}, u32[]{:S(2)}) %collective-permute-start.4) | collective-permute-done | bytes 147488 | tf_op jit(solution)/shard_map/ppermute | solution.py:214
  20.5 0.0 collective-permute-start.8
  20.5 0.0 collective-permute-done.3.refs_2_
  20.5 0.5 collective-permute-start.7
  21.0 0.7 pad.12
  21.7 0.7 pad.13
  22.3 0.6 pad_add_fusion.place_ref.refs_0_
  22.9 0.6 broadcast_in_dim.8.category_ref
  23.5 0.6 broadcast_in_dim.7.points_ref
  24.1 7.7 %point_weight.1.refs_11_ = bf16[11776,128]{1,0:T(8,128)(2,1)} custom-call(s32[2]{0:T(128)} %pad_add_fusion.place_ref.refs_0_, s32[13]{0:T(128)} %counts_ref.1, s32[8,128]{1,0:T(8,128)} %broadcast_in_dim.7.points_ref, s32[8,128]{1,0:T(8,128)} %broadcast_in_dim.8.category_ref), custom_call_target="tpu_custom_call" | custom-call | tf_op jit(solution)/shard_map/point_weight/pallas_call | solution.py:68
  31.9 0.0 collective-permute-done.8.refs_7_
  31.9 0.0 collective-permute-done.7.refs_6_
  31.9 0.6 copy-done.4
  32.5 0.1 copy-done.5
  32.6 0.1 copy-done.6
  32.7 0.7 copy-done.7
  33.3 47.6 %layers.1 = (bf16[11776,512]{1,0:T(8,128)(2,1)}, bf16[11776,512]{1,0:T(8,128)(2,1)}, f32[16,16,1152]{2,1,0:T(8,128)}, bf16[16,16,1152]{2,1,0:T(8,128)(2,1)}) custom-call(s32[2]{0:T(128)} %pad_add_fusion.place_ref.refs_0_, bf16[4,16,1152]{2,1,0:T(8,128)(2,1)} %copy-done, bf16[4,16,1152]{2,1,0:T(8,128)(2,1)} %copy-done.3, bf16[4,16,1152]{2,1,0:T(8,128)(2,1)} %copy-done.2, ...), custom_call_target="tpu_custom_call" | custom-call | tf_op jit(solution)/shard_map/layers/pallas_call | solution.py:192
  80.9 0.1 collective-permute-start.10
  81.1 2.1 %collective-permute-done.10 = bf16[16,16,1152]{2,1,0:T(8,128)(2,1)S(1)} collective-permute-done((bf16[16,16,1152]{2,1,0:T(8,128)(2,1)}, bf16[16,16,1152]{2,1,0:T(8,128)(2,1)S(1)}, u32[]{:S(2)}, u32[]{:S(2)}) %collective-permute-start.10) | collective-permute-done | bytes 589856 | tf_op jit(solution)/shard_map/ppermute | solution.py:214
  83.2 1.4 %fusion.5 = (bf16[16,16,1152]{2,1,0:T(8,128)(2,1)S(1)}, f32[16,16,1152]{2,1,0:T(8,128)S(1)}) fusion(f32[16,16,1152]{2,1,0:T(8,128)} %get-tuple-element.14, bf16[16,16,1152]{2,1,0:T(8,128)(2,1)S(1)} %collective-permute-done.10), kind=kLoop, calls=%fused_computation.19 | loop fusion | flops 884736 | bytes 3538944 | tf_op jit(solution)/shard_map/convert.5
  84.7 1.2 %collective-permute-start.11 = (bf16[4,16,1152]{2,1,0:T(8,128)(2,1)S(1)}, bf16[4,16,1152]{2,1,0:T(8,128)(2,1)S(1)}, u32[]{:S(2)}, u32[]{:S(2)}) collective-permute-start(bf16[4,16,1152]{2,1,0:T(8,128)(2,1)S(1)} %get-tuple-element.20), channel_id=1, source_target_pairs={{0,1},{1,0},{2,3},{3,2},{4,5},{5,4},{6,7},{7,6},{8,9},{9,8},{10,11... | collective-permute-start | bytes 442376 | tf_op jit(solution)/shard_map/ppermute | solution.py:214
  85.8 1.9 %collective-permute-start.13 = (bf16[4,16,1152]{2,1,0:T(8,128)(2,1)S(1)}, bf16[4,16,1152]{2,1,0:T(8,128)(2,1)S(1)}, u32[]{:S(2)}, u32[]{:S(2)}) collective-permute-start(bf16[4,16,1152]{2,1,0:T(8,128)(2,1)S(1)} %get-tuple-element.21), channel_id=1, source_target_pairs={{0,17},{1,16},{2,19},{3,18},{4,21},{5,20},{6,23},{7,22},{8,25},{9,... | collective-permute-start | bytes 442376 | tf_op jit(solution)/shard_map/ppermute | solution.py:214
  87.7 0.5 collective-permute-start.12
  88.2 5.6 %collective-permute-done.11 = bf16[4,16,1152]{2,1,0:T(8,128)(2,1)S(1)} collective-permute-done((bf16[4,16,1152]{2,1,0:T(8,128)(2,1)S(1)}, bf16[4,16,1152]{2,1,0:T(8,128)(2,1)S(1)}, u32[]{:S(2)}, u32[]{:S(2)}) %collective-permute-start.11) | collective-permute-done | bytes 147488 | tf_op jit(solution)/shard_map/ppermute | solution.py:214
  93.8 0.0 collective-permute-done.13
  93.8 1.2 %collective-permute-done.12 = bf16[4,16,1152]{2,1,0:T(8,128)(2,1)S(1)} collective-permute-done((bf16[4,16,1152]{2,1,0:T(8,128)(2,1)S(1)}, bf16[4,16,1152]{2,1,0:T(8,128)(2,1)S(1)}, u32[]{:S(2)}, u32[]{:S(2)}) %collective-permute-start.12) | collective-permute-done | bytes 147488 | tf_op jit(solution)/shard_map/ppermute | solution.py:214
  95.0 0.1 fusion.4
  95.1 0.3 collective-permute-start.14
  95.4 3.3 %collective-permute-start.16 = (bf16[16,1152]{1,0:T(8,128)(2,1)S(1)}, bf16[16,1152]{1,0:T(8,128)(2,1)S(1)}, u32[]{:S(2)}, u32[]{:S(2)}) collective-permute-start(bf16[16,1152]{1,0:T(8,128)(2,1)S(1)} %get-tuple-element.24), channel_id=1, source_target_pairs={{0,6},{1,7},{2,4},{3,5},{4,2},{5,3},{6,0},{7,1},{8,14},{9,15},{10,... | collective-permute-start | bytes 110600 | tf_op jit(solution)/shard_map/ppermute | solution.py:214
  98.7 0.0 collective-permute-start.15
  98.7 0.8 collective-permute-done.14
  99.5 1.8 %collective-permute-done.16 = bf16[16,1152]{1,0:T(8,128)(2,1)S(1)} collective-permute-done((bf16[16,1152]{1,0:T(8,128)(2,1)S(1)}, bf16[16,1152]{1,0:T(8,128)(2,1)S(1)}, u32[]{:S(2)}, u32[]{:S(2)}) %collective-permute-start.16) | collective-permute-done | bytes 36896 | tf_op jit(solution)/shard_map/ppermute | solution.py:214
  101.2 2.3 %collective-permute-done.15 = bf16[16,1152]{1,0:T(8,128)(2,1)S(1)} collective-permute-done((bf16[16,1152]{1,0:T(8,128)(2,1)S(1)}, bf16[16,1152]{1,0:T(8,128)(2,1)S(1)}, u32[]{:S(2)}, u32[]{:S(2)}) %collective-permute-start.15) | collective-permute-done | bytes 36896 | tf_op jit(solution)/shard_map/ppermute | solution.py:214
  103.6 0.5 slice_bitcast_fusion.4
  104.1 0.6 fusion.7
  (21 shorter events, 0.1 us)
Async XLA Ops:
  2.2 7.0 %collective-permute-start.2 = (bf16[1,16,1152]{2,1,0:T(8,128)(2,1)S(1)}, bf16[1,16,1152]{2,1,0:T(8,128)(2,1)S(1)}, u32[]{:S(2)}, u32[]{:S(2)}) collective-permute-start(bf16[1,16,1152]{2,1,0:T(8,128)(2,1)S(1)} %fusion.3), channel_id=1, source_target_pairs={{0,6},{1,7},{2,4},{3,5},{4,2},{5,3},{6,0},{7,1},{8,14},{9,15},{10,... | collective-permute-start | bytes 110600 | tf_op jit(solution)/shard_map/ppermute | solution.py:214
  7.2 4.9 %collective-permute-start.1 = (bf16[1,16,1152]{2,1,0:T(8,128)(2,1)S(1)}, bf16[1,16,1152]{2,1,0:T(8,128)(2,1)S(1)}, u32[]{:S(2)}, u32[]{:S(2)}) collective-permute-start(bf16[1,16,1152]{2,1,0:T(8,128)(2,1)S(1)} %fusion.3), channel_id=1, source_target_pairs={{0,4},{1,5},{2,6},{3,7},{4,0},{5,1},{6,2},{7,3},{8,12},{9,13},{10,... | collective-permute-start | bytes 110600 | tf_op jit(solution)/shard_map/ppermute | solution.py:214
  7.2 4.9 %collective-permute-start = (bf16[1,16,1152]{2,1,0:T(8,128)(2,1)S(1)}, bf16[1,16,1152]{2,1,0:T(8,128)(2,1)S(1)}, u32[]{:S(2)}, u32[]{:S(2)}) collective-permute-start(bf16[1,16,1152]{2,1,0:T(8,128)(2,1)S(1)} %fusion.3), channel_id=1, source_target_pairs={{0,2},{1,3},{2,0},{3,1},{4,6},{5,7},{6,4},{7,5},{8,10},{9,11},{10,... | collective-permute-start | bytes 110600 | tf_op jit(solution)/shard_map/ppermute | solution.py:214
  12.1 19.7 %copy-start = (bf16[4,16,1152]{2,1,0:T(8,128)(2,1)}, bf16[4,16,1152]{2,1,0:T(8,128)(2,1)S(1)}, u32[]{:S(2)}) copy-start(bf16[4,16,1152]{2,1,0:T(8,128)(2,1)S(1)} %pad_maximum_fusion.refs_1_) | copy-start | bytes 442372
  12.1 6.7 %collective-permute-start.5 = (bf16[4,16,1152]{2,1,0:T(8,128)(2,1)S(1)}, bf16[4,16,1152]{2,1,0:T(8,128)(2,1)S(1)}, u32[]{:S(2)}, u32[]{:S(2)}) collective-permute-start(bf16[4,16,1152]{2,1,0:T(8,128)(2,1)S(1)} %pad_maximum_fusion.refs_1_), channel_id=1, source_target_pairs={{0,17},{1,16},{2,19},{3,18},{4,21},{5,20},{6,23},{7,22},{8,25},{9,... | collective-permute-start | bytes 442376 | tf_op jit(solution)/shard_map/ppermute | solution.py:214
  14.7 5.8 %collective-permute-start.4 = (bf16[4,16,1152]{2,1,0:T(8,128)(2,1)S(1)}, bf16[4,16,1152]{2,1,0:T(8,128)(2,1)S(1)}, u32[]{:S(2)}, u32[]{:S(2)}) collective-permute-start(bf16[4,16,1152]{2,1,0:T(8,128)(2,1)S(1)} %pad_maximum_fusion.refs_1_), channel_id=1, source_target_pairs={{0,16},{1,17},{2,18},{3,19},{4,20},{5,21},{6,22},{7,23},{8,24},{9,... | collective-permute-start | bytes 442376 | tf_op jit(solution)/shard_map/ppermute | solution.py:214
  15.2 5.3 %collective-permute-start.3 = (bf16[4,16,1152]{2,1,0:T(8,128)(2,1)S(1)}, bf16[4,16,1152]{2,1,0:T(8,128)(2,1)S(1)}, u32[]{:S(2)}, u32[]{:S(2)}) collective-permute-start(bf16[4,16,1152]{2,1,0:T(8,128)(2,1)S(1)} %pad_maximum_fusion.refs_1_), channel_id=1, source_target_pairs={{0,1},{1,0},{2,3},{3,2},{4,5},{5,4},{6,7},{7,6},{8,9},{9,8},{10,11... | collective-permute-start | bytes 442376 | tf_op jit(solution)/shard_map/ppermute | solution.py:214
  15.7 16.2 %collective-permute-start.6 = (bf16[4,16,1152]{2,1,0:T(8,128)(2,1)S(1)}, bf16[4,16,1152]{2,1,0:T(8,128)(2,1)S(1)}, u32[]{:S(2)}, u32[]{:S(2)}) collective-permute-start(bf16[4,16,1152]{2,1,0:T(8,128)(2,1)S(1)} %pad_maximum_fusion.refs_1_), channel_id=1, source_target_pairs={{0,8},{1,9},{2,10},{3,11},{4,12},{5,13},{6,14},{7,15},{8,0},{9,1},... | collective-permute-start | bytes 442376 | tf_op jit(solution)/shard_map/ppermute | solution.py:214
  18.9 13.0 %copy-start.1 = (bf16[4,16,1152]{2,1,0:T(8,128)(2,1)}, bf16[4,16,1152]{2,1,0:T(8,128)(2,1)S(1)}, u32[]{:S(2)}) copy-start(bf16[4,16,1152]{2,1,0:T(8,128)(2,1)S(1)} %collective-permute-done.5.refs_4_) | copy-start | bytes 442372
  18.9 13.0 %collective-permute-start.9 = (bf16[4,16,1152]{2,1,0:T(8,128)(2,1)S(1)}, bf16[4,16,1152]{2,1,0:T(8,128)(2,1)S(1)}, u32[]{:S(2)}, u32[]{:S(2)}) collective-permute-start(bf16[4,16,1152]{2,1,0:T(8,128)(2,1)S(1)} %collective-permute-done.5.refs_4_), channel_id=1, source_target_pairs={{0,8},{1,9},{2,10},{3,11},{4,12},{5,13},{6,14},{7,15},{8,0},{9,1},... | collective-permute-start | bytes 442376 | tf_op jit(solution)/shard_map/ppermute | solution.py:214
  20.5 11.4 %copy-start.2 = (bf16[4,16,1152]{2,1,0:T(8,128)(2,1)}, bf16[4,16,1152]{2,1,0:T(8,128)(2,1)S(1)}, u32[]{:S(2)}) copy-start(bf16[4,16,1152]{2,1,0:T(8,128)(2,1)S(1)} %collective-permute-done.4.refs_3_) | copy-start | bytes 442372
  20.5 11.4 %collective-permute-start.8 = (bf16[4,16,1152]{2,1,0:T(8,128)(2,1)S(1)}, bf16[4,16,1152]{2,1,0:T(8,128)(2,1)S(1)}, u32[]{:S(2)}, u32[]{:S(2)}) collective-permute-start(bf16[4,16,1152]{2,1,0:T(8,128)(2,1)S(1)} %collective-permute-done.4.refs_3_), channel_id=1, source_target_pairs={{0,8},{1,9},{2,10},{3,11},{4,12},{5,13},{6,14},{7,15},{8,0},{9,1},... | collective-permute-start | bytes 442376 | tf_op jit(solution)/shard_map/ppermute | solution.py:214
  20.5 11.4 %copy-start.3 = (bf16[4,16,1152]{2,1,0:T(8,128)(2,1)}, bf16[4,16,1152]{2,1,0:T(8,128)(2,1)S(1)}, u32[]{:S(2)}) copy-start(bf16[4,16,1152]{2,1,0:T(8,128)(2,1)S(1)} %collective-permute-done.3.refs_2_) | copy-start | bytes 442372
  20.5 11.4 %collective-permute-start.7 = (bf16[4,16,1152]{2,1,0:T(8,128)(2,1)S(1)}, bf16[4,16,1152]{2,1,0:T(8,128)(2,1)S(1)}, u32[]{:S(2)}, u32[]{:S(2)}) collective-permute-start(bf16[4,16,1152]{2,1,0:T(8,128)(2,1)S(1)} %collective-permute-done.3.refs_2_), channel_id=1, source_target_pairs={{0,8},{1,9},{2,10},{3,11},{4,12},{5,13},{6,14},{7,15},{8,0},{9,1},... | collective-permute-start | bytes 442376 | tf_op jit(solution)/shard_map/ppermute | solution.py:214
  31.9 0.7 copy-start.4
  31.9 0.7 copy-start.5
  31.9 0.7 copy-start.6
  32.6 0.7 copy-start.7
  80.9 2.3 %collective-permute-start.10 = (bf16[16,16,1152]{2,1,0:T(8,128)(2,1)}, bf16[16,16,1152]{2,1,0:T(8,128)(2,1)S(1)}, u32[]{:S(2)}, u32[]{:S(2)}) collective-permute-start(bf16[16,16,1152]{2,1,0:T(8,128)(2,1)} %get-tuple-element.15), channel_id=1, source_target_pairs={{0,8},{1,9},{2,10},{3,11},{4,12},{5,13},{6,14},{7,15},{8,0},{9,1},... | collective-permute-start | bytes 1769480 | tf_op jit(solution)/shard_map/ppermute | solution.py:214
  84.7 9.1 %collective-permute-start.11 = (bf16[4,16,1152]{2,1,0:T(8,128)(2,1)S(1)}, bf16[4,16,1152]{2,1,0:T(8,128)(2,1)S(1)}, u32[]{:S(2)}, u32[]{:S(2)}) collective-permute-start(bf16[4,16,1152]{2,1,0:T(8,128)(2,1)S(1)} %get-tuple-element.20), channel_id=1, source_target_pairs={{0,1},{1,0},{2,3},{3,2},{4,5},{5,4},{6,7},{7,6},{8,9},{9,8},{10,11... | collective-permute-start | bytes 442376 | tf_op jit(solution)/shard_map/ppermute | solution.py:214
  85.8 8.0 %collective-permute-start.13 = (bf16[4,16,1152]{2,1,0:T(8,128)(2,1)S(1)}, bf16[4,16,1152]{2,1,0:T(8,128)(2,1)S(1)}, u32[]{:S(2)}, u32[]{:S(2)}) collective-permute-start(bf16[4,16,1152]{2,1,0:T(8,128)(2,1)S(1)} %get-tuple-element.21), channel_id=1, source_target_pairs={{0,17},{1,16},{2,19},{3,18},{4,21},{5,20},{6,23},{7,22},{8,25},{9,... | collective-permute-start | bytes 442376 | tf_op jit(solution)/shard_map/ppermute | solution.py:214
  87.7 7.3 %collective-permute-start.12 = (bf16[4,16,1152]{2,1,0:T(8,128)(2,1)S(1)}, bf16[4,16,1152]{2,1,0:T(8,128)(2,1)S(1)}, u32[]{:S(2)}, u32[]{:S(2)}) collective-permute-start(bf16[4,16,1152]{2,1,0:T(8,128)(2,1)S(1)} %get-tuple-element.22), channel_id=1, source_target_pairs={{0,16},{1,17},{2,18},{3,19},{4,20},{5,21},{6,22},{7,23},{8,24},{9,... | collective-permute-start | bytes 442376 | tf_op jit(solution)/shard_map/ppermute | solution.py:214
  95.1 4.4 %collective-permute-start.14 = (bf16[16,1152]{1,0:T(8,128)(2,1)S(1)}, bf16[16,1152]{1,0:T(8,128)(2,1)S(1)}, u32[]{:S(2)}, u32[]{:S(2)}) collective-permute-start(bf16[16,1152]{1,0:T(8,128)(2,1)S(1)} %get-tuple-element.23), channel_id=1, source_target_pairs={{0,2},{1,3},{2,0},{3,1},{4,6},{5,7},{6,4},{7,5},{8,10},{9,11},{10,... | collective-permute-start | bytes 110600 | tf_op jit(solution)/shard_map/ppermute | solution.py:214
  95.4 5.9 %collective-permute-start.16 = (bf16[16,1152]{1,0:T(8,128)(2,1)S(1)}, bf16[16,1152]{1,0:T(8,128)(2,1)S(1)}, u32[]{:S(2)}, u32[]{:S(2)}) collective-permute-start(bf16[16,1152]{1,0:T(8,128)(2,1)S(1)} %get-tuple-element.24), channel_id=1, source_target_pairs={{0,6},{1,7},{2,4},{3,5},{4,2},{5,3},{6,0},{7,1},{8,14},{9,15},{10,... | collective-permute-start | bytes 110600 | tf_op jit(solution)/shard_map/ppermute | solution.py:214
  98.7 4.9 %collective-permute-start.15 = (bf16[16,1152]{1,0:T(8,128)(2,1)S(1)}, bf16[16,1152]{1,0:T(8,128)(2,1)S(1)}, u32[]{:S(2)}, u32[]{:S(2)}) collective-permute-start(bf16[16,1152]{1,0:T(8,128)(2,1)S(1)} %get-tuple-element.25), channel_id=1, source_target_pairs={{0,4},{1,5},{2,6},{3,7},{4,0},{5,1},{6,2},{7,3},{8,12},{9,13},{10,... | collective-permute-start | bytes 110600 | tf_op jit(solution)/shard_map/ppermute | solution.py:214

commit v2 on v1

--- a/solution.py
+++ b/solution.py
@@ -1,4 +1,5 @@
 import functools
+import math
 
 import jax
 import jax.numpy as jnp
@@ -13,7 +14,7 @@
 LANES = 128
 F32 = jnp.float32
 BF16 = jnp.bfloat16
-VMEM_BYTES = 60 << 20
+VMEM_BYTES = 44 << 20
 
 
 def pick_tile(rows):
@@ -27,68 +28,67 @@
     return jnp.dot(left, right, preferred_element_type=F32)
 
 
-def point_weight_kernel(average, place_ref, counts_ref, points_ref, category_ref, out_ref, table):
-    shapes = points_ref.shape[1]
-    points = points_ref[...]
-    lane = lax.broadcasted_iota(jnp.int32, points.shape, 1)
-    ends = points
-    shift = 1
-    while shift < shapes:
-        ends = ends + jnp.where(lane >= shift, pltpu.roll(ends, shift, 1), 0)
-        shift *= 2
-    starts = ends - points
-
-    @pl.when(pl.program_id(0) == 0)
+def point_weight_kernel(average, place_ref, counts_ref, points_ref, category_ref, mine_ref, out_ref, same_ref, table):
+    lines = out_ref.shape[0] // LANES
+    step = pl.program_id(0)
+
+    @pl.when(step == 0)
     def _():
-        count = jnp.zeros(points.shape, jnp.int32)
-        for cat in range(counts_ref.shape[0]):
-            count = jnp.where(category_ref[...] == cat, counts_ref[cat], count)
-        weight = (
-            count.astype(F32) * (average / 4.0) / jnp.maximum(points, average // 2).astype(F32)
+        same_ref[...] = mine_ref[...]
+        line = lax.broadcasted_iota(jnp.int32, table.shape, 0)
+        position = place_ref[1] + line * LANES + lax.broadcasted_iota(jnp.int32, table.shape, 1)
+
+        def enter(shape, carry):
+            start, count, points = carry
+            after = position >= start
+            count = jnp.where(after, counts_ref[category_ref[shape]], count)
+            points = jnp.where(after, points_ref[shape], points)
+            return start + points_ref[shape], count, points
+
+        zero = jnp.zeros(table.shape, jnp.int32)
+        shapes = points_ref.shape[0]
+        _, count, points = lax.fori_loop(
+            0, shapes, enter, (jnp.int32(0), zero, zero), unroll=math.gcd(shapes, 8)
         )
-        square = lax.broadcasted_iota(jnp.int32, (shapes, shapes), 0) == lax.broadcasted_iota(
-            jnp.int32, (shapes, shapes), 1
+        table[...] = (
+            count.astype(F32)
+            * (average / 8.0)
+            / jnp.maximum(points, average // 2).astype(F32)
         )
-        column = jnp.sum(jnp.where(square, 0.5 * weight[0:1, :], 0.0), axis=1, keepdims=True)
-        table[...] = jnp.broadcast_to(column, table.shape).astype(BF16)
-
-    rows = out_ref.shape[0]
-    first = place_ref[1] + pl.program_id(0) * rows
-    position = first + lax.broadcasted_iota(jnp.int32, (rows, shapes), 0)
-    inside = (position >= starts[0:1, :]) & (position < ends[0:1, :])
-    out_ref[...] = dot(jnp.where(inside, 1.0, 0.0).astype(BF16), table[...]).astype(BF16)
-
-
-def point_weights(place, shape_points, shape_category, category_counts, rows, average):
-    shapes = shape_points.shape[0]
-    padded = -(-shapes // LANES) * LANES
-    wide = lambda v: jnp.broadcast_to(jnp.pad(v, (0, padded - shapes))[None, :], (8, padded))
-    tile = pick_tile(rows)
-    whole = pl.BlockSpec((8, padded), lambda i: (0, 0))
+
+    for k in range(lines):
+        row = jnp.broadcast_to(table[pl.ds(step * lines + k, 1), :], (LANES, LANES))
+        out_ref[pl.ds(k * LANES, LANES), :] = row.T.astype(BF16)
+
+
+def point_weights(place, shape_points, shape_category, category_counts, mine, rows, average):
+    scalars = pl.BlockSpec(memory_space=pltpu.SMEM)
+    steps = 4 if rows % (4 * LANES) == 0 else 1
+    lines = -(-rows // LANES // 8) * 8
+    whole = pl.BlockSpec(mine.shape, lambda i: (0,) * mine.ndim)
     return pl.pallas_call(
         functools.partial(point_weight_kernel, average),
-        grid=(rows // tile,),
-        in_specs=[
-            pl.BlockSpec(memory_space=pltpu.SMEM),
-            pl.BlockSpec(memory_space=pltpu.SMEM),
-            whole,
-            whole,
+        grid=(steps,),
+        in_specs=[scalars] * 4 + [whole],
+        out_specs=[pl.BlockSpec((rows // steps, LANES), lambda i: (i, 0)), whole],
+        out_shape=[
+            jax.ShapeDtypeStruct((rows, LANES), BF16),
+            jax.ShapeDtypeStruct(mine.shape, mine.dtype),
         ],
-        out_specs=pl.BlockSpec((tile, LANES), lambda i: (i, 0)),
-        out_shape=jax.ShapeDtypeStruct((rows, LANES), BF16),
-        scratch_shapes=[pltpu.VMEM((padded, LANES), BF16)],
-        compiler_params=pltpu.CompilerParams(vmem_limit_bytes=VMEM_BYTES),
+        scratch_shapes=[pltpu.VMEM((lines, LANES), F32)],
+        compiler_params=pltpu.CompilerParams(vmem_limit_bytes=16 << 20),
+        cost_estimate=pl.CostEstimate(
+            flops=50 * rows * LANES, bytes_accessed=2 * rows * LANES, transcendentals=0
+        ),
         name="point_weight",
-    )(place, category_counts, wide(shape_points), wide(shape_category))
+    )(place, category_counts, shape_points, shape_category, mine)
 
 
 def activate(half):
-    one = jnp.asarray(1, BF16)
-    half = half.astype(BF16)
-    bent = jnp.tanh(half)
-    lift = one + bent
-    value = half * lift
-    return value, lift + value * (one - bent)
+    lift = 1.0 + jnp.tanh(half)
+    value = (half * lift).astype(BF16)
+    lift = lift.astype(BF16)
+    return value, lift + value * (jnp.asarray(2, BF16) - lift)
 
 
 def layers_kernel(masks, parts, *refs):
@@ -96,7 +96,7 @@
     place_ref = refs[0]
     x_ref, cot_ref, pw_ref = refs[9:12]
     out_ref, in_grad_ref, keep_ref, send_ref = refs[12:16]
-    dir_a, dir_b, w_a, w_b, wt_a, wt_b, gw_a, gw_b, vec, gsum = refs[16:26]
+    dir_a, dir_b, w_a, w_b, wt_a, wt_b, gw_a, gw_b, vec, gsum, landed, columns, arrived = refs[16:]
     step = pl.program_id(0)
     width = x_ref.shape[1]
     tile = x_ref.shape[0]
@@ -107,18 +107,21 @@
 
     @pl.when(step == 0)
     def _():
-        lane = lax.broadcasted_iota(jnp.int32, (8, width), 1) // SLOT
-        small = jnp.zeros((8, width), F32)
+        copies = [
+            pltpu.make_async_copy(ref, landed.at[k], arrived.at[k])
+            for k, ref in enumerate(gathered)
+        ]
+        for copy in copies:
+            copy.start()
+        for copy in copies:
+            copy.wait()
         for slot in range(len(masks)):
-            home = owner(slot)
-            rows = pl.ds(pl.multiple_of(home * SLOT, SLOT), SLOT)
-            block = gathered[slot // 4][slot % 4]
+            rows = pl.ds(pl.multiple_of(owner(slot) * SLOT, SLOT), SLOT)
+            block = landed[slot // 4, slot % 4]
             dir_a[rows, :] = block[:, 0:width]
             dir_b[rows, :] = block[:, width : 2 * width]
-            extra = block[:, 2 * width :].astype(F32)[0:8]
-            small = jnp.where(
-                lane == home, jnp.concatenate([extra] * (width // LANES), axis=1), small
-            )
+            columns[rows, :] = block[:, 2 * width :].astype(F32)
+        small = columns[...].T
         for k, (direction, w, wt) in enumerate(((dir_a, w_a, wt_a), (dir_b, w_b, wt_b))):
             full = direction[...].astype(F32)
             norm = lax.rsqrt(jnp.sum(full * full, axis=0, keepdims=True) + EPS)
@@ -193,7 +196,7 @@
         functools.partial(layers_kernel, masks, parts),
         grid=(rows // tile,),
         in_specs=[pl.BlockSpec(memory_space=pltpu.SMEM)]
-        + [whole(4, SLOT, span)] * 8
+        + [pl.BlockSpec(memory_space=pl.ANY)] * 8
         + [by_row(width), by_row(width), by_row(LANES)],
         out_specs=[by_row(width), by_row(width), whole(half, SLOT, span), whole(half, SLOT, span)],
         out_shape=[
@@ -204,7 +207,13 @@
         ],
         scratch_shapes=[square(BF16)] * 6
         + [square(F32)] * 2
-        + [pltpu.VMEM((8, width), F32), pltpu.VMEM((16, width), F32)],
+        + [
+            pltpu.VMEM((8, width), F32),
+            pltpu.VMEM((16, width), F32),
+            pltpu.VMEM((8, 4, SLOT, span), BF16),
+            pltpu.VMEM((width, LANES), F32),
+            pltpu.SemaphoreType.DMA((8,)),
+        ],
         compiler_params=pltpu.CompilerParams(vmem_limit_bytes=VMEM_BYTES),
         name="layers",
     )(place, *gathered, layer_input, cotangent, weights)
@@ -237,10 +246,14 @@
     fast = share == SLOT and groups == 32 and fsdp == 8
     small = jnp.stack([gain_a, bias_a, gain_b, bias_b])
     place = jnp.stack([me if fast else jnp.zeros_like(me), me * rows])
+    weigh = lambda held: point_weights(
+        place, shape_points, shape_category, category_counts, held, rows, average
+    )
     if fast:
-        extra = jnp.pad(jnp.tile(small, (1, LANES // SLOT)), ((0, SLOT - 4), (0, 0)))
+        extra = jnp.pad(small.T, ((0, 0), (0, LANES - 4)))
         mine = jnp.concatenate([dir_a, dir_b, extra], axis=1)[None]
-        near = [mine] + [swap(mine, m, groups) for m in (2, 4, 6)]
+        weights, same = weigh(mine)
+        near = [same] + [swap(mine, m, groups) for m in (2, 4, 6)]
         near = jnp.concatenate(near, axis=0)
         wide = [near] + [swap(near, m, groups) for m in (1, 16, 17)]
         gathered = wide + [swap(v, 8, groups) for v in wide]
@@ -248,13 +261,12 @@
     else:
         full = [lax.all_gather(v, AXES, axis=0, tiled=True) for v in (dir_a, dir_b)]
         vectors = lax.all_gather(small, AXES, axis=1, tiled=True)
-        extra = jnp.tile(vectors.reshape(4, slots, SLOT).transpose(1, 0, 2), (1, 1, LANES // SLOT))
-        extra = jnp.pad(extra, ((0, 0), (0, SLOT - 4), (0, 0)))
+        extra = jnp.pad(vectors.T.reshape(slots, SLOT, 4), ((0, 0), (0, 0), (0, LANES - 4)))
         blocks = [v.reshape(slots, SLOT, width) for v in full] + [extra]
         blocks = jnp.concatenate(blocks, axis=2)
         gathered = [blocks[4 * k : 4 * k + 4] for k in range(8)]
         masks = list(range(slots))
-    weights = point_weights(place, shape_points, shape_category, category_counts, rows, average)
+        weights, _ = weigh(dir_a)
     layer_output, input_grad, keep, send = layers(
         place, gathered, layer_input, cotangent, weights, masks
     )

time: 105 us -> 96.5 us (0.919)
  Pallas kernels: 55.3 us -> 52.1 us
  waiting for transfers between devices: 22.8 us -> 20.4 us
  local copies, waits for them, and re-layouts: 5.2 us -> 3.3 us
  other arithmetic: 3.59 us -> 1.79 us
    pallas_call x1, Pallas kernels: 7.75 us -> 2.16 us  [point_weights(): pl.pallas_call(functools.partial(point_weight_kernel, average), grid=(ste...]
    ppermute x17, waiting for transfers between devices: 22.8 us -> 20.4 us  [swap(): return lax.ppermute(value, AXES, [(k, k ^ mask) for k in range(groups)])]
    pallas_call x1, Pallas kernels: 47.6 us -> 50 us  [layers(): pl.pallas_call(functools.partial(layers_kernel, masks, parts), grid=(rows...]
    pad x2 -> x0, local copies, waits for them, and re-layouts: 1.32 us -> none  [point_weights(): jnp.pad(v, (0, padded - shapes))[None, :]]
    another operation x2, other arithmetic: 1.5 us -> 0.24 us
    broadcast_in_dim x2 -> x0, local copies, waits for them, and re-layouts: 1.19 us -> none  [point_weights(): jnp.broadcast_to(jnp.pad(v, (0, padded - shapes))[None, :], (8, padded))]
  transfers between devices with their start and end apart: 17 -> 17, of which waited for: 10 -> 9; matrix products, arithmetic and copies ran while one was open for 3% -> 0% of each run, Pallas kernels for 7% -> 2%
where the time goes in v2:
time: 96.5 us; the launch traced here: 96.1 us
  Pallas kernels  52.1 us (54%)
  waiting for transfers between devices  20.4 us (21%)
  starting transfers between devices  17.8 us (18%)
  local copies, waits for them, and re-layouts  3.3 us (3%)
  other arithmetic  1.79 us (2%)
    pallas_call x1, Pallas kernels, layers(): pl.pallas_call(functools.partial(layers_kernel, masks, parts), grid=(rows...  50 us
    ppermute x17, waiting for transfers between devices, swap(): return lax.ppermute(value, AXES, [(k, k ^ mask) for k in range(groups)])  20.4 us
    ppermute x17, starting transfers between devices, swap(): return lax.ppermute(value, AXES, [(k, k ^ mask) for k in range(groups)])  17.8 us
    pallas_call x1, Pallas kernels, point_weights(): pl.pallas_call(functools.partial(point_weight_kernel, average), grid=(ste...  2.16 us
    unnamed x9, local copies, waits for them, and re-layouts  1.99 us
  transfers between devices with their start and end apart: 17, of which 9 were waited for; matrix products, arithmetic and copies ran while one was open for 0% of the time, Pallas kernels for 2%

profile of v2, /device:TPU:0, one launch (start us, length us, event | category | flops | bytes accessed | tf_op | source)
XLA Modules:
  0.0 96.1 jit_solution(10630940324127772730)
XLA Ops:
  0.6 0.7 pad_maximum_fusion
  1.4 0.1 copy.23
  1.4 0.7 fusion.3.mine_ref
  2.2 5.0 %collective-permute-start.2 = (bf16[1,16,1152]{2,1,0:T(8,128)(2,1)S(1)}, bf16[1,16,1152]{2,1,0:T(8,128)(2,1)S(1)}, u32[]{:S(2)}, u32[]{:S(2)}) collective-permute-start(bf16[1,16,1152]{2,1,0:T(8,128)(2,1)S(1)} %fusion.3.mine_ref), channel_id=1, source_target_pairs={{0,6},{1,7},{2,4},{3,5},{4,2},{5,3},{6,0},{7,1},{8,14},{9,15},{10,... | collective-permute-start | bytes 110600 | tf_op jit(solution)/shard_map/ppermute | solution.py:223
  7.2 0.0 collective-permute-start.1
  7.2 0.6 collective-permute-start
  7.9 0.1 pad_add_fusion.place_ref.refs_0_
  8.0 0.0 copy-start
  8.0 0.7 copy-done
  8.6 0.7 copy-done.1
  9.3 0.7 copy-done.2
  9.9 2.2 %point_weight.1 = (bf16[11776,128]{1,0:T(8,128)(2,1)S(1)}, bf16[1,16,1152]{2,1,0:T(8,128)(2,1)S(1)}) custom-call(s32[2]{0:T(128)S(1)} %pad_add_fusion.place_ref.refs_0_, s32[13]{0:T(128)S(1)} %copy-done, s32[64]{0:T(128)S(1)} %copy-done.1, s32[64]{0:T(128)S(1)} %copy-done.2, bf16[1,16,1152]{2,1,0:T(8,128)(2,1)S(1)} %fusion.3.mine_ref), custom_call_target="tpu_custom_call" | custom-call | flops 75366400 | bytes 3014656 | tf_op jit(solution)/shard_map/point_weight/pallas_call | solution.py:69
  12.1 0.0 collective-permute-done
  12.1 0.0 collective-permute-done.1
  12.1 0.0 collective-permute-done.2
  12.2 2.7 %collective-permute-start.5 = (bf16[4,16,1152]{2,1,0:T(8,128)(2,1)S(1)}, bf16[4,16,1152]{2,1,0:T(8,128)(2,1)S(1)}, u32[]{:S(2)}, u32[]{:S(2)}) collective-permute-start(bf16[4,16,1152]{2,1,0:T(8,128)(2,1)S(1)} %constant_dynamic-update-slice_fusion.refs_1_), channel_id=1, source_target_pairs={{0,17},{1,16},{2,19},{3,18},{4,21},{5,20},{6,23},{7,22},{8,25},{9,... | collective-permute-start | bytes 442376 | tf_op jit(solution)/shard_map/ppermute | solution.py:223
  14.8 0.5 collective-permute-start.4
  15.4 0.4 collective-permute-start.3
  15.7 0.0 collective-permute-start.6
  15.7 4.0 %collective-permute-done.5.refs_4_ = bf16[4,16,1152]{2,1,0:T(8,128)(2,1)S(1)} collective-permute-done((bf16[4,16,1152]{2,1,0:T(8,128)(2,1)S(1)}, bf16[4,16,1152]{2,1,0:T(8,128)(2,1)S(1)}, u32[]{:S(2)}, u32[]{:S(2)}) %collective-permute-start.5) | collective-permute-done | bytes 147488 | tf_op jit(solution)/shard_map/ppermute | solution.py:223
  19.8 0.0 collective-permute-start.9
  19.8 1.6 %collective-permute-done.4.refs_3_ = bf16[4,16,1152]{2,1,0:T(8,128)(2,1)S(1)} collective-permute-done((bf16[4,16,1152]{2,1,0:T(8,128)(2,1)S(1)}, bf16[4,16,1152]{2,1,0:T(8,128)(2,1)S(1)}, u32[]{:S(2)}, u32[]{:S(2)}) %collective-permute-start.4) | collective-permute-done | bytes 147488 | tf_op jit(solution)/shard_map/ppermute | solution.py:223
  21.4 0.0 collective-permute-start.8
  21.4 0.0 collective-permute-done.3.refs_2_
  21.4 0.5 collective-permute-start.7
  21.9 0.0 collective-permute-done.6.refs_5_
  21.9 0.0 collective-permute-done.9.refs_8_
  21.9 0.9 collective-permute-done.8.refs_7_
  22.8 0.2 collective-permute-done.7.refs_6_
  23.0 50.0 %layers.1 = (bf16[11776,512]{1,0:T(8,128)(2,1)}, bf16[11776,512]{1,0:T(8,128)(2,1)}, f32[16,16,1152]{2,1,0:T(8,128)S(1)}, bf16[16,16,1152]{2,1,0:T(8,128)(2,1)S(1)}) custom-call(s32[2]{0:T(128)S(1)} %pad_add_fusion.place_ref.refs_0_, bf16[4,16,1152]{2,1,0:T(8,128)(2,1)S(1)} %constant_dynamic-update-slice_fusion.refs_1_, ...), custom_call_target="tpu_custom_call" | custom-call | tf_op jit(solution)/shard_map/layers/pallas_call | solution.py:195
  73.0 0.4 collective-permute-start.10
  73.3 1.7 %collective-permute-done.10 = bf16[16,16,1152]{2,1,0:T(8,128)(2,1)S(1)} collective-permute-done((bf16[16,16,1152]{2,1,0:T(8,128)(2,1)S(1)}, bf16[16,16,1152]{2,1,0:T(8,128)(2,1)S(1)}, u32[]{:S(2)}, u32[]{:S(2)}) %collective-permute-start.10) | collective-permute-done | bytes 589856 | tf_op jit(solution)/shard_map/ppermute | solution.py:223
  75.0 0.2 fusion.5
  75.2 1.3 %collective-permute-start.11 = (bf16[4,16,1152]{2,1,0:T(8,128)(2,1)S(1)}, bf16[4,16,1152]{2,1,0:T(8,128)(2,1)S(1)}, u32[]{:S(2)}, u32[]{:S(2)}) collective-permute-start(bf16[4,16,1152]{2,1,0:T(8,128)(2,1)S(1)} %get-tuple-element.24), channel_id=1, source_target_pairs={{0,1},{1,0},{2,3},{3,2},{4,5},{5,4},{6,7},{7,6},{8,9},{9,8},{10,11... | collective-permute-start | bytes 442376 | tf_op jit(solution)/shard_map/ppermute | solution.py:223
  76.5 1.7 %collective-permute-start.13 = (bf16[4,16,1152]{2,1,0:T(8,128)(2,1)S(1)}, bf16[4,16,1152]{2,1,0:T(8,128)(2,1)S(1)}, u32[]{:S(2)}, u32[]{:S(2)}) collective-permute-start(bf16[4,16,1152]{2,1,0:T(8,128)(2,1)S(1)} %get-tuple-element.25), channel_id=1, source_target_pairs={{0,17},{1,16},{2,19},{3,18},{4,21},{5,20},{6,23},{7,22},{8,25},{9,... | collective-permute-start | bytes 442376 | tf_op jit(solution)/shard_map/ppermute | solution.py:223
  78.3 0.5 collective-permute-start.12
  78.8 5.7 %collective-permute-done.11 = bf16[4,16,1152]{2,1,0:T(8,128)(2,1)S(1)} collective-permute-done((bf16[4,16,1152]{2,1,0:T(8,128)(2,1)S(1)}, bf16[4,16,1152]{2,1,0:T(8,128)(2,1)S(1)}, u32[]{:S(2)}, u32[]{:S(2)}) %collective-permute-start.11) | collective-permute-done | bytes 147488 | tf_op jit(solution)/shard_map/ppermute | solution.py:223
  84.5 0.0 collective-permute-done.13
  84.5 1.2 %collective-permute-done.12 = bf16[4,16,1152]{2,1,0:T(8,128)(2,1)S(1)} collective-permute-done((bf16[4,16,1152]{2,1,0:T(8,128)(2,1)S(1)}, bf16[4,16,1152]{2,1,0:T(8,128)(2,1)S(1)}, u32[]{:S(2)}, u32[]{:S(2)}) %collective-permute-start.12) | collective-permute-done | bytes 147488 | tf_op jit(solution)/shard_map/ppermute | solution.py:223
  85.7 0.1 fusion.4
  85.8 1.5 %collective-permute-start.14 = (bf16[16,1152]{1,0:T(8,128)(2,1)S(1)}, bf16[16,1152]{1,0:T(8,128)(2,1)S(1)}, u32[]{:S(2)}, u32[]{:S(2)}) collective-permute-start(bf16[16,1152]{1,0:T(8,128)(2,1)S(1)} %get-tuple-element.27), channel_id=1, source_target_pairs={{0,2},{1,3},{2,0},{3,1},{4,6},{5,7},{6,4},{7,5},{8,10},{9,11},{10,... | collective-permute-start | bytes 110600 | tf_op jit(solution)/shard_map/ppermute | solution.py:223
  87.3 2.4 %collective-permute-start.16 = (bf16[16,1152]{1,0:T(8,128)(2,1)S(1)}, bf16[16,1152]{1,0:T(8,128)(2,1)S(1)}, u32[]{:S(2)}, u32[]{:S(2)}) collective-permute-start(bf16[16,1152]{1,0:T(8,128)(2,1)S(1)} %get-tuple-element.28), channel_id=1, source_target_pairs={{0,6},{1,7},{2,4},{3,5},{4,2},{5,3},{6,0},{7,1},{8,14},{9,15},{10,... | collective-permute-start | bytes 110600 | tf_op jit(solution)/shard_map/ppermute | solution.py:223
  89.7 0.3 collective-permute-start.15
  89.9 0.0 collective-permute-done.14
  89.9 3.1 %collective-permute-done.16 = bf16[16,1152]{1,0:T(8,128)(2,1)S(1)} collective-permute-done((bf16[16,1152]{1,0:T(8,128)(2,1)S(1)}, bf16[16,1152]{1,0:T(8,128)(2,1)S(1)}, u32[]{:S(2)}, u32[]{:S(2)}) %collective-permute-start.16) | collective-permute-done | bytes 36896 | tf_op jit(solution)/shard_map/ppermute | solution.py:223
  93.1 1.9 %collective-permute-done.15 = bf16[16,1152]{1,0:T(8,128)(2,1)S(1)} collective-permute-done((bf16[16,1152]{1,0:T(8,128)(2,1)S(1)}, bf16[16,1152]{1,0:T(8,128)(2,1)S(1)}, u32[]{:S(2)}, u32[]{:S(2)}) %collective-permute-start.15) | collective-permute-done | bytes 36896 | tf_op jit(solution)/shard_map/ppermute | solution.py:223
  94.9 0.5 slice_bitcast_fusion.4
  95.5 0.6 fusion.7
  (9 shorter events, 0.1 us)
Async XLA Ops:
  2.2 10.0 %collective-permute-start.2 = (bf16[1,16,1152]{2,1,0:T(8,128)(2,1)S(1)}, bf16[1,16,1152]{2,1,0:T(8,128)(2,1)S(1)}, u32[]{:S(2)}, u32[]{:S(2)}) collective-permute-start(bf16[1,16,1152]{2,1,0:T(8,128)(2,1)S(1)} %fusion.3.mine_ref), channel_id=1, source_target_pairs={{0,6},{1,7},{2,4},{3,5},{4,2},{5,3},{6,0},{7,1},{8,14},{9,15},{10,... | collective-permute-start | bytes 110600 | tf_op jit(solution)/shard_map/ppermute | solution.py:223
  7.2 4.9 %collective-permute-start.1 = (bf16[1,16,1152]{2,1,0:T(8,128)(2,1)S(1)}, bf16[1,16,1152]{2,1,0:T(8,128)(2,1)S(1)}, u32[]{:S(2)}, u32[]{:S(2)}) collective-permute-start(bf16[1,16,1152]{2,1,0:T(8,128)(2,1)S(1)} %fusion.3.mine_ref), channel_id=1, source_target_pairs={{0,4},{1,5},{2,6},{3,7},{4,0},{5,1},{6,2},{7,3},{8,12},{9,13},{10,... | collective-permute-start | bytes 110600 | tf_op jit(solution)/shard_map/ppermute | solution.py:223
  7.2 4.9 %collective-permute-start = (bf16[1,16,1152]{2,1,0:T(8,128)(2,1)S(1)}, bf16[1,16,1152]{2,1,0:T(8,128)(2,1)S(1)}, u32[]{:S(2)}, u32[]{:S(2)}) collective-permute-start(bf16[1,16,1152]{2,1,0:T(8,128)(2,1)S(1)} %fusion.3.mine_ref), channel_id=1, source_target_pairs={{0,2},{1,3},{2,0},{3,1},{4,6},{5,7},{6,4},{7,5},{8,10},{9,11},{10,... | collective-permute-start | bytes 110600 | tf_op jit(solution)/shard_map/ppermute | solution.py:223
  8.0 0.7 copy-start
  8.6 0.7 copy-start.1
  9.3 0.7 copy-start.2
  12.2 7.6 %collective-permute-start.5 = (bf16[4,16,1152]{2,1,0:T(8,128)(2,1)S(1)}, bf16[4,16,1152]{2,1,0:T(8,128)(2,1)S(1)}, u32[]{:S(2)}, u32[]{:S(2)}) collective-permute-start(bf16[4,16,1152]{2,1,0:T(8,128)(2,1)S(1)} %constant_dynamic-update-slice_fusion.refs_1_), channel_id=1, source_target_pairs={{0,17},{1,16},{2,19},{3,18},{4,21},{5,20},{6,23},{7,22},{8,25},{9,... | collective-permute-start | bytes 442376 | tf_op jit(solution)/shard_map/ppermute | solution.py:223
  14.8 6.5 %collective-permute-start.4 = (bf16[4,16,1152]{2,1,0:T(8,128)(2,1)S(1)}, bf16[4,16,1152]{2,1,0:T(8,128)(2,1)S(1)}, u32[]{:S(2)}, u32[]{:S(2)}) collective-permute-start(bf16[4,16,1152]{2,1,0:T(8,128)(2,1)S(1)} %constant_dynamic-update-slice_fusion.refs_1_), channel_id=1, source_target_pairs={{0,16},{1,17},{2,18},{3,19},{4,20},{5,21},{6,22},{7,23},{8,24},{9,... | collective-permute-start | bytes 442376 | tf_op jit(solution)/shard_map/ppermute | solution.py:223
  15.4 6.0 %collective-permute-start.3 = (bf16[4,16,1152]{2,1,0:T(8,128)(2,1)S(1)}, bf16[4,16,1152]{2,1,0:T(8,128)(2,1)S(1)}, u32[]{:S(2)}, u32[]{:S(2)}) collective-permute-start(bf16[4,16,1152]{2,1,0:T(8,128)(2,1)S(1)} %constant_dynamic-update-slice_fusion.refs_1_), channel_id=1, source_target_pairs={{0,1},{1,0},{2,3},{3,2},{4,5},{5,4},{6,7},{7,6},{8,9},{9,8},{10,11... | collective-permute-start | bytes 442376 | tf_op jit(solution)/shard_map/ppermute | solution.py:223
  15.7 6.2 %collective-permute-start.6 = (bf16[4,16,1152]{2,1,0:T(8,128)(2,1)S(1)}, bf16[4,16,1152]{2,1,0:T(8,128)(2,1)S(1)}, u32[]{:S(2)}, u32[]{:S(2)}) collective-permute-start(bf16[4,16,1152]{2,1,0:T(8,128)(2,1)S(1)} %constant_dynamic-update-slice_fusion.refs_1_), channel_id=1, source_target_pairs={{0,8},{1,9},{2,10},{3,11},{4,12},{5,13},{6,14},{7,15},{8,0},{9,1},... | collective-permute-start | bytes 442376 | tf_op jit(solution)/shard_map/ppermute | solution.py:223
  19.8 2.1 %collective-permute-start.9 = (bf16[4,16,1152]{2,1,0:T(8,128)(2,1)S(1)}, bf16[4,16,1152]{2,1,0:T(8,128)(2,1)S(1)}, u32[]{:S(2)}, u32[]{:S(2)}) collective-permute-start(bf16[4,16,1152]{2,1,0:T(8,128)(2,1)S(1)} %collective-permute-done.5.refs_4_), channel_id=1, source_target_pairs={{0,8},{1,9},{2,10},{3,11},{4,12},{5,13},{6,14},{7,15},{8,0},{9,1},... | collective-permute-start | bytes 442376 | tf_op jit(solution)/shard_map/ppermute | solution.py:223
  21.4 1.4 %collective-permute-start.8 = (bf16[4,16,1152]{2,1,0:T(8,128)(2,1)S(1)}, bf16[4,16,1152]{2,1,0:T(8,128)(2,1)S(1)}, u32[]{:S(2)}, u32[]{:S(2)}) collective-permute-start(bf16[4,16,1152]{2,1,0:T(8,128)(2,1)S(1)} %collective-permute-done.4.refs_3_), channel_id=1, source_target_pairs={{0,8},{1,9},{2,10},{3,11},{4,12},{5,13},{6,14},{7,15},{8,0},{9,1},... | collective-permute-start | bytes 442376 | tf_op jit(solution)/shard_map/ppermute | solution.py:223
  21.4 1.6 %collective-permute-start.7 = (bf16[4,16,1152]{2,1,0:T(8,128)(2,1)S(1)}, bf16[4,16,1152]{2,1,0:T(8,128)(2,1)S(1)}, u32[]{:S(2)}, u32[]{:S(2)}) collective-permute-start(bf16[4,16,1152]{2,1,0:T(8,128)(2,1)S(1)} %collective-permute-done.3.refs_2_), channel_id=1, source_target_pairs={{0,8},{1,9},{2,10},{3,11},{4,12},{5,13},{6,14},{7,15},{8,0},{9,1},... | collective-permute-start | bytes 442376 | tf_op jit(solution)/shard_map/ppermute | solution.py:223
  73.0 2.1 %collective-permute-start.10 = (bf16[16,16,1152]{2,1,0:T(8,128)(2,1)S(1)}, bf16[16,16,1152]{2,1,0:T(8,128)(2,1)S(1)}, u32[]{:S(2)}, u32[]{:S(2)}) collective-permute-start(bf16[16,16,1152]{2,1,0:T(8,128)(2,1)S(1)} %get-tuple-element.19), channel_id=1, source_target_pairs={{0,8},{1,9},{2,10},{3,11},{4,12},{5,13},{6,14},{7,15},{8,0},{9,1},... | collective-permute-start | bytes 1769480 | tf_op jit(solution)/shard_map/ppermute | solution.py:223
  75.2 9.3 %collective-permute-start.11 = (bf16[4,16,1152]{2,1,0:T(8,128)(2,1)S(1)}, bf16[4,16,1152]{2,1,0:T(8,128)(2,1)S(1)}, u32[]{:S(2)}, u32[]{:S(2)}) collective-permute-start(bf16[4,16,1152]{2,1,0:T(8,128)(2,1)S(1)} %get-tuple-element.24), channel_id=1, source_target_pairs={{0,1},{1,0},{2,3},{3,2},{4,5},{5,4},{6,7},{7,6},{8,9},{9,8},{10,11... | collective-permute-start | bytes 442376 | tf_op jit(solution)/shard_map/ppermute | solution.py:223
  76.5 8.0 %collective-permute-start.13 = (bf16[4,16,1152]{2,1,0:T(8,128)(2,1)S(1)}, bf16[4,16,1152]{2,1,0:T(8,128)(2,1)S(1)}, u32[]{:S(2)}, u32[]{:S(2)}) collective-permute-start(bf16[4,16,1152]{2,1,0:T(8,128)(2,1)S(1)} %get-tuple-element.25), channel_id=1, source_target_pairs={{0,17},{1,16},{2,19},{3,18},{4,21},{5,20},{6,23},{7,22},{8,25},{9,... | collective-permute-start | bytes 442376 | tf_op jit(solution)/shard_map/ppermute | solution.py:223
  78.3 7.5 %collective-permute-start.12 = (bf16[4,16,1152]{2,1,0:T(8,128)(2,1)S(1)}, bf16[4,16,1152]{2,1,0:T(8,128)(2,1)S(1)}, u32[]{:S(2)}, u32[]{:S(2)}) collective-permute-start(bf16[4,16,1152]{2,1,0:T(8,128)(2,1)S(1)} %get-tuple-element.26), channel_id=1, source_target_pairs={{0,16},{1,17},{2,18},{3,19},{4,20},{5,21},{6,22},{7,23},{8,24},{9,... | collective-permute-start | bytes 442376 | tf_op jit(solution)/shard_map/ppermute | solution.py:223
  85.8 4.1 %collective-permute-start.14 = (bf16[16,1152]{1,0:T(8,128)(2,1)S(1)}, bf16[16,1152]{1,0:T(8,128)(2,1)S(1)}, u32[]{:S(2)}, u32[]{:S(2)}) collective-permute-start(bf16[16,1152]{1,0:T(8,128)(2,1)S(1)} %get-tuple-element.27), channel_id=1, source_target_pairs={{0,2},{1,3},{2,0},{3,1},{4,6},{5,7},{6,4},{7,5},{8,10},{9,11},{10,... | collective-permute-start | bytes 110600 | tf_op jit(solution)/shard_map/ppermute | solution.py:223
  87.3 5.8 %collective-permute-start.16 = (bf16[16,1152]{1,0:T(8,128)(2,1)S(1)}, bf16[16,1152]{1,0:T(8,128)(2,1)S(1)}, u32[]{:S(2)}, u32[]{:S(2)}) collective-permute-start(bf16[16,1152]{1,0:T(8,128)(2,1)S(1)} %get-tuple-element.28), channel_id=1, source_target_pairs={{0,6},{1,7},{2,4},{3,5},{4,2},{5,3},{6,0},{7,1},{8,14},{9,15},{10,... | collective-permute-start | bytes 110600 | tf_op jit(solution)/shard_map/ppermute | solution.py:223
  89.7 5.3 %collective-permute-start.15 = (bf16[16,1152]{1,0:T(8,128)(2,1)S(1)}, bf16[16,1152]{1,0:T(8,128)(2,1)S(1)}, u32[]{:S(2)}, u32[]{:S(2)}) collective-permute-start(bf16[16,1152]{1,0:T(8,128)(2,1)S(1)} %get-tuple-element.29), channel_id=1, source_target_pairs={{0,4},{1,5},{2,6},{3,7},{4,0},{5,1},{6,2},{7,3},{8,12},{9,13},{10,... | collective-permute-start | bytes 110600 | tf_op jit(solution)/shard_map/ppermute | solution.py:223

commit v3 on v2

--- a/solution.py
+++ b/solution.py
@@ -14,7 +14,8 @@
 LANES = 128
 F32 = jnp.float32
 BF16 = jnp.bfloat16
-VMEM_BYTES = 44 << 20
+VMEM_BYTES = 36 << 20
+GRAD_VMEM = 10 << 20
 
 
 def pick_tile(rows):
@@ -84,6 +85,42 @@
     )(place, category_counts, shape_points, shape_category, mine)
 
 
+def input_grad_kernel(grad_ref, w_ref, held_ref, *refs):
+    out_ref, same_ref = refs[-2:]
+
+    @pl.when(pl.program_id(0) == 0)
+    def _():
+        same_ref[...] = held_ref[...]
+
+    out_ref[...] = dot(grad_ref[...], w_ref[...]).astype(BF16)
+
+
+def input_grads(grads, weight, held, whole, tile, first, count):
+    rows, width = grads.shape
+    by_row = pl.BlockSpec((tile, width), lambda i: (i + first, 0))
+    every = pl.BlockSpec(held.shape, lambda i: (0,) * held.ndim)
+    more = [] if whole is None else [whole]
+    return pl.pallas_call(
+        input_grad_kernel,
+        grid=(count,),
+        in_specs=[by_row, pl.BlockSpec((width, width), lambda i: (0, 0)), every]
+        + [pl.BlockSpec(memory_space=pl.ANY)] * len(more),
+        out_specs=[by_row, every],
+        out_shape=[
+            jax.ShapeDtypeStruct((rows, width), BF16),
+            jax.ShapeDtypeStruct(held.shape, held.dtype),
+        ],
+        input_output_aliases={3: 0} if more else {},
+        cost_estimate=pl.CostEstimate(
+            flops=2 * count * tile * width * width,
+            bytes_accessed=4 * count * tile * width,
+            transcendentals=0,
+        ),
+        compiler_params=pltpu.CompilerParams(vmem_limit_bytes=GRAD_VMEM),
+        name="input_grad",
+    )(grads, weight, held, *more)
+
+
 def activate(half):
     lift = 1.0 + jnp.tanh(half)
     value = (half * lift).astype(BF16)
@@ -95,8 +132,8 @@
     gathered = refs[1:9]
     place_ref = refs[0]
     x_ref, cot_ref, pw_ref = refs[9:12]
-    out_ref, in_grad_ref, keep_ref, send_ref = refs[12:16]
-    dir_a, dir_b, w_a, w_b, wt_a, wt_b, gw_a, gw_b, vec, gsum, landed, columns, arrived = refs[16:]
+    out_ref, grad_ref, wt_a, keep_ref, send_ref = refs[12:17]
+    dir_a, dir_b, w_a, w_b, wt_b, gw_a, gw_b, vec, gsum, landed, columns, arrived = refs[17:]
     step = pl.program_id(0)
     width = x_ref.shape[1]
     tile = x_ref.shape[0]
@@ -149,7 +186,7 @@
         grads.append((cot_ref[s, :] * weight) * slope_b)
     grads_a = [dot(g, wt_b[...]).astype(BF16) * sa for g, sa in zip(grads, slope_a)]
     for s, g in zip(spans, grads_a):
-        in_grad_ref[s, :] = dot(g, wt_a[...]).astype(BF16)
+        grad_ref[s, :] = g
     ones = jnp.ones((SLOT, tile), BF16)
     join = lambda pieces: jnp.concatenate(pieces, axis=0)
     both = dot(join([join(hidden).T, ones]), join(grads))
@@ -198,14 +235,21 @@
         in_specs=[pl.BlockSpec(memory_space=pltpu.SMEM)]
         + [pl.BlockSpec(memory_space=pl.ANY)] * 8
         + [by_row(width), by_row(width), by_row(LANES)],
-        out_specs=[by_row(width), by_row(width), whole(half, SLOT, span), whole(half, SLOT, span)],
+        out_specs=[
+            by_row(width),
+            by_row(width),
+            whole(width, width),
+            whole(half, SLOT, span),
+            whole(half, SLOT, span),
+        ],
         out_shape=[
             jax.ShapeDtypeStruct((rows, width), BF16),
-            jax.ShapeDtypeStruct((rows, width), BF16),
+            pltpu.VMEM((rows, width), BF16),
+            jax.ShapeDtypeStruct((width, width), BF16),
             jax.ShapeDtypeStruct((half, SLOT, span), F32),
             jax.ShapeDtypeStruct((half, SLOT, span), BF16),
         ],
-        scratch_shapes=[square(BF16)] * 6
+        scratch_shapes=[square(BF16)] * 5
         + [square(F32)] * 2
         + [
             pltpu.VMEM((8, width), F32),
@@ -267,19 +311,27 @@
         gathered = [blocks[4 * k : 4 * k + 4] for k in range(8)]
         masks = list(range(slots))
         weights, _ = weigh(dir_a)
-    layer_output, input_grad, keep, send = layers(
+    tile = pick_tile(rows)
+    tiles = rows // tile
+    first = tiles * 5 // 8
+    layer_output, grads, weight, keep, send = layers(
         place, gathered, layer_input, cotangent, weights, masks
     )
     if fast:
         total = keep + swap(send, 8, groups).astype(F32)
         parts = [total[4 * k : 4 * k + 4] for k in range(4)]
         came = [swap(parts[k].astype(BF16), m, groups) for k, m in ((1, 1), (2, 16), (3, 17))]
-        total = parts[0] + sum(v.astype(F32) for v in came)
+        input_grad, held = input_grads(grads, weight, parts[0], None, tile, 0, first)
+        total = held + sum(v.astype(F32) for v in came)
         came = [swap(total[k].astype(BF16), m, groups) for k, m in ((1, 2), (2, 4), (3, 6))]
-        total = total[0] + sum(v.astype(F32) for v in came)
+        input_grad, held = input_grads(
+            grads, weight, total[0], input_grad, tile, first, tiles - first
+        )
+        total = held + sum(v.astype(F32) for v in came)
         vectors = total[0:4, 2 * width : 2 * width + SLOT]
         grad_a, grad_b = total[:, :width], total[:, width : 2 * width]
     else:
+        input_grad, _ = input_grads(grads, weight, keep[0], None, tile, 0, tiles)
         total = jnp.concatenate([keep, send.astype(F32)], axis=0)
         scatter = lambda v, d: lax.psum_scatter(v, AXES, scatter_dimension=d, tiled=True)
         square = total[:, :, : 2 * width].reshape(width, 2 * width)

time: 96.5 us -> 90.8 us (0.941)
  waiting for transfers between devices: 20.4 us -> 9.91 us
  Pallas kernels: 52.1 us -> 56.8 us
    ppermute x17, waiting for transfers between devices: 20.4 us -> 9.91 us  [swap(): return lax.ppermute(value, AXES, [(k, k ^ mask) for k in range(groups)])]
    pallas_call x0 -> x2, Pallas kernels: none -> 10.4 us  [input_grads(): pl.pallas_call(input_grad_kernel, grid=(count,), in_specs=[by_row, pl.Blo...]
    pallas_call x1, Pallas kernels: 50 us -> 44.3 us  [layers(): pl.pallas_call(functools.partial(layers_kernel, masks, parts), grid=(rows...]
  transfers between devices with their start and end apart: 17 -> 17, of which waited for: 9 -> 7; matrix products, arithmetic and copies ran while one was open for 0% -> 0% of each run, Pallas kernels for 2% -> 14%
where the time goes in v3:
time: 90.8 us; the launch traced here: 90.4 us
  Pallas kernels  56.8 us (63%)
  starting transfers between devices  17.8 us (20%)
  waiting for transfers between devices  9.91 us (11%)
  local copies, waits for them, and re-layouts  3.33 us (4%)
  other arithmetic  1.79 us (2%)
    pallas_call x1, Pallas kernels, layers(): pl.pallas_call(functools.partial(layers_kernel, masks, parts), grid=(rows...  44.3 us
    ppermute x17, starting transfers between devices, swap(): return lax.ppermute(value, AXES, [(k, k ^ mask) for k in range(groups)])  17.8 us
    pallas_call x2, Pallas kernels, input_grads(): pl.pallas_call(input_grad_kernel, grid=(count,), in_specs=[by_row, pl.Blo...  10.4 us
    ppermute x17, waiting for transfers between devices, swap(): return lax.ppermute(value, AXES, [(k, k ^ mask) for k in range(groups)])  9.91 us
    pallas_call x1, Pallas kernels, point_weights(): pl.pallas_call(functools.partial(point_weight_kernel, average), grid=(ste...  2.16 us
    unnamed x9, local copies, waits for them, and re-layouts  1.99 us
  transfers between devices with their start and end apart: 17, of which 7 were waited for; matrix products, arithmetic and copies ran while one was open for 0% of the time, Pallas kernels for 14%

profile of v3, /device:TPU:0, one launch (start us, length us, event | category | flops | bytes accessed | tf_op | source)
XLA Modules:
  0.0 90.4 jit_solution(9441149074777635059)
XLA Ops:
  0.6 0.7 pad_maximum_fusion
  1.4 0.1 copy.24
  1.4 0.7 fusion.2.mine_ref
  2.2 5.0 %collective-permute-start.2 = (bf16[1,16,1152]{2,1,0:T(8,128)(2,1)S(1)}, bf16[1,16,1152]{2,1,0:T(8,128)(2,1)S(1)}, u32[]{:S(2)}, u32[]{:S(2)}) collective-permute-start(bf16[1,16,1152]{2,1,0:T(8,128)(2,1)S(1)} %fusion.2.mine_ref), channel_id=1, source_target_pairs={{0,6},{1,7},{2,4},{3,5},{4,2},{5,3},{6,0},{7,1},{8,14},{9,15},{10,... | collective-permute-start | bytes 110600 | tf_op jit(solution)/shard_map/ppermute | solution.py:267
  7.2 0.0 collective-permute-start.1
  7.2 0.6 collective-permute-start
  7.9 0.1 pad_add_fusion.place_ref.refs_0_
  8.0 0.7 copy-done
  8.6 0.7 copy-done.1
  9.3 0.7 copy-done.2
  9.9 2.2 %point_weight.1 = (bf16[11776,128]{1,0:T(8,128)(2,1)S(1)}, bf16[1,16,1152]{2,1,0:T(8,128)(2,1)S(1)}) custom-call(s32[2]{0:T(128)S(1)} %pad_add_fusion.place_ref.refs_0_, s32[13]{0:T(128)S(1)} %copy-done, s32[64]{0:T(128)S(1)} %copy-done.1, s32[64]{0:T(128)S(1)} %copy-done.2, bf16[1,16,1152]{2,1,0:T(8,128)(2,1)S(1)} %fusion.2.mine_ref), custom_call_target="tpu_custom_call" | custom-call | flops 75366400 | bytes 3014656 | tf_op jit(solution)/shard_map/point_weight/pallas_call | solution.py:70
  12.1 0.0 collective-permute-done
  12.1 0.0 collective-permute-done.1
  12.1 0.0 collective-permute-done.2
  12.2 2.7 %collective-permute-start.5 = (bf16[4,16,1152]{2,1,0:T(8,128)(2,1)S(1)}, bf16[4,16,1152]{2,1,0:T(8,128)(2,1)S(1)}, u32[]{:S(2)}, u32[]{:S(2)}) collective-permute-start(bf16[4,16,1152]{2,1,0:T(8,128)(2,1)S(1)} %constant_dynamic-update-slice_fusion.refs_1_), channel_id=1, source_target_pairs={{0,17},{1,16},{2,19},{3,18},{4,21},{5,20},{6,23},{7,22},{8,25},{9,... | collective-permute-start | bytes 442376 | tf_op jit(solution)/shard_map/ppermute | solution.py:267
  14.8 0.5 collective-permute-start.4
  15.4 0.4 collective-permute-start.3
  15.7 0.0 collective-permute-start.6
  15.7 4.0 %collective-permute-done.5.refs_4_ = bf16[4,16,1152]{2,1,0:T(8,128)(2,1)S(1)} collective-permute-done((bf16[4,16,1152]{2,1,0:T(8,128)(2,1)S(1)}, bf16[4,16,1152]{2,1,0:T(8,128)(2,1)S(1)}, u32[]{:S(2)}, u32[]{:S(2)}) %collective-permute-start.5) | collective-permute-done | bytes 147488 | tf_op jit(solution)/shard_map/ppermute | solution.py:267
  19.8 0.0 collective-permute-start.9
  19.8 1.6 %collective-permute-done.4.refs_3_ = bf16[4,16,1152]{2,1,0:T(8,128)(2,1)S(1)} collective-permute-done((bf16[4,16,1152]{2,1,0:T(8,128)(2,1)S(1)}, bf16[4,16,1152]{2,1,0:T(8,128)(2,1)S(1)}, u32[]{:S(2)}, u32[]{:S(2)}) %collective-permute-start.4) | collective-permute-done | bytes 147488 | tf_op jit(solution)/shard_map/ppermute | solution.py:267
  21.4 0.0 collective-permute-start.8
  21.4 0.0 collective-permute-done.3.refs_2_
  21.4 0.5 collective-permute-start.7
  21.9 0.0 collective-permute-done.6.refs_5_
  21.9 0.0 collective-permute-done.9.refs_8_
  21.9 0.9 collective-permute-done.8.refs_7_
  22.8 0.2 collective-permute-done.7.refs_6_
  23.0 44.3 %layers.1 = (bf16[11776,512]{1,0:T(8,128)(2,1)}, bf16[11776,512]{1,0:T(8,128)(2,1)S(1)}, bf16[512,512]{1,0:T(8,128)(2,1)S(1)}, f32[16,16,1152]{2,1,0:T(8,128)S(1)}, bf16[16,16,1152]{2,1,0:T(8,128)(2,1)S(1)}) custom-call(s32[2]{0:T(128)S(1)} %pad_add_fusion.place_ref.refs_0_, bf16[4,16,1152]{2,1,0:T(8,128)(2,1)S(1)} %constant_dynamic-update-slice_fusion.refs_1_, ...), custom_call_target="tpu_custom_call" | custom-call | tf_op jit(solution)/shard_map/layers/pallas_call | solution.py:232
  67.2 0.4 collective-permute-start.10
  67.6 1.7 %collective-permute-done.10 = bf16[16,16,1152]{2,1,0:T(8,128)(2,1)S(1)} collective-permute-done((bf16[16,16,1152]{2,1,0:T(8,128)(2,1)S(1)}, bf16[16,16,1152]{2,1,0:T(8,128)(2,1)S(1)}, u32[]{:S(2)}, u32[]{:S(2)}) %collective-permute-start.10) | collective-permute-done | bytes 589856 | tf_op jit(solution)/shard_map/ppermute | solution.py:267
  69.3 0.2 fusion.4
  69.5 1.3 %collective-permute-start.11 = (bf16[4,16,1152]{2,1,0:T(8,128)(2,1)S(1)}, bf16[4,16,1152]{2,1,0:T(8,128)(2,1)S(1)}, u32[]{:S(2)}, u32[]{:S(2)}) collective-permute-start(bf16[4,16,1152]{2,1,0:T(8,128)(2,1)S(1)} %get-tuple-element.34), channel_id=1, source_target_pairs={{0,1},{1,0},{2,3},{3,2},{4,5},{5,4},{6,7},{7,6},{8,9},{9,8},{10,11... | collective-permute-start | bytes 442376 | tf_op jit(solution)/shard_map/ppermute | solution.py:267
  70.8 1.7 %collective-permute-start.13 = (bf16[4,16,1152]{2,1,0:T(8,128)(2,1)S(1)}, bf16[4,16,1152]{2,1,0:T(8,128)(2,1)S(1)}, u32[]{:S(2)}, u32[]{:S(2)}) collective-permute-start(bf16[4,16,1152]{2,1,0:T(8,128)(2,1)S(1)} %get-tuple-element.35), channel_id=1, source_target_pairs={{0,17},{1,16},{2,19},{3,18},{4,21},{5,20},{6,23},{7,22},{8,25},{9,... | collective-permute-start | bytes 442376 | tf_op jit(solution)/shard_map/ppermute | solution.py:267
  72.5 0.5 collective-permute-start.12
  73.1 6.3 %input_grad.2 = (bf16[11776,512]{1,0:T(8,128)(2,1)}, f32[4,16,1152]{2,1,0:T(8,128)S(1)}) custom-call(bf16[11776,512]{1,0:T(8,128)(2,1)S(1)} %get-tuple-element.22.grad_ref, bf16[512,512]{1,0:T(8,128)(2,1)S(1)} %get-tuple-element.23.w_ref, f32[4,16,1152]{2,1,0:T(8,128)S(1)} %slice.67.held_ref), custom_call_target="tpu_custom_call" | custom-call | flops 3858759680 | bytes 15073280 | tf_op jit(solution)/shard_map/input_grad/pallas_call | solution.py:103
  79.4 0.0 collective-permute-done.11
  79.4 0.0 collective-permute-done.13
  79.4 0.7 collective-permute-done.12
  80.0 0.1 fusion.3
  80.1 1.5 %collective-permute-start.14 = (bf16[16,1152]{1,0:T(8,128)(2,1)S(1)}, bf16[16,1152]{1,0:T(8,128)(2,1)S(1)}, u32[]{:S(2)}, u32[]{:S(2)}) collective-permute-start(bf16[16,1152]{1,0:T(8,128)(2,1)S(1)} %get-tuple-element.37), channel_id=1, source_target_pairs={{0,2},{1,3},{2,0},{3,1},{4,6},{5,7},{6,4},{7,5},{8,10},{9,11},{10,... | collective-permute-start | bytes 110600 | tf_op jit(solution)/shard_map/ppermute | solution.py:267
  81.6 2.4 %collective-permute-start.16 = (bf16[16,1152]{1,0:T(8,128)(2,1)S(1)}, bf16[16,1152]{1,0:T(8,128)(2,1)S(1)}, u32[]{:S(2)}, u32[]{:S(2)}) collective-permute-start(bf16[16,1152]{1,0:T(8,128)(2,1)S(1)} %get-tuple-element.38), channel_id=1, source_target_pairs={{0,6},{1,7},{2,4},{3,5},{4,2},{5,3},{6,0},{7,1},{8,14},{9,15},{10,... | collective-permute-start | bytes 110600 | tf_op jit(solution)/shard_map/ppermute | solution.py:267
  83.9 0.3 collective-permute-start.15
  84.2 4.1 %input_grad.3 = (bf16[11776,512]{1,0:T(8,128)(2,1)}, f32[16,1152]{1,0:T(8,128)S(1)}) custom-call(bf16[11776,512]{1,0:T(8,128)(2,1)S(1)} %get-tuple-element.22.grad_ref, bf16[512,512]{1,0:T(8,128)(2,1)S(1)} %get-tuple-element.23.w_ref, f32[16,1152]{1,0:T(8,128)S(1)} %slice_bitcast_fusion.held_ref, ...), custom_call_target="tpu_custom_call", output_to_operand_aliasing={{0}: (3, {})} | custom-call | flops 2315255808 | bytes 9043968 | tf_op jit(solution)/shard_map/input_grad/pallas_call | solution.py:103
  88.4 0.0 collective-permute-done.16
  88.4 0.8 collective-permute-done.15
  89.2 0.5 slice_bitcast_fusion.4
  89.8 0.6 fusion.6
  (13 shorter events, 0.1 us)
Async XLA Ops:
  2.2 10.0 %collective-permute-start.2 = (bf16[1,16,1152]{2,1,0:T(8,128)(2,1)S(1)}, bf16[1,16,1152]{2,1,0:T(8,128)(2,1)S(1)}, u32[]{:S(2)}, u32[]{:S(2)}) collective-permute-start(bf16[1,16,1152]{2,1,0:T(8,128)(2,1)S(1)} %fusion.2.mine_ref), channel_id=1, source_target_pairs={{0,6},{1,7},{2,4},{3,5},{4,2},{5,3},{6,0},{7,1},{8,14},{9,15},{10,... | collective-permute-start | bytes 110600 | tf_op jit(solution)/shard_map/ppermute | solution.py:267
  7.2 4.9 %collective-permute-start.1 = (bf16[1,16,1152]{2,1,0:T(8,128)(2,1)S(1)}, bf16[1,16,1152]{2,1,0:T(8,128)(2,1)S(1)}, u32[]{:S(2)}, u32[]{:S(2)}) collective-permute-start(bf16[1,16,1152]{2,1,0:T(8,128)(2,1)S(1)} %fusion.2.mine_ref), channel_id=1, source_target_pairs={{0,4},{1,5},{2,6},{3,7},{4,0},{5,1},{6,2},{7,3},{8,12},{9,13},{10,... | collective-permute-start | bytes 110600 | tf_op jit(solution)/shard_map/ppermute | solution.py:267
  7.2 4.9 %collective-permute-start = (bf16[1,16,1152]{2,1,0:T(8,128)(2,1)S(1)}, bf16[1,16,1152]{2,1,0:T(8,128)(2,1)S(1)}, u32[]{:S(2)}, u32[]{:S(2)}) collective-permute-start(bf16[1,16,1152]{2,1,0:T(8,128)(2,1)S(1)} %fusion.2.mine_ref), channel_id=1, source_target_pairs={{0,2},{1,3},{2,0},{3,1},{4,6},{5,7},{6,4},{7,5},{8,10},{9,11},{10,... | collective-permute-start | bytes 110600 | tf_op jit(solution)/shard_map/ppermute | solution.py:267
  8.0 0.7 copy-start
  8.6 0.7 copy-start.1
  9.3 0.7 copy-start.2
  12.2 7.6 %collective-permute-start.5 = (bf16[4,16,1152]{2,1,0:T(8,128)(2,1)S(1)}, bf16[4,16,1152]{2,1,0:T(8,128)(2,1)S(1)}, u32[]{:S(2)}, u32[]{:S(2)}) collective-permute-start(bf16[4,16,1152]{2,1,0:T(8,128)(2,1)S(1)} %constant_dynamic-update-slice_fusion.refs_1_), channel_id=1, source_target_pairs={{0,17},{1,16},{2,19},{3,18},{4,21},{5,20},{6,23},{7,22},{8,25},{9,... | collective-permute-start | bytes 442376 | tf_op jit(solution)/shard_map/ppermute | solution.py:267
  14.8 6.5 %collective-permute-start.4 = (bf16[4,16,1152]{2,1,0:T(8,128)(2,1)S(1)}, bf16[4,16,1152]{2,1,0:T(8,128)(2,1)S(1)}, u32[]{:S(2)}, u32[]{:S(2)}) collective-permute-start(bf16[4,16,1152]{2,1,0:T(8,128)(2,1)S(1)} %constant_dynamic-update-slice_fusion.refs_1_), channel_id=1, source_target_pairs={{0,16},{1,17},{2,18},{3,19},{4,20},{5,21},{6,22},{7,23},{8,24},{9,... | collective-permute-start | bytes 442376 | tf_op jit(solution)/shard_map/ppermute | solution.py:267
  15.4 6.0 %collective-permute-start.3 = (bf16[4,16,1152]{2,1,0:T(8,128)(2,1)S(1)}, bf16[4,16,1152]{2,1,0:T(8,128)(2,1)S(1)}, u32[]{:S(2)}, u32[]{:S(2)}) collective-permute-start(bf16[4,16,1152]{2,1,0:T(8,128)(2,1)S(1)} %constant_dynamic-update-slice_fusion.refs_1_), channel_id=1, source_target_pairs={{0,1},{1,0},{2,3},{3,2},{4,5},{5,4},{6,7},{7,6},{8,9},{9,8},{10,11... | collective-permute-start | bytes 442376 | tf_op jit(solution)/shard_map/ppermute | solution.py:267
  15.7 6.2 %collective-permute-start.6 = (bf16[4,16,1152]{2,1,0:T(8,128)(2,1)S(1)}, bf16[4,16,1152]{2,1,0:T(8,128)(2,1)S(1)}, u32[]{:S(2)}, u32[]{:S(2)}) collective-permute-start(bf16[4,16,1152]{2,1,0:T(8,128)(2,1)S(1)} %constant_dynamic-update-slice_fusion.refs_1_), channel_id=1, source_target_pairs={{0,8},{1,9},{2,10},{3,11},{4,12},{5,13},{6,14},{7,15},{8,0},{9,1},... | collective-permute-start | bytes 442376 | tf_op jit(solution)/shard_map/ppermute | solution.py:267
  19.8 2.1 %collective-permute-start.9 = (bf16[4,16,1152]{2,1,0:T(8,128)(2,1)S(1)}, bf16[4,16,1152]{2,1,0:T(8,128)(2,1)S(1)}, u32[]{:S(2)}, u32[]{:S(2)}) collective-permute-start(bf16[4,16,1152]{2,1,0:T(8,128)(2,1)S(1)} %collective-permute-done.5.refs_4_), channel_id=1, source_target_pairs={{0,8},{1,9},{2,10},{3,11},{4,12},{5,13},{6,14},{7,15},{8,0},{9,1},... | collective-permute-start | bytes 442376 | tf_op jit(solution)/shard_map/ppermute | solution.py:267
  21.4 1.4 %collective-permute-start.8 = (bf16[4,16,1152]{2,1,0:T(8,128)(2,1)S(1)}, bf16[4,16,1152]{2,1,0:T(8,128)(2,1)S(1)}, u32[]{:S(2)}, u32[]{:S(2)}) collective-permute-start(bf16[4,16,1152]{2,1,0:T(8,128)(2,1)S(1)} %collective-permute-done.4.refs_3_), channel_id=1, source_target_pairs={{0,8},{1,9},{2,10},{3,11},{4,12},{5,13},{6,14},{7,15},{8,0},{9,1},... | collective-permute-start | bytes 442376 | tf_op jit(solution)/shard_map/ppermute | solution.py:267
  21.4 1.6 %collective-permute-start.7 = (bf16[4,16,1152]{2,1,0:T(8,128)(2,1)S(1)}, bf16[4,16,1152]{2,1,0:T(8,128)(2,1)S(1)}, u32[]{:S(2)}, u32[]{:S(2)}) collective-permute-start(bf16[4,16,1152]{2,1,0:T(8,128)(2,1)S(1)} %collective-permute-done.3.refs_2_), channel_id=1, source_target_pairs={{0,8},{1,9},{2,10},{3,11},{4,12},{5,13},{6,14},{7,15},{8,0},{9,1},... | collective-permute-start | bytes 442376 | tf_op jit(solution)/shard_map/ppermute | solution.py:267
  67.2 2.1 %collective-permute-start.10 = (bf16[16,16,1152]{2,1,0:T(8,128)(2,1)S(1)}, bf16[16,16,1152]{2,1,0:T(8,128)(2,1)S(1)}, u32[]{:S(2)}, u32[]{:S(2)}) collective-permute-start(bf16[16,16,1152]{2,1,0:T(8,128)(2,1)S(1)} %get-tuple-element.25), channel_id=1, source_target_pairs={{0,8},{1,9},{2,10},{3,11},{4,12},{5,13},{6,14},{7,15},{8,0},{9,1},... | collective-permute-start | bytes 1769480 | tf_op jit(solution)/shard_map/ppermute | solution.py:267
  69.5 9.8 %collective-permute-start.11 = (bf16[4,16,1152]{2,1,0:T(8,128)(2,1)S(1)}, bf16[4,16,1152]{2,1,0:T(8,128)(2,1)S(1)}, u32[]{:S(2)}, u32[]{:S(2)}) collective-permute-start(bf16[4,16,1152]{2,1,0:T(8,128)(2,1)S(1)} %get-tuple-element.34), channel_id=1, source_target_pairs={{0,1},{1,0},{2,3},{3,2},{4,5},{5,4},{6,7},{7,6},{8,9},{9,8},{10,11... | collective-permute-start | bytes 442376 | tf_op jit(solution)/shard_map/ppermute | solution.py:267
  70.8 8.5 %collective-permute-start.13 = (bf16[4,16,1152]{2,1,0:T(8,128)(2,1)S(1)}, bf16[4,16,1152]{2,1,0:T(8,128)(2,1)S(1)}, u32[]{:S(2)}, u32[]{:S(2)}) collective-permute-start(bf16[4,16,1152]{2,1,0:T(8,128)(2,1)S(1)} %get-tuple-element.35), channel_id=1, source_target_pairs={{0,17},{1,16},{2,19},{3,18},{4,21},{5,20},{6,23},{7,22},{8,25},{9,... | collective-permute-start | bytes 442376 | tf_op jit(solution)/shard_map/ppermute | solution.py:267
  72.5 7.5 %collective-permute-start.12 = (bf16[4,16,1152]{2,1,0:T(8,128)(2,1)S(1)}, bf16[4,16,1152]{2,1,0:T(8,128)(2,1)S(1)}, u32[]{:S(2)}, u32[]{:S(2)}) collective-permute-start(bf16[4,16,1152]{2,1,0:T(8,128)(2,1)S(1)} %get-tuple-element.36), channel_id=1, source_target_pairs={{0,16},{1,17},{2,18},{3,19},{4,20},{5,21},{6,22},{7,23},{8,24},{9,... | collective-permute-start | bytes 442376 | tf_op jit(solution)/shard_map/ppermute | solution.py:267
  80.1 8.3 %collective-permute-start.14 = (bf16[16,1152]{1,0:T(8,128)(2,1)S(1)}, bf16[16,1152]{1,0:T(8,128)(2,1)S(1)}, u32[]{:S(2)}, u32[]{:S(2)}) collective-permute-start(bf16[16,1152]{1,0:T(8,128)(2,1)S(1)} %get-tuple-element.37), channel_id=1, source_target_pairs={{0,2},{1,3},{2,0},{3,1},{4,6},{5,7},{6,4},{7,5},{8,10},{9,11},{10,... | collective-permute-start | bytes 110600 | tf_op jit(solution)/shard_map/ppermute | solution.py:267
  81.6 6.8 %collective-permute-start.16 = (bf16[16,1152]{1,0:T(8,128)(2,1)S(1)}, bf16[16,1152]{1,0:T(8,128)(2,1)S(1)}, u32[]{:S(2)}, u32[]{:S(2)}) collective-permute-start(bf16[16,1152]{1,0:T(8,128)(2,1)S(1)} %get-tuple-element.38), channel_id=1, source_target_pairs={{0,6},{1,7},{2,4},{3,5},{4,2},{5,3},{6,0},{7,1},{8,14},{9,15},{10,... | collective-permute-start | bytes 110600 | tf_op jit(solution)/shard_map/ppermute | solution.py:267
  83.9 5.3 %collective-permute-start.15 = (bf16[16,1152]{1,0:T(8,128)(2,1)S(1)}, bf16[16,1152]{1,0:T(8,128)(2,1)S(1)}, u32[]{:S(2)}, u32[]{:S(2)}) collective-permute-start(bf16[16,1152]{1,0:T(8,128)(2,1)S(1)} %get-tuple-element.39), channel_id=1, source_target_pairs={{0,4},{1,5},{2,6},{3,7},{4,0},{5,1},{6,2},{7,3},{8,12},{9,13},{10,... | collective-permute-start | bytes 110600 | tf_op jit(solution)/shard_map/ppermute | solution.py:267

commit v4 on v3

--- a/solution.py
+++ b/solution.py
@@ -131,13 +131,34 @@
 def layers_kernel(masks, parts, *refs):
     gathered = refs[1:9]
     place_ref = refs[0]
-    x_ref, cot_ref, pw_ref = refs[9:12]
-    out_ref, grad_ref, wt_a, keep_ref, send_ref = refs[12:17]
-    dir_a, dir_b, w_a, w_b, wt_b, gw_a, gw_b, vec, gsum, landed, columns, arrived = refs[17:]
-    step = pl.program_id(0)
-    width = x_ref.shape[1]
-    tile = x_ref.shape[0]
+    sources = refs[9:12]
+    out_hbm, grad_ref, wt_a, keep_ref, send_ref = refs[12:17]
+    dir_a, dir_b, w_a, w_b, wt_b, gw_a, gw_b, vec, gsum, landed, columns, arrived = refs[17:29]
+    held, out_held, came, left = refs[29:32], refs[32], refs[33], refs[34]
+    step, steps = pl.program_id(0), pl.num_programs(0)
+    tile, width = held[0].shape[1:]
     sub = tile // parts
+    slot_now = lax.rem(step, 2)
+    x_ref, cot_ref, pw_ref = [ref.at[slot_now] for ref in held]
+    out_ref = out_held.at[slot_now]
+
+    def fetches(index):
+        rows = pl.ds(pl.multiple_of(index * tile, tile), tile)
+        place = lax.rem(index, 2)
+        return [
+            pltpu.make_async_copy(source.at[rows, :], ref.at[place], came.at[k, place])
+            for k, (source, ref) in enumerate(zip(sources, held))
+        ]
+
+    def leaving(index):
+        rows = pl.ds(pl.multiple_of(index * tile, tile), tile)
+        place = lax.rem(index, 2)
+        return pltpu.make_async_copy(out_held.at[place], out_hbm.at[rows, :], left.at[place])
+
+    @pl.when(step == 0)
+    def _():
+        for copy in fetches(0):
+            copy.start()
 
     def owner(slot):
         return place_ref[0] ^ masks[slot]
@@ -174,6 +195,17 @@
         gw_b[...] = jnp.zeros_like(gw_b)
         gsum[...] = jnp.zeros_like(gsum)
 
+    @pl.when(step + 1 < steps)
+    def _():
+        for copy in fetches(step + 1):
+            copy.start()
+
+    @pl.when(step >= 2)
+    def _():
+        leaving(step - 2).wait()
+
+    for copy in fetches(step):
+        copy.wait()
     spans = [pl.ds(k * sub, sub) for k in range(parts)]
     hidden, slope_a = zip(
         *[activate(dot(x_ref[s, :], w_a[...]) + vec[0:1, :]) for s in spans]
@@ -184,6 +216,7 @@
         out_ref[s, :] = value
         weight = jnp.concatenate([pw_ref[s, :]] * (width // LANES), axis=1)
         grads.append((cot_ref[s, :] * weight) * slope_b)
+    leaving(step).start()
     grads_a = [dot(g, wt_b[...]).astype(BF16) * sa for g, sa in zip(grads, slope_a)]
     for s, g in zip(spans, grads_a):
         grad_ref[s, :] = g
@@ -196,7 +229,7 @@
     gw_a[...] += both[:width]
     gsum[0:8, :] += both[width : width + 8]
 
-    @pl.when(step == pl.num_programs(0) - 1)
+    @pl.when(step == steps - 1)
     def _():
         small = []
         for k, (direction, gw) in enumerate(((dir_a, gw_a), (dir_b, gw_b))):
@@ -219,6 +252,12 @@
             else:
                 send_ref[slot - len(masks) // 2] = block.astype(BF16)
 
+        @pl.when(steps > 1)
+        def _():
+            leaving(step - 1).wait()
+
+        leaving(step).wait()
+
 
 def layers(place, gathered, layer_input, cotangent, weights, masks):
     rows, width = layer_input.shape
@@ -234,9 +273,9 @@
         grid=(rows // tile,),
         in_specs=[pl.BlockSpec(memory_space=pltpu.SMEM)]
         + [pl.BlockSpec(memory_space=pl.ANY)] * 8
-        + [by_row(width), by_row(width), by_row(LANES)],
+        + [pl.BlockSpec(memory_space=pl.ANY)] * 3,
         out_specs=[
-            by_row(width),
+            pl.BlockSpec(memory_space=pl.ANY),
             by_row(width),
             whole(width, width),
             whole(half, SLOT, span),
@@ -257,6 +296,12 @@
             pltpu.VMEM((8, 4, SLOT, span), BF16),
             pltpu.VMEM((width, LANES), F32),
             pltpu.SemaphoreType.DMA((8,)),
+            pltpu.VMEM((2, tile, width), BF16),
+            pltpu.VMEM((2, tile, width), BF16),
+            pltpu.VMEM((2, tile, LANES), BF16),
+            pltpu.VMEM((2, tile, width), BF16),
+            pltpu.SemaphoreType.DMA((3, 2)),
+            pltpu.SemaphoreType.DMA((2,)),
         ],
         compiler_params=pltpu.CompilerParams(vmem_limit_bytes=VMEM_BYTES),
         name="layers",
@@ -296,10 +341,10 @@
     if fast:
         extra = jnp.pad(small.T, ((0, 0), (0, LANES - 4)))
         mine = jnp.concatenate([dir_a, dir_b, extra], axis=1)[None]
-        weights, same = weigh(mine)
-        near = [same] + [swap(mine, m, groups) for m in (2, 4, 6)]
+        near = [mine] + [swap(mine, m, groups) for m in (2, 4, 6)]
         near = jnp.concatenate(near, axis=0)
-        wide = [near] + [swap(near, m, groups) for m in (1, 16, 17)]
+        weights, same = weigh(near)
+        wide = [same] + [swap(near, m, groups) for m in (1, 16, 17)]
         gathered = wide + [swap(v, 8, groups) for v in wide]
         masks = [c ^ xy ^ z for c in (0, 8) for xy in (0, 1, 16, 17) for z in (0, 2, 4, 6)]
     else:

time: 90.8 us -> 87.9 us (0.968)
  waiting for transfers between devices: 9.91 us -> 8.35 us
  Pallas kernels: 56.8 us -> 55.5 us
    ppermute x17, waiting for transfers between devices: 9.91 us -> 8.35 us  [swap(): return lax.ppermute(value, AXES, [(k, k ^ mask) for k in range(groups)])]
    pallas_call x1, Pallas kernels: 44.3 us -> 42.9 us  [layers(): pl.pallas_call(functools.partial(layers_kernel, masks, parts), grid=(rows...]
    unnamed x9 -> x6, local copies, waits for them, and re-layouts: 1.99 us -> 1.96 us
  transfers between devices with their start and end apart: 17 -> 17, of which waited for: 7 -> 9; matrix products, arithmetic and copies ran while one was open for 0% -> 0% of each run, Pallas kernels for 14% -> 14%
where the time goes in v4:
time: 87.9 us; the launch traced here: 87.5 us
  Pallas kernels  55.5 us (63%)
  starting transfers between devices  17.8 us (20%)
  waiting for transfers between devices  8.35 us (9%)
  local copies, waits for them, and re-layouts  3.29 us (4%)
  other arithmetic  1.81 us (2%)
    pallas_call x1, Pallas kernels, layers(): pl.pallas_call(functools.partial(layers_kernel, masks, parts), grid=(rows...  42.9 us
    ppermute x17, starting transfers between devices, swap(): return lax.ppermute(value, AXES, [(k, k ^ mask) for k in range(groups)])  17.8 us
    pallas_call x2, Pallas kernels, input_grads(): pl.pallas_call(input_grad_kernel, grid=(count,), in_specs=[by_row, pl.Blo...  10.4 us
    ppermute x17, waiting for transfers between devices, swap(): return lax.ppermute(value, AXES, [(k, k ^ mask) for k in range(groups)])  8.35 us
    pallas_call x1, Pallas kernels, point_weights(): pl.pallas_call(functools.partial(point_weight_kernel, average), grid=(ste...  2.16 us
    unnamed x6, local copies, waits for them, and re-layouts  1.96 us
  transfers between devices with their start and end apart: 17, of which 9 were waited for; matrix products, arithmetic and copies ran while one was open for 0% of the time, Pallas kernels for 14%

profile of v4, /device:TPU:0, one launch (start us, length us, event | category | flops | bytes accessed | tf_op | source)
XLA Modules:
  0.0 87.5 jit_solution(7805764716283872702)
XLA Ops:
  0.6 0.7 pad_maximum_fusion.1
  1.4 0.1 copy.24
  1.4 0.7 fusion.2
  2.2 5.0 %collective-permute-start.2 = (bf16[1,16,1152]{2,1,0:T(8,128)(2,1)S(1)}, bf16[1,16,1152]{2,1,0:T(8,128)(2,1)S(1)}, u32[]{:S(2)}, u32[]{:S(2)}) collective-permute-start(bf16[1,16,1152]{2,1,0:T(8,128)(2,1)S(1)} %fusion.2), channel_id=1, source_target_pairs={{0,6},{1,7},{2,4},{3,5},{4,2},{5,3},{6,0},{7,1},{8,14},{9,15},{10,... | collective-permute-start | bytes 110600 | tf_op jit(solution)/shard_map/ppermute | solution.py:312
  7.2 0.0 collective-permute-start.1
  7.2 0.6 collective-permute-start
  7.9 1.3 %collective-permute-done.2 = bf16[1,16,1152]{2,1,0:T(8,128)(2,1)S(1)} collective-permute-done((bf16[1,16,1152]{2,1,0:T(8,128)(2,1)S(1)}, bf16[1,16,1152]{2,1,0:T(8,128)(2,1)S(1)}, u32[]{:S(2)}, u32[]{:S(2)}) %collective-permute-start.2) | collective-permute-done | bytes 36896 | tf_op jit(solution)/shard_map/ppermute | solution.py:312
  9.2 2.9 %collective-permute-done.1 = bf16[1,16,1152]{2,1,0:T(8,128)(2,1)S(1)} collective-permute-done((bf16[1,16,1152]{2,1,0:T(8,128)(2,1)S(1)}, bf16[1,16,1152]{2,1,0:T(8,128)(2,1)S(1)}, u32[]{:S(2)}, u32[]{:S(2)}) %collective-permute-start.1) | collective-permute-done | bytes 36896 | tf_op jit(solution)/shard_map/ppermute | solution.py:312
  12.1 0.0 collective-permute-done
  12.1 2.5 %collective-permute-start.5 = (bf16[4,16,1152]{2,1,0:T(8,128)(2,1)S(1)}, bf16[4,16,1152]{2,1,0:T(8,128)(2,1)S(1)}, u32[]{:S(2)}, u32[]{:S(2)}) collective-permute-start(bf16[4,16,1152]{2,1,0:T(8,128)(2,1)S(1)} %pad_maximum_fusion.mine_ref), channel_id=1, source_target_pairs={{0,17},{1,16},{2,19},{3,18},{4,21},{5,20},{6,23},{7,22},{8,25},{9,... | collective-permute-start | bytes 442376 | tf_op jit(solution)/shard_map/ppermute | solution.py:312
  14.6 0.5 collective-permute-start.4
  15.2 0.5 collective-permute-start.3
  15.7 0.1 pad_add_fusion.place_ref.refs_0_
  15.8 0.7 copy-done
  16.4 0.7 copy-done.1
  17.1 0.7 copy-done.2
  17.7 2.2 %point_weight.1 = (bf16[11776,128]{1,0:T(8,128)(2,1)S(1)}, bf16[4,16,1152]{2,1,0:T(8,128)(2,1)S(1)}) custom-call(s32[2]{0:T(128)S(1)} %pad_add_fusion.place_ref.refs_0_, s32[13]{0:T(128)S(1)} %copy-done, s32[64]{0:T(128)S(1)} %copy-done.1, s32[64]{0:T(128)S(1)} %copy-done.2, bf16[4,16,1152]{2,1,0:T(8,128)(2,1)S(1)} %pad_maximum_fusion.mine_ref), custom_call_target="tpu_custom_call" | custom-call | flops 75366400 | bytes 3014656 | tf_op jit(solution)/shard_map/point_weight/pallas_call | solution.py:70
  19.9 0.1 collective-permute-start.6
  20.0 0.0 collective-permute-done.5.refs_4_
  20.0 0.5 collective-permute-start.9
  20.5 0.0 collective-permute-done.4.refs_3_
  20.5 0.1 collective-permute-start.8
  20.6 0.0 collective-permute-done.3.refs_2_
  20.6 0.4 collective-permute-start.7
  21.0 0.3 collective-permute-done.6.refs_5_
  21.3 0.2 collective-permute-done.9.refs_8_
  21.5 0.3 collective-permute-done.8.refs_7_
  21.9 0.2 collective-permute-done.7.refs_6_
  22.1 42.9 %layers.1 = (bf16[11776,512]{1,0:T(8,128)(2,1)}, bf16[11776,512]{1,0:T(8,128)(2,1)S(1)}, bf16[512,512]{1,0:T(8,128)(2,1)S(1)}, f32[16,16,1152]{2,1,0:T(8,128)S(1)}, bf16[16,16,1152]{2,1,0:T(8,128)(2,1)S(1)}) custom-call(s32[2]{0:T(128)S(1)} %pad_add_fusion.place_ref.refs_0_, bf16[4,16,1152]{2,1,0:T(8,128)(2,1)S(1)} %get-tuple-element.19.refs_1_, ...), custom_call_target="tpu_custom_call" | custom-call | tf_op jit(solution)/shard_map/layers/pallas_call | solution.py:271
  65.0 0.4 collective-permute-start.10
  65.4 1.7 %collective-permute-done.10 = bf16[16,16,1152]{2,1,0:T(8,128)(2,1)S(1)} collective-permute-done((bf16[16,16,1152]{2,1,0:T(8,128)(2,1)S(1)}, bf16[16,16,1152]{2,1,0:T(8,128)(2,1)S(1)}, u32[]{:S(2)}, u32[]{:S(2)}) %collective-permute-start.10) | collective-permute-done | bytes 589856 | tf_op jit(solution)/shard_map/ppermute | solution.py:312
  67.1 0.2 fusion.4
  67.3 1.6 %collective-permute-start.11 = (bf16[4,16,1152]{2,1,0:T(8,128)(2,1)S(1)}, bf16[4,16,1152]{2,1,0:T(8,128)(2,1)S(1)}, u32[]{:S(2)}, u32[]{:S(2)}) collective-permute-start(bf16[4,16,1152]{2,1,0:T(8,128)(2,1)S(1)} %get-tuple-element.34), channel_id=1, source_target_pairs={{0,1},{1,0},{2,3},{3,2},{4,5},{5,4},{6,7},{7,6},{8,9},{9,8},{10,11... | collective-permute-start | bytes 442376 | tf_op jit(solution)/shard_map/ppermute | solution.py:312
  68.9 1.4 %collective-permute-start.13 = (bf16[4,16,1152]{2,1,0:T(8,128)(2,1)S(1)}, bf16[4,16,1152]{2,1,0:T(8,128)(2,1)S(1)}, u32[]{:S(2)}, u32[]{:S(2)}) collective-permute-start(bf16[4,16,1152]{2,1,0:T(8,128)(2,1)S(1)} %get-tuple-element.35), channel_id=1, source_target_pairs={{0,17},{1,16},{2,19},{3,18},{4,21},{5,20},{6,23},{7,22},{8,25},{9,... | collective-permute-start | bytes 442376 | tf_op jit(solution)/shard_map/ppermute | solution.py:312
  70.3 0.5 collective-permute-start.12
  70.9 6.3 %input_grad.2 = (bf16[11776,512]{1,0:T(8,128)(2,1)}, f32[4,16,1152]{2,1,0:T(8,128)S(1)}) custom-call(bf16[11776,512]{1,0:T(8,128)(2,1)S(1)} %get-tuple-element.22.grad_ref, bf16[512,512]{1,0:T(8,128)(2,1)S(1)} %get-tuple-element.23.w_ref, f32[4,16,1152]{2,1,0:T(8,128)S(1)} %slice.67.held_ref), custom_call_target="tpu_custom_call" | custom-call | flops 3858759680 | bytes 15073280 | tf_op jit(solution)/shard_map/input_grad/pallas_call | solution.py:103
  77.1 0.0 collective-permute-done.11
  77.1 0.0 collective-permute-done.13
  77.1 0.7 collective-permute-done.12
  77.8 0.1 fusion.3
  77.9 0.3 collective-permute-start.14
  78.1 3.3 %collective-permute-start.16 = (bf16[16,1152]{1,0:T(8,128)(2,1)S(1)}, bf16[16,1152]{1,0:T(8,128)(2,1)S(1)}, u32[]{:S(2)}, u32[]{:S(2)}) collective-permute-start(bf16[16,1152]{1,0:T(8,128)(2,1)S(1)} %get-tuple-element.38), channel_id=1, source_target_pairs={{0,6},{1,7},{2,4},{3,5},{4,2},{5,3},{6,0},{7,1},{8,14},{9,15},{10,... | collective-permute-start | bytes 110600 | tf_op jit(solution)/shard_map/ppermute | solution.py:312
  81.4 0.0 collective-permute-start.15
  81.5 4.2 %input_grad.3 = (bf16[11776,512]{1,0:T(8,128)(2,1)}, f32[16,1152]{1,0:T(8,128)S(1)}) custom-call(bf16[11776,512]{1,0:T(8,128)(2,1)S(1)} %get-tuple-element.22.grad_ref, bf16[512,512]{1,0:T(8,128)(2,1)S(1)} %get-tuple-element.23.w_ref, f32[16,1152]{1,0:T(8,128)S(1)} %slice_bitcast_fusion.held_ref, ...), custom_call_target="tpu_custom_call", output_to_operand_aliasing={{0}: (3, {})} | custom-call | flops 2315255808 | bytes 9043968 | tf_op jit(solution)/shard_map/input_grad/pallas_call | solution.py:103
  85.6 0.0 collective-permute-done.14
  85.6 0.7 collective-permute-done.15
  86.3 0.5 slice_bitcast_fusion.4
  86.9 0.6 fusion.6
  (10 shorter events, 0.1 us)
Async XLA Ops:
  2.2 7.0 %collective-permute-start.2 = (bf16[1,16,1152]{2,1,0:T(8,128)(2,1)S(1)}, bf16[1,16,1152]{2,1,0:T(8,128)(2,1)S(1)}, u32[]{:S(2)}, u32[]{:S(2)}) collective-permute-start(bf16[1,16,1152]{2,1,0:T(8,128)(2,1)S(1)} %fusion.2), channel_id=1, source_target_pairs={{0,6},{1,7},{2,4},{3,5},{4,2},{5,3},{6,0},{7,1},{8,14},{9,15},{10,... | collective-permute-start | bytes 110600 | tf_op jit(solution)/shard_map/ppermute | solution.py:312
  7.2 4.9 %collective-permute-start.1 = (bf16[1,16,1152]{2,1,0:T(8,128)(2,1)S(1)}, bf16[1,16,1152]{2,1,0:T(8,128)(2,1)S(1)}, u32[]{:S(2)}, u32[]{:S(2)}) collective-permute-start(bf16[1,16,1152]{2,1,0:T(8,128)(2,1)S(1)} %fusion.2), channel_id=1, source_target_pairs={{0,4},{1,5},{2,6},{3,7},{4,0},{5,1},{6,2},{7,3},{8,12},{9,13},{10,... | collective-permute-start | bytes 110600 | tf_op jit(solution)/shard_map/ppermute | solution.py:312
  7.2 4.9 %collective-permute-start = (bf16[1,16,1152]{2,1,0:T(8,128)(2,1)S(1)}, bf16[1,16,1152]{2,1,0:T(8,128)(2,1)S(1)}, u32[]{:S(2)}, u32[]{:S(2)}) collective-permute-start(bf16[1,16,1152]{2,1,0:T(8,128)(2,1)S(1)} %fusion.2), channel_id=1, source_target_pairs={{0,2},{1,3},{2,0},{3,1},{4,6},{5,7},{6,4},{7,5},{8,10},{9,11},{10,... | collective-permute-start | bytes 110600 | tf_op jit(solution)/shard_map/ppermute | solution.py:312
  12.1 7.9 %collective-permute-start.5 = (bf16[4,16,1152]{2,1,0:T(8,128)(2,1)S(1)}, bf16[4,16,1152]{2,1,0:T(8,128)(2,1)S(1)}, u32[]{:S(2)}, u32[]{:S(2)}) collective-permute-start(bf16[4,16,1152]{2,1,0:T(8,128)(2,1)S(1)} %pad_maximum_fusion.mine_ref), channel_id=1, source_target_pairs={{0,17},{1,16},{2,19},{3,18},{4,21},{5,20},{6,23},{7,22},{8,25},{9,... | collective-permute-start | bytes 442376 | tf_op jit(solution)/shard_map/ppermute | solution.py:312
  14.6 5.8 %collective-permute-start.4 = (bf16[4,16,1152]{2,1,0:T(8,128)(2,1)S(1)}, bf16[4,16,1152]{2,1,0:T(8,128)(2,1)S(1)}, u32[]{:S(2)}, u32[]{:S(2)}) collective-permute-start(bf16[4,16,1152]{2,1,0:T(8,128)(2,1)S(1)} %pad_maximum_fusion.mine_ref), channel_id=1, source_target_pairs={{0,16},{1,17},{2,18},{3,19},{4,20},{5,21},{6,22},{7,23},{8,24},{9,... | collective-permute-start | bytes 442376 | tf_op jit(solution)/shard_map/ppermute | solution.py:312
  15.2 5.4 %collective-permute-start.3 = (bf16[4,16,1152]{2,1,0:T(8,128)(2,1)S(1)}, bf16[4,16,1152]{2,1,0:T(8,128)(2,1)S(1)}, u32[]{:S(2)}, u32[]{:S(2)}) collective-permute-start(bf16[4,16,1152]{2,1,0:T(8,128)(2,1)S(1)} %pad_maximum_fusion.mine_ref), channel_id=1, source_target_pairs={{0,1},{1,0},{2,3},{3,2},{4,5},{5,4},{6,7},{7,6},{8,9},{9,8},{10,11... | collective-permute-start | bytes 442376 | tf_op jit(solution)/shard_map/ppermute | solution.py:312
  15.8 0.7 copy-start
  16.4 0.7 copy-start.1
  17.1 0.7 copy-start.2
  19.9 1.4 %collective-permute-start.6 = (bf16[4,16,1152]{2,1,0:T(8,128)(2,1)S(1)}, bf16[4,16,1152]{2,1,0:T(8,128)(2,1)S(1)}, u32[]{:S(2)}, u32[]{:S(2)}) collective-permute-start(bf16[4,16,1152]{2,1,0:T(8,128)(2,1)S(1)} %get-tuple-element.19.refs_1_), channel_id=1, source_target_pairs={{0,8},{1,9},{2,10},{3,11},{4,12},{5,13},{6,14},{7,15},{8,0},{9,1},... | collective-permute-start | bytes 442376 | tf_op jit(solution)/shard_map/ppermute | solution.py:312
  20.0 1.6 %collective-permute-start.9 = (bf16[4,16,1152]{2,1,0:T(8,128)(2,1)S(1)}, bf16[4,16,1152]{2,1,0:T(8,128)(2,1)S(1)}, u32[]{:S(2)}, u32[]{:S(2)}) collective-permute-start(bf16[4,16,1152]{2,1,0:T(8,128)(2,1)S(1)} %collective-permute-done.5.refs_4_), channel_id=1, source_target_pairs={{0,8},{1,9},{2,10},{3,11},{4,12},{5,13},{6,14},{7,15},{8,0},{9,1},... | collective-permute-start | bytes 442376 | tf_op jit(solution)/shard_map/ppermute | solution.py:312
  20.5 1.4 %collective-permute-start.8 = (bf16[4,16,1152]{2,1,0:T(8,128)(2,1)S(1)}, bf16[4,16,1152]{2,1,0:T(8,128)(2,1)S(1)}, u32[]{:S(2)}, u32[]{:S(2)}) collective-permute-start(bf16[4,16,1152]{2,1,0:T(8,128)(2,1)S(1)} %collective-permute-done.4.refs_3_), channel_id=1, source_target_pairs={{0,8},{1,9},{2,10},{3,11},{4,12},{5,13},{6,14},{7,15},{8,0},{9,1},... | collective-permute-start | bytes 442376 | tf_op jit(solution)/shard_map/ppermute | solution.py:312
  20.6 1.5 %collective-permute-start.7 = (bf16[4,16,1152]{2,1,0:T(8,128)(2,1)S(1)}, bf16[4,16,1152]{2,1,0:T(8,128)(2,1)S(1)}, u32[]{:S(2)}, u32[]{:S(2)}) collective-permute-start(bf16[4,16,1152]{2,1,0:T(8,128)(2,1)S(1)} %collective-permute-done.3.refs_2_), channel_id=1, source_target_pairs={{0,8},{1,9},{2,10},{3,11},{4,12},{5,13},{6,14},{7,15},{8,0},{9,1},... | collective-permute-start | bytes 442376 | tf_op jit(solution)/shard_map/ppermute | solution.py:312
  65.0 2.1 %collective-permute-start.10 = (bf16[16,16,1152]{2,1,0:T(8,128)(2,1)S(1)}, bf16[16,16,1152]{2,1,0:T(8,128)(2,1)S(1)}, u32[]{:S(2)}, u32[]{:S(2)}) collective-permute-start(bf16[16,16,1152]{2,1,0:T(8,128)(2,1)S(1)} %get-tuple-element.25), channel_id=1, source_target_pairs={{0,8},{1,9},{2,10},{3,11},{4,12},{5,13},{6,14},{7,15},{8,0},{9,1},... | collective-permute-start | bytes 1769480 | tf_op jit(solution)/shard_map/ppermute | solution.py:312
  67.3 9.8 %collective-permute-start.11 = (bf16[4,16,1152]{2,1,0:T(8,128)(2,1)S(1)}, bf16[4,16,1152]{2,1,0:T(8,128)(2,1)S(1)}, u32[]{:S(2)}, u32[]{:S(2)}) collective-permute-start(bf16[4,16,1152]{2,1,0:T(8,128)(2,1)S(1)} %get-tuple-element.34), channel_id=1, source_target_pairs={{0,1},{1,0},{2,3},{3,2},{4,5},{5,4},{6,7},{7,6},{8,9},{9,8},{10,11... | collective-permute-start | bytes 442376 | tf_op jit(solution)/shard_map/ppermute | solution.py:312
  68.9 8.3 %collective-permute-start.13 = (bf16[4,16,1152]{2,1,0:T(8,128)(2,1)S(1)}, bf16[4,16,1152]{2,1,0:T(8,128)(2,1)S(1)}, u32[]{:S(2)}, u32[]{:S(2)}) collective-permute-start(bf16[4,16,1152]{2,1,0:T(8,128)(2,1)S(1)} %get-tuple-element.35), channel_id=1, source_target_pairs={{0,17},{1,16},{2,19},{3,18},{4,21},{5,20},{6,23},{7,22},{8,25},{9,... | collective-permute-start | bytes 442376 | tf_op jit(solution)/shard_map/ppermute | solution.py:312
  70.3 7.5 %collective-permute-start.12 = (bf16[4,16,1152]{2,1,0:T(8,128)(2,1)S(1)}, bf16[4,16,1152]{2,1,0:T(8,128)(2,1)S(1)}, u32[]{:S(2)}, u32[]{:S(2)}) collective-permute-start(bf16[4,16,1152]{2,1,0:T(8,128)(2,1)S(1)} %get-tuple-element.36), channel_id=1, source_target_pairs={{0,16},{1,17},{2,18},{3,19},{4,20},{5,21},{6,22},{7,23},{8,24},{9,... | collective-permute-start | bytes 442376 | tf_op jit(solution)/shard_map/ppermute | solution.py:312
  77.9 7.7 %collective-permute-start.14 = (bf16[16,1152]{1,0:T(8,128)(2,1)S(1)}, bf16[16,1152]{1,0:T(8,128)(2,1)S(1)}, u32[]{:S(2)}, u32[]{:S(2)}) collective-permute-start(bf16[16,1152]{1,0:T(8,128)(2,1)S(1)} %get-tuple-element.37), channel_id=1, source_target_pairs={{0,2},{1,3},{2,0},{3,1},{4,6},{5,7},{6,4},{7,5},{8,10},{9,11},{10,... | collective-permute-start | bytes 110600 | tf_op jit(solution)/shard_map/ppermute | solution.py:312
  78.1 7.5 %collective-permute-start.16 = (bf16[16,1152]{1,0:T(8,128)(2,1)S(1)}, bf16[16,1152]{1,0:T(8,128)(2,1)S(1)}, u32[]{:S(2)}, u32[]{:S(2)}) collective-permute-start(bf16[16,1152]{1,0:T(8,128)(2,1)S(1)} %get-tuple-element.38), channel_id=1, source_target_pairs={{0,6},{1,7},{2,4},{3,5},{4,2},{5,3},{6,0},{7,1},{8,14},{9,15},{10,... | collective-permute-start | bytes 110600 | tf_op jit(solution)/shard_map/ppermute | solution.py:312
  81.4 4.9 %collective-permute-start.15 = (bf16[16,1152]{1,0:T(8,128)(2,1)S(1)}, bf16[16,1152]{1,0:T(8,128)(2,1)S(1)}, u32[]{:S(2)}, u32[]{:S(2)}) collective-permute-start(bf16[16,1152]{1,0:T(8,128)(2,1)S(1)} %get-tuple-element.39), channel_id=1, source_target_pairs={{0,4},{1,5},{2,6},{3,7},{4,0},{5,1},{6,2},{7,3},{8,12},{9,13},{10,... | collective-permute-start | bytes 110600 | tf_op jit(solution)/shard_map/ppermute | solution.py:312

commit v5 on v3

v5 whole, which is shorter than its diff:
```python
import functools
import math

import jax
import jax.numpy as jnp
from jax import lax
from jax.experimental import pallas as pl
from jax.experimental.pallas import tpu as pltpu
from jax.sharding import PartitionSpec as P

AXES = ("dp", "fsdp")
EPS = 1e-06
SLOT = 16
LANES = 128
F32 = jnp.float32
BF16 = jnp.bfloat16
VMEM_BYTES = 36 << 20
BIG_TILE = 1792
PART = 256
GRAD_VMEM = 10 << 20


def pick_tile(rows):
    for tile in (1472, 736, 512, 368, 256, 128, 64, 32, 16):
        if rows % tile == 0:
            return tile
    return rows


def dot(left, right):
    return jnp.dot(left, right, preferred_element_type=F32)


def point_weight_kernel(average, place_ref, counts_ref, points_ref, category_ref, mine_ref, out_ref, same_ref):
    same_ref[...] = mine_ref[...]
    line = lax.broadcasted_iota(jnp.int32, out_ref.shape, 0)
    position = place_ref[1] + line * LANES + lax.broadcasted_iota(jnp.int32, out_ref.shape, 1)

    def enter(shape, carry):
        start, count, points = carry
        after = position >= start
        count = jnp.where(after, counts_ref[category_ref[shape]], count)
        points = jnp.where(after, points_ref[shape], points)
        return start + points_ref[shape], count, points

    zero = jnp.zeros(out_ref.shape, jnp.int32)
    shapes = points_ref.shape[0]
    _, count, points = lax.fori_loop(
        0, shapes, enter, (jnp.int32(0), zero, zero), unroll=math.gcd(shapes, 8)
    )
    out_ref[...] = (
        count.astype(F32) * (average / 8.0) / jnp.maximum(points, average // 2).astype(F32)
    )


def point_weights(place, shape_points, shape_category, category_counts, mine, rows, average):
    lines = -(-rows // LANES // 8) * 8
    return pl.pallas_call(
        functools.partial(point_weight_kernel, average),
        in_specs=[pl.BlockSpec(memory_space=pltpu.SMEM)] * 4
        + [pl.BlockSpec(memory_space=pltpu.VMEM)],
        out_specs=[pl.BlockSpec(memory_space=pltpu.VMEM)] * 2,
        out_shape=[
            jax.ShapeDtypeStruct((lines, LANES), F32),
            jax.ShapeDtypeStruct(mine.shape, mine.dtype),
        ],
        compiler_params=pltpu.CompilerParams(vmem_limit_bytes=8 << 20),
        cost_estimate=pl.CostEstimate(
            flops=50 * rows * LANES, bytes_accessed=2 * rows * LANES, transcendentals=0
        ),
        name="point_weight",
    )(place, category_counts, shape_points, shape_category, mine)


def input_grad_kernel(grad_ref, w_ref, held_ref, *refs):
    out_ref, same_ref = refs[-2:]

    @pl.when(pl.program_id(0) == 0)
    def _():
        same_ref[...] = held_ref[...]

    out_ref[...] = dot(grad_ref[...], w_ref[...]).astype(BF16)


def input_grads(grads, weight, held, whole, tile, first, count):
    rows, width = grads.shape
    by_row = pl.BlockSpec((tile, width), lambda i: (i + first, 0))
    every = pl.BlockSpec(held.shape, lambda i: (0,) * held.ndim)
    more = [] if whole is None else [whole]
    return pl.pallas_call(
        input_grad_kernel,
        grid=(count,),
        in_specs=[by_row, pl.BlockSpec((width, width), lambda i: (0, 0)), every]
        + [pl.BlockSpec(memory_space=pl.ANY)] * len(more),
        out_specs=[by_row, every],
        out_shape=[
            jax.ShapeDtypeStruct((rows, width), BF16),
            jax.ShapeDtypeStruct(held.shape, held.dtype),
        ],
        input_output_aliases={3: 0} if more else {},
        cost_estimate=pl.CostEstimate(
            flops=2 * count * tile * width * width,
            bytes_accessed=4 * count * tile * width,
            transcendentals=0,
        ),
        compiler_params=pltpu.CompilerParams(vmem_limit_bytes=GRAD_VMEM),
        name="input_grad",
    )(grads, weight, held, *more)


def activate(half):
    lift = 1.0 + jnp.tanh(half)
    value = (half * lift).astype(BF16)
    lift = lift.astype(BF16)
    return value, lift + value * (jnp.asarray(2, BF16) - lift)


def layers_kernel(masks, *refs):
    gathered = refs[1:9]
    place_ref = refs[0]
    sources, weight_ref = refs[9:11], refs[11]
    out_hbm, grad_out, wt_a, keep_ref, send_ref = refs[12:17]
    dir_a, dir_b, w_a, w_b, wt_b, gw_a, gw_b, vec, gsum, landed, columns, arrived = refs[17:29]
    held, leaving, came, left = refs[29:31], refs[31:33], refs[33], refs[34]
    tile, width = held[0].shape[1:]
    total = sources[0].shape[0]
    first = total % tile or tile
    count = (total - first) // tile

    def fetches(start, size, place):
        return [
            pltpu.make_async_copy(
                source.at[pl.ds(start, size), :],
                ref.at[place, pl.ds(0, size), :],
                came.at[k, place],
            )
            for k, (source, ref) in enumerate(zip(sources, held))
        ]

    def leaves(start, size, place):
        return [
            pltpu.make_async_copy(
                ref.at[place, pl.ds(0, size), :],
                target.at[pl.ds(start, size), :],
                left.at[k, place],
            )
            for k, (ref, target) in enumerate(zip(leaving, (out_hbm, grad_out)))
        ]

    def start_of(index):
        return pl.multiple_of(first + (index - 1) * tile, SLOT)

    def begin(copies):
        for copy in copies:
            copy.start()

    def finish(copies):
        for copy in copies:
            copy.wait()

    begin(fetches(0, first, 0))

    def owner(slot):
        return place_ref[0] ^ masks[slot]

    copies = [
        pltpu.make_async_copy(ref, landed.at[k], arrived.at[k])
        for k, ref in enumerate(gathered)
    ]
    for copy in copies:
        copy.start()
    for copy in copies:
        copy.wait()
    for slot in range(len(masks)):
        rows = pl.ds(pl.multiple_of(owner(slot) * SLOT, SLOT), SLOT)
        block = landed[slot // 4, slot % 4]
        dir_a[rows, :] = block[:, 0:width]
        dir_b[rows, :] = block[:, width : 2 * width]
        columns[rows, :] = block[:, 2 * width :].astype(F32)
    small = columns[...].T
    for k, (direction, w, wt) in enumerate(((dir_a, w_a, wt_a), (dir_b, w_b, wt_b))):
        full = direction[...].astype(F32)
        norm = lax.rsqrt(jnp.sum(full * full, axis=0, keepdims=True) + EPS)
        scale = small[2 * k : 2 * k + 1] * norm
        weight = (scale * full).astype(BF16)
        half = weight * jnp.asarray(0.5, BF16)
        w[...] = half
        wt[...] = (weight if k == 0 else half).T
        vec[3 * k : 3 * k + 1, :] = 0.5 * small[2 * k + 1 : 2 * k + 2]
        vec[3 * k + 1 : 3 * k + 2, :] = scale
        vec[3 * k + 2 : 3 * k + 3, :] = norm
    gw_a[...] = jnp.zeros_like(gw_a)
    gw_b[...] = jnp.zeros_like(gw_b)
    gsum[...] = jnp.zeros_like(gsum)

    join = lambda pieces: jnp.concatenate(pieces, axis=0)

    def work(line, size, place):
        x_ref, cot_ref, out_ref, grad_ref = [ref.at[place] for ref in (*held, *leaving)]
        whole = pl.ds(0, size)
        spans = [pl.ds(k, min(PART, size - k)) for k in range(0, size, PART)]
        hidden, slope_a = zip(
            *[activate(dot(x_ref[s, :], w_a[...]) + vec[0:1, :]) for s in spans]
        )
        grads = []
        for s, h in zip(spans, hidden):
            value, slope_b = activate(dot(h, w_b[...]) + vec[3:4, :])
            out_ref[s, :] = value
            rows = [
                jnp.broadcast_to(weight_ref[pl.ds(line + k, 1), :], (LANES, LANES))
                for k in range(s.start // LANES, (s.start + s.size) // LANES)
            ]
            weight = join([row.T.astype(BF16) for row in rows])
            weight = jnp.concatenate([weight] * (width // LANES), axis=1)
            grads.append((cot_ref[s, :] * weight) * slope_b)
        grads_a = [dot(g, wt_b[...]).astype(BF16) * sa for g, sa in zip(grads, slope_a)]
        for s, g in zip(spans, grads_a):
            grad_ref[s, :] = g
        ones = jnp.ones((SLOT, size), BF16)
        both = dot(join([join(hidden).T, ones]), join(grads))
        gw_b[...] += both[:width]
        gsum[8:16, :] += both[width : width + 8]
        both = dot(join([x_ref[whole, :].T, ones]), grad_ref[whole, :])
        gw_a[...] += both[:width]
        gsum[0:8, :] += both[width : width + 8]

    if count:
        begin(fetches(start_of(1), tile, 1))
    finish(fetches(0, first, 0))
    work(0, first, 0)
    begin(leaves(0, first, 0))

    def turn(index, carry):
        place = lax.rem(index, 2)

        @pl.when(index < count)
        def _():
            begin(fetches(start_of(index + 1), tile, 1 - place))

        @pl.when(index == 2)
        def _():
            finish(leaves(0, first, 0))

        @pl.when(index > 2)
        def _():
            finish(leaves(start_of(index - 2), tile, place))

        finish(fetches(start_of(index), tile, place))
        work(start_of(index) // LANES, tile, place)
        begin(leaves(start_of(index), tile, place))
        return carry

    lax.fori_loop(1, count + 1, turn, 0)

    small = []
    for k, (direction, gw) in enumerate(((dir_a, gw_a), (dir_b, gw_b))):
        full = direction[...].astype(F32)
        grad = gw[...]
        scale, norm = vec[3 * k + 1 : 3 * k + 2, :], vec[3 * k + 2 : 3 * k + 3, :]
        inner = jnp.sum(grad * full, axis=0, keepdims=True)
        gw[...] = scale * grad - (scale * norm * norm * inner) * full
        small += [norm * inner, gsum[8 * k : 8 * k + 1, :]]
    gsum[0:8, :] = jnp.concatenate(small + [jnp.zeros((4, width), F32)], axis=0)
    for slot in range(len(masks)):
        home = owner(slot)
        rows = pl.ds(pl.multiple_of(home * SLOT, SLOT), SLOT)
        chunk = pl.ds(pl.multiple_of(home * SLOT // LANES * LANES, LANES), LANES)
        extra = pltpu.roll(gsum[0:8, chunk], LANES - home * SLOT % LANES, 1)
        extra = jnp.concatenate([extra, jnp.zeros((8, LANES), F32)], axis=0)
        block = jnp.concatenate([gw_a[rows, :], gw_b[rows, :], extra], axis=1)
        if slot < len(masks) // 2:
            keep_ref[slot] = block
        else:
            send_ref[slot - len(masks) // 2] = block.astype(BF16)

    if count < 2:
        finish(leaves(0, first, 0))
    for index in range(max(1, count - 1), count + 1):
        finish(leaves(start_of(index), tile, index % 2))


def layers(place, gathered, layer_input, cotangent, weights, masks):
    rows, width = layer_input.shape
    tile = min(BIG_TILE, rows)
    span = 2 * width + LANES
    half = len(masks) // 2
    square = lambda dtype: pltpu.VMEM((width, width), dtype)
    return pl.pallas_call(
        functools.partial(layers_kernel, masks),
        in_specs=[pl.BlockSpec(memory_space=pltpu.SMEM)]
        + [pl.BlockSpec(memory_space=pl.ANY)] * 8
        + [pl.BlockSpec(memory_space=pl.ANY)] * 2
        + [pl.BlockSpec(memory_space=pltpu.VMEM)],
        out_specs=[
            pl.BlockSpec(memory_space=pl.ANY),
            pl.BlockSpec(memory_space=pl.ANY),
            pl.BlockSpec(memory_space=pltpu.VMEM),
            pl.BlockSpec(memory_space=pltpu.VMEM),
            pl.BlockSpec(memory_space=pltpu.VMEM),
        ],
        out_shape=[
            jax.ShapeDtypeStruct((rows, width), BF16),
            pltpu.VMEM((rows, width), BF16),
            jax.ShapeDtypeStruct((width, width), BF16),
            jax.ShapeDtypeStruct((half, SLOT, span), F32),
            jax.ShapeDtypeStruct((half, SLOT, span), BF16),
        ],
        scratch_shapes=[square(BF16)] * 5
        + [square(F32)] * 2
        + [
            pltpu.VMEM((8, width), F32),
            pltpu.VMEM((16, width), F32),
            pltpu.VMEM((8, 4, SLOT, span), BF16),
            pltpu.VMEM((width, LANES), F32),
            pltpu.SemaphoreType.DMA((8,)),
            pltpu.VMEM((2, tile, width), BF16),
            pltpu.VMEM((2, tile, width), BF16),
            pltpu.VMEM((2, tile, width), BF16),
            pltpu.VMEM((2, tile, width), BF16),
            pltpu.SemaphoreType.DMA((2, 2)),
            pltpu.SemaphoreType.DMA((2, 2)),
        ],
        compiler_params=pltpu.CompilerParams(vmem_limit_bytes=VMEM_BYTES),
        name="layers",
    )(place, *gathered, layer_input, cotangent, weights)


def swap(value, mask, groups):
    return lax.ppermute(value, AXES, [(k, k ^ mask) for k in range(groups)])


def body(
    layer_input,
    cotangent,
    shape_points,
    shape_category,
    category_counts,
    dir_a,
    gain_a,
    bias_a,
    dir_b,
    gain_b,
    bias_b,
):
    dp, fsdp = lax.axis_size("dp"), lax.axis_size("fsdp")
    groups = dp * fsdp
    rows, width = layer_input.shape
    share = dir_a.shape[0]
    slots = width // SLOT
    average = groups * rows // shape_points.shape[0]
    me = lax.axis_index(AXES).astype(jnp.int32)
    fast = share == SLOT and groups == 32 and fsdp == 8
    small = jnp.stack([gain_a, bias_a, gain_b, bias_b])
    place = jnp.stack([me if fast else jnp.zeros_like(me), me * rows])
    weigh = lambda held: point_weights(
        place, shape_points, shape_category, category_counts, held, rows, average
    )
    if fast:
        extra = jnp.pad(small.T, ((0, 0), (0, LANES - 4)))
        mine = jnp.concatenate([dir_a, dir_b, extra], axis=1)[None]
        near = [mine] + [swap(mine, m, groups) for m in (2, 4, 6)]
        near = jnp.concatenate(near, axis=0)
        weights, same = weigh(near)
        wide = [same] + [swap(near, m, groups) for m in (1, 16, 17)]
        gathered = wide + [swap(v, 8, groups) for v in wide]
        masks = [c ^ xy ^ z for c in (0, 8) for xy in (0, 1, 16, 17) for z in (0, 2, 4, 6)]
    else:
        full = [lax.all_gather(v, AXES, axis=0, tiled=True) for v in (dir_a, dir_b)]
        vectors = lax.all_gather(small, AXES, axis=1, tiled=True)
        extra = jnp.pad(vectors.T.reshape(slots, SLOT, 4), ((0, 0), (0, 0), (0, LANES - 4)))
        blocks = [v.reshape(slots, SLOT, width) for v in full] + [extra]
        blocks = jnp.concatenate(blocks, axis=2)
        gathered = [blocks[4 * k : 4 * k + 4] for k in range(8)]
        masks = list(range(slots))
        weights, _ = weigh(dir_a)
    tile = pick_tile(rows)
    tiles = rows // tile
    first = tiles * 5 // 8
    layer_output, grads, weight, keep, send = layers(
        place, gathered, layer_input, cotangent, weights, masks
    )
    if fast:
        total = keep + swap(send, 8, groups).astype(F32)
        parts = [total[4 * k : 4 * k + 4] for k in range(4)]
        came = [swap(parts[k].astype(BF16), m, groups) for k, m in ((1, 1), (2, 16), (3, 17))]
        input_grad, held = input_grads(grads, weight, parts[0], None, tile, 0, first)
        total = held + sum(v.astype(F32) for v in came)
        came = [swap(total[k].astype(BF16), m, groups) for k, m in ((1, 2), (2, 4), (3, 6))]
        input_grad, held = input_grads(
            grads, weight, total[0], input_grad, tile, first, tiles - first
        )
        total = held + sum(v.astype(F32) for v in came)
        vectors = total[0:4, 2 * width : 2 * width + SLOT]
        grad_a, grad_b = total[:, :width], total[:, width : 2 * width]
    else:
        input_grad, _ = input_grads(grads, weight, keep[0], None, tile, 0, tiles)
        total = jnp.concatenate([keep, send.astype(F32)], axis=0)
        scatter = lambda v, d: lax.psum_scatter(v, AXES, scatter_dimension=d, tiled=True)
        square = total[:, :, : 2 * width].reshape(width, 2 * width)
        square = scatter(square, 0)
        grad_a, grad_b = square[:, :width], square[:, width:]
        vectors = total[:, 0:4, 2 * width : 2 * width + SLOT].transpose(1, 0, 2).reshape(4, width)
        vectors = scatter(vectors, 1)
    return (
        layer_output,
        input_grad,
        grad_a,
        vectors[0],
        vectors[1],
        grad_b,
        vectors[2],
        vectors[3],
    )


def solution(mesh):
    rows, row, none = P(AXES, None), P(AXES), P()
    in_specs = (rows, rows, none, none, none, rows, row, row, rows, row, row)
    out_specs = (rows, rows, rows, row, row, rows, row, row)
    return jax.shard_map(body, mesh=mesh, in_specs=in_specs, out_specs=out_specs, check_vma=False)
```

time: 90.8 us -> 85.7 us (0.944)
  Pallas kernels: 56.8 us -> 52.2 us
    pallas_call x2, Pallas kernels: 46.4 us -> 41.8 us  [the longest x1 40.8 us: layers(): pl.pallas_call(functools.partial(layers_kernel, masks), in_specs=[pl.Bloc...]
    unnamed x9 -> x6, local copies, waits for them, and re-layouts: 1.99 us -> 1.96 us
  transfers between devices with their start and end apart: 17 -> 17, of which waited for: 7 -> 8; matrix products, arithmetic and copies ran while one was open for 0% -> 0% of each run, Pallas kernels for 14% -> 13%
where the time goes in v5:
time: 85.7 us; the launch traced here: 85.4 us
  Pallas kernels  52.2 us (61%)
  starting transfers between devices  17.8 us (21%)
  waiting for transfers between devices  9.56 us (11%)
  local copies, waits for them, and re-layouts  3.29 us (4%)
  other arithmetic  1.81 us (2%)
    pallas_call x1, Pallas kernels, layers(): pl.pallas_call(functools.partial(layers_kernel, masks), in_specs=[pl.Bloc...  40.8 us
    ppermute x17, starting transfers between devices, swap(): return lax.ppermute(value, AXES, [(k, k ^ mask) for k in range(groups)])  17.8 us
    pallas_call x2, Pallas kernels, input_grads(): pl.pallas_call(input_grad_kernel, grid=(count,), in_specs=[by_row, pl.Blo...  10.4 us
    ppermute x17, waiting for transfers between devices, swap(): return lax.ppermute(value, AXES, [(k, k ^ mask) for k in range(groups)])  9.56 us
    unnamed x6, local copies, waits for them, and re-layouts  1.96 us
  transfers between devices with their start and end apart: 17, of which 8 were waited for; matrix products, arithmetic and copies ran while one was open for 0% of the time, Pallas kernels for 13%

profile of v5, /device:TPU:0, one launch (start us, length us, event | category | flops | bytes accessed | tf_op | source)
XLA Modules:
  0.0 85.4 jit_solution(463353581398939711)
XLA Ops:
  0.6 0.7 pad_maximum_fusion.1
  1.4 0.1 copy.24
  1.4 0.7 fusion.2
  2.2 5.0 %collective-permute-start.2 = (bf16[1,16,1152]{2,1,0:T(8,128)(2,1)S(1)}, bf16[1,16,1152]{2,1,0:T(8,128)(2,1)S(1)}, u32[]{:S(2)}, u32[]{:S(2)}) collective-permute-start(bf16[1,16,1152]{2,1,0:T(8,128)(2,1)S(1)} %fusion.2), channel_id=1, source_target_pairs={{0,6},{1,7},{2,4},{3,5},{4,2},{5,3},{6,0},{7,1},{8,14},{9,15},{10,... | collective-permute-start | bytes 110600 | tf_op jit(solution)/shard_map/ppermute | solution.py:329
  7.2 0.0 collective-permute-start.1
  7.2 0.6 collective-permute-start
  7.9 1.3 %collective-permute-done.2 = bf16[1,16,1152]{2,1,0:T(8,128)(2,1)S(1)} collective-permute-done((bf16[1,16,1152]{2,1,0:T(8,128)(2,1)S(1)}, bf16[1,16,1152]{2,1,0:T(8,128)(2,1)S(1)}, u32[]{:S(2)}, u32[]{:S(2)}) %collective-permute-start.2) | collective-permute-done | bytes 36896 | tf_op jit(solution)/shard_map/ppermute | solution.py:329
  9.2 2.9 %collective-permute-done.1 = bf16[1,16,1152]{2,1,0:T(8,128)(2,1)S(1)} collective-permute-done((bf16[1,16,1152]{2,1,0:T(8,128)(2,1)S(1)}, bf16[1,16,1152]{2,1,0:T(8,128)(2,1)S(1)}, u32[]{:S(2)}, u32[]{:S(2)}) %collective-permute-start.1) | collective-permute-done | bytes 36896 | tf_op jit(solution)/shard_map/ppermute | solution.py:329
  12.1 0.0 collective-permute-done
  12.1 2.5 %collective-permute-start.5 = (bf16[4,16,1152]{2,1,0:T(8,128)(2,1)S(1)}, bf16[4,16,1152]{2,1,0:T(8,128)(2,1)S(1)}, u32[]{:S(2)}, u32[]{:S(2)}) collective-permute-start(bf16[4,16,1152]{2,1,0:T(8,128)(2,1)S(1)} %pad_maximum_fusion.mine_ref), channel_id=1, source_target_pairs={{0,17},{1,16},{2,19},{3,18},{4,21},{5,20},{6,23},{7,22},{8,25},{9,... | collective-permute-start | bytes 442376 | tf_op jit(solution)/shard_map/ppermute | solution.py:329
  14.6 0.5 collective-permute-start.4
  15.2 0.5 collective-permute-start.3
  15.7 0.1 pad_add_fusion.place_ref.refs_0_
  15.8 0.7 copy-done
  16.4 0.7 copy-done.1
  17.1 0.7 copy-done.2
  17.7 1.0 %point_weight.1 = (f32[96,128]{1,0:T(8,128)S(1)}, bf16[4,16,1152]{2,1,0:T(8,128)(2,1)S(1)}) custom-call(s32[2]{0:T(128)S(1)} %pad_add_fusion.place_ref.refs_0_, s32[13]{0:T(128)S(1)} %copy-done, s32[64]{0:T(128)S(1)} %copy-done.1, s32[64]{0:T(128)S(1)} %copy-done.2, bf16[4,16,1152]{2,1,0:T(8,128)(2,1)S(1)} %pad_maximum_fusion.mine_ref), custom_call_target="tpu_custom_call" | custom-call | flops 75366400 | bytes 3014656 | tf_op jit(solution)/shard_map/point_weight/pallas_call | solution.py:58
  18.7 0.1 collective-permute-start.6
  18.8 0.0 collective-permute-done.5.refs_4_
  18.8 0.5 collective-permute-start.9
  19.3 1.2 %collective-permute-done.4.refs_3_ = bf16[4,16,1152]{2,1,0:T(8,128)(2,1)S(1)} collective-permute-done((bf16[4,16,1152]{2,1,0:T(8,128)(2,1)S(1)}, bf16[4,16,1152]{2,1,0:T(8,128)(2,1)S(1)}, u32[]{:S(2)}, u32[]{:S(2)}) %collective-permute-start.4) | collective-permute-done | bytes 147488 | tf_op jit(solution)/shard_map/ppermute | solution.py:329
  20.5 0.0 collective-permute-start.8
  20.5 0.0 collective-permute-done.3.refs_2_
  20.5 0.5 collective-permute-start.7
  21.0 0.0 collective-permute-done.6.refs_5_
  21.0 0.0 collective-permute-done.9.refs_8_
  21.0 0.9 collective-permute-done.8.refs_7_
  21.8 0.2 collective-permute-done.7.refs_6_
  22.1 40.8 %layers.1 = (bf16[11776,512]{1,0:T(8,128)(2,1)}, bf16[11776,512]{1,0:T(8,128)(2,1)S(1)}, bf16[512,512]{1,0:T(8,128)(2,1)S(1)}, f32[16,16,1152]{2,1,0:T(8,128)S(1)}, bf16[16,16,1152]{2,1,0:T(8,128)(2,1)S(1)}) custom-call(s32[2]{0:T(128)S(1)} %pad_add_fusion.place_ref.refs_0_, bf16[4,16,1152]{2,1,0:T(8,128)(2,1)S(1)} %get-tuple-element.19.refs_1_, ...), custom_call_target="tpu_custom_call" | custom-call | tf_op jit(solution)/shard_map/layers/pallas_call | solution.py:288
  62.9 0.4 collective-permute-start.10
  63.2 1.7 %collective-permute-done.10 = bf16[16,16,1152]{2,1,0:T(8,128)(2,1)S(1)} collective-permute-done((bf16[16,16,1152]{2,1,0:T(8,128)(2,1)S(1)}, bf16[16,16,1152]{2,1,0:T(8,128)(2,1)S(1)}, u32[]{:S(2)}, u32[]{:S(2)}) %collective-permute-start.10) | collective-permute-done | bytes 589856 | tf_op jit(solution)/shard_map/ppermute | solution.py:329
  64.9 0.2 fusion.4
  65.2 1.3 %collective-permute-start.11 = (bf16[4,16,1152]{2,1,0:T(8,128)(2,1)S(1)}, bf16[4,16,1152]{2,1,0:T(8,128)(2,1)S(1)}, u32[]{:S(2)}, u32[]{:S(2)}) collective-permute-start(bf16[4,16,1152]{2,1,0:T(8,128)(2,1)S(1)} %get-tuple-element.34), channel_id=1, source_target_pairs={{0,1},{1,0},{2,3},{3,2},{4,5},{5,4},{6,7},{7,6},{8,9},{9,8},{10,11... | collective-permute-start | bytes 442376 | tf_op jit(solution)/shard_map/ppermute | solution.py:329
  66.5 1.7 %collective-permute-start.13 = (bf16[4,16,1152]{2,1,0:T(8,128)(2,1)S(1)}, bf16[4,16,1152]{2,1,0:T(8,128)(2,1)S(1)}, u32[]{:S(2)}, u32[]{:S(2)}) collective-permute-start(bf16[4,16,1152]{2,1,0:T(8,128)(2,1)S(1)} %get-tuple-element.35), channel_id=1, source_target_pairs={{0,17},{1,16},{2,19},{3,18},{4,21},{5,20},{6,23},{7,22},{8,25},{9,... | collective-permute-start | bytes 442376 | tf_op jit(solution)/shard_map/ppermute | solution.py:329
  68.2 0.5 collective-permute-start.12
  68.7 6.3 %input_grad.2 = (bf16[11776,512]{1,0:T(8,128)(2,1)}, f32[4,16,1152]{2,1,0:T(8,128)S(1)}) custom-call(bf16[11776,512]{1,0:T(8,128)(2,1)S(1)} %get-tuple-element.22.grad_ref, bf16[512,512]{1,0:T(8,128)(2,1)S(1)} %get-tuple-element.23.w_ref, f32[4,16,1152]{2,1,0:T(8,128)S(1)} %slice.67.held_ref), custom_call_target="tpu_custom_call" | custom-call | flops 3858759680 | bytes 15073280 | tf_op jit(solution)/shard_map/input_grad/pallas_call | solution.py:90
  75.0 0.0 collective-permute-done.11
  75.0 0.7 collective-permute-done.12
  75.7 0.1 fusion.3
  75.8 0.3 collective-permute-start.14
  76.0 3.3 %collective-permute-start.16 = (bf16[16,1152]{1,0:T(8,128)(2,1)S(1)}, bf16[16,1152]{1,0:T(8,128)(2,1)S(1)}, u32[]{:S(2)}, u32[]{:S(2)}) collective-permute-start(bf16[16,1152]{1,0:T(8,128)(2,1)S(1)} %get-tuple-element.38), channel_id=1, source_target_pairs={{0,6},{1,7},{2,4},{3,5},{4,2},{5,3},{6,0},{7,1},{8,14},{9,15},{10,... | collective-permute-start | bytes 110600 | tf_op jit(solution)/shard_map/ppermute | solution.py:329
  79.3 0.0 collective-permute-start.15
  79.3 4.2 %input_grad.3 = (bf16[11776,512]{1,0:T(8,128)(2,1)}, f32[16,1152]{1,0:T(8,128)S(1)}) custom-call(bf16[11776,512]{1,0:T(8,128)(2,1)S(1)} %get-tuple-element.22.grad_ref, bf16[512,512]{1,0:T(8,128)(2,1)S(1)} %get-tuple-element.23.w_ref, f32[16,1152]{1,0:T(8,128)S(1)} %slice_bitcast_fusion.held_ref, ...), custom_call_target="tpu_custom_call", output_to_operand_aliasing={{0}: (3, {})} | custom-call | flops 2315255808 | bytes 9043968 | tf_op jit(solution)/shard_map/input_grad/pallas_call | solution.py:90
  83.5 0.0 collective-permute-done.14
  83.5 0.0 collective-permute-done.16
  83.5 0.7 collective-permute-done.15
  84.2 0.5 slice_bitcast_fusion.4
  84.7 0.6 fusion.6
  (10 shorter events, 0.1 us)
Async XLA Ops:
  2.2 7.0 %collective-permute-start.2 = (bf16[1,16,1152]{2,1,0:T(8,128)(2,1)S(1)}, bf16[1,16,1152]{2,1,0:T(8,128)(2,1)S(1)}, u32[]{:S(2)}, u32[]{:S(2)}) collective-permute-start(bf16[1,16,1152]{2,1,0:T(8,128)(2,1)S(1)} %fusion.2), channel_id=1, source_target_pairs={{0,6},{1,7},{2,4},{3,5},{4,2},{5,3},{6,0},{7,1},{8,14},{9,15},{10,... | collective-permute-start | bytes 110600 | tf_op jit(solution)/shard_map/ppermute | solution.py:329
  7.2 4.9 %collective-permute-start.1 = (bf16[1,16,1152]{2,1,0:T(8,128)(2,1)S(1)}, bf16[1,16,1152]{2,1,0:T(8,128)(2,1)S(1)}, u32[]{:S(2)}, u32[]{:S(2)}) collective-permute-start(bf16[1,16,1152]{2,1,0:T(8,128)(2,1)S(1)} %fusion.2), channel_id=1, source_target_pairs={{0,4},{1,5},{2,6},{3,7},{4,0},{5,1},{6,2},{7,3},{8,12},{9,13},{10,... | collective-permute-start | bytes 110600 | tf_op jit(solution)/shard_map/ppermute | solution.py:329
  7.2 4.9 %collective-permute-start = (bf16[1,16,1152]{2,1,0:T(8,128)(2,1)S(1)}, bf16[1,16,1152]{2,1,0:T(8,128)(2,1)S(1)}, u32[]{:S(2)}, u32[]{:S(2)}) collective-permute-start(bf16[1,16,1152]{2,1,0:T(8,128)(2,1)S(1)} %fusion.2), channel_id=1, source_target_pairs={{0,2},{1,3},{2,0},{3,1},{4,6},{5,7},{6,4},{7,5},{8,10},{9,11},{10,... | collective-permute-start | bytes 110600 | tf_op jit(solution)/shard_map/ppermute | solution.py:329
  12.1 6.7 %collective-permute-start.5 = (bf16[4,16,1152]{2,1,0:T(8,128)(2,1)S(1)}, bf16[4,16,1152]{2,1,0:T(8,128)(2,1)S(1)}, u32[]{:S(2)}, u32[]{:S(2)}) collective-permute-start(bf16[4,16,1152]{2,1,0:T(8,128)(2,1)S(1)} %pad_maximum_fusion.mine_ref), channel_id=1, source_target_pairs={{0,17},{1,16},{2,19},{3,18},{4,21},{5,20},{6,23},{7,22},{8,25},{9,... | collective-permute-start | bytes 442376 | tf_op jit(solution)/shard_map/ppermute | solution.py:329
  14.6 5.8 %collective-permute-start.4 = (bf16[4,16,1152]{2,1,0:T(8,128)(2,1)S(1)}, bf16[4,16,1152]{2,1,0:T(8,128)(2,1)S(1)}, u32[]{:S(2)}, u32[]{:S(2)}) collective-permute-start(bf16[4,16,1152]{2,1,0:T(8,128)(2,1)S(1)} %pad_maximum_fusion.mine_ref), channel_id=1, source_target_pairs={{0,16},{1,17},{2,18},{3,19},{4,20},{5,21},{6,22},{7,23},{8,24},{9,... | collective-permute-start | bytes 442376 | tf_op jit(solution)/shard_map/ppermute | solution.py:329
  15.2 5.3 %collective-permute-start.3 = (bf16[4,16,1152]{2,1,0:T(8,128)(2,1)S(1)}, bf16[4,16,1152]{2,1,0:T(8,128)(2,1)S(1)}, u32[]{:S(2)}, u32[]{:S(2)}) collective-permute-start(bf16[4,16,1152]{2,1,0:T(8,128)(2,1)S(1)} %pad_maximum_fusion.mine_ref), channel_id=1, source_target_pairs={{0,1},{1,0},{2,3},{3,2},{4,5},{5,4},{6,7},{7,6},{8,9},{9,8},{10,11... | collective-permute-start | bytes 442376 | tf_op jit(solution)/shard_map/ppermute | solution.py:329
  15.8 0.7 copy-start
  16.4 0.7 copy-start.1
  17.1 0.7 copy-start.2
  18.7 2.3 %collective-permute-start.6 = (bf16[4,16,1152]{2,1,0:T(8,128)(2,1)S(1)}, bf16[4,16,1152]{2,1,0:T(8,128)(2,1)S(1)}, u32[]{:S(2)}, u32[]{:S(2)}) collective-permute-start(bf16[4,16,1152]{2,1,0:T(8,128)(2,1)S(1)} %get-tuple-element.19.refs_1_), channel_id=1, source_target_pairs={{0,8},{1,9},{2,10},{3,11},{4,12},{5,13},{6,14},{7,15},{8,0},{9,1},... | collective-permute-start | bytes 442376 | tf_op jit(solution)/shard_map/ppermute | solution.py:329
  18.8 2.2 %collective-permute-start.9 = (bf16[4,16,1152]{2,1,0:T(8,128)(2,1)S(1)}, bf16[4,16,1152]{2,1,0:T(8,128)(2,1)S(1)}, u32[]{:S(2)}, u32[]{:S(2)}) collective-permute-start(bf16[4,16,1152]{2,1,0:T(8,128)(2,1)S(1)} %collective-permute-done.5.refs_4_), channel_id=1, source_target_pairs={{0,8},{1,9},{2,10},{3,11},{4,12},{5,13},{6,14},{7,15},{8,0},{9,1},... | collective-permute-start | bytes 442376 | tf_op jit(solution)/shard_map/ppermute | solution.py:329
  20.5 1.4 %collective-permute-start.8 = (bf16[4,16,1152]{2,1,0:T(8,128)(2,1)S(1)}, bf16[4,16,1152]{2,1,0:T(8,128)(2,1)S(1)}, u32[]{:S(2)}, u32[]{:S(2)}) collective-permute-start(bf16[4,16,1152]{2,1,0:T(8,128)(2,1)S(1)} %collective-permute-done.4.refs_3_), channel_id=1, source_target_pairs={{0,8},{1,9},{2,10},{3,11},{4,12},{5,13},{6,14},{7,15},{8,0},{9,1},... | collective-permute-start | bytes 442376 | tf_op jit(solution)/shard_map/ppermute | solution.py:329
  20.5 1.6 %collective-permute-start.7 = (bf16[4,16,1152]{2,1,0:T(8,128)(2,1)S(1)}, bf16[4,16,1152]{2,1,0:T(8,128)(2,1)S(1)}, u32[]{:S(2)}, u32[]{:S(2)}) collective-permute-start(bf16[4,16,1152]{2,1,0:T(8,128)(2,1)S(1)} %collective-permute-done.3.refs_2_), channel_id=1, source_target_pairs={{0,8},{1,9},{2,10},{3,11},{4,12},{5,13},{6,14},{7,15},{8,0},{9,1},... | collective-permute-start | bytes 442376 | tf_op jit(solution)/shard_map/ppermute | solution.py:329
  62.9 2.1 %collective-permute-start.10 = (bf16[16,16,1152]{2,1,0:T(8,128)(2,1)S(1)}, bf16[16,16,1152]{2,1,0:T(8,128)(2,1)S(1)}, u32[]{:S(2)}, u32[]{:S(2)}) collective-permute-start(bf16[16,16,1152]{2,1,0:T(8,128)(2,1)S(1)} %get-tuple-element.25), channel_id=1, source_target_pairs={{0,8},{1,9},{2,10},{3,11},{4,12},{5,13},{6,14},{7,15},{8,0},{9,1},... | collective-permute-start | bytes 1769480 | tf_op jit(solution)/shard_map/ppermute | solution.py:329
  65.2 9.8 %collective-permute-start.11 = (bf16[4,16,1152]{2,1,0:T(8,128)(2,1)S(1)}, bf16[4,16,1152]{2,1,0:T(8,128)(2,1)S(1)}, u32[]{:S(2)}, u32[]{:S(2)}) collective-permute-start(bf16[4,16,1152]{2,1,0:T(8,128)(2,1)S(1)} %get-tuple-element.34), channel_id=1, source_target_pairs={{0,1},{1,0},{2,3},{3,2},{4,5},{5,4},{6,7},{7,6},{8,9},{9,8},{10,11... | collective-permute-start | bytes 442376 | tf_op jit(solution)/shard_map/ppermute | solution.py:329
  66.5 8.5 %collective-permute-start.13 = (bf16[4,16,1152]{2,1,0:T(8,128)(2,1)S(1)}, bf16[4,16,1152]{2,1,0:T(8,128)(2,1)S(1)}, u32[]{:S(2)}, u32[]{:S(2)}) collective-permute-start(bf16[4,16,1152]{2,1,0:T(8,128)(2,1)S(1)} %get-tuple-element.35), channel_id=1, source_target_pairs={{0,17},{1,16},{2,19},{3,18},{4,21},{5,20},{6,23},{7,22},{8,25},{9,... | collective-permute-start | bytes 442376 | tf_op jit(solution)/shard_map/ppermute | solution.py:329
  68.2 7.5 %collective-permute-start.12 = (bf16[4,16,1152]{2,1,0:T(8,128)(2,1)S(1)}, bf16[4,16,1152]{2,1,0:T(8,128)(2,1)S(1)}, u32[]{:S(2)}, u32[]{:S(2)}) collective-permute-start(bf16[4,16,1152]{2,1,0:T(8,128)(2,1)S(1)} %get-tuple-element.36), channel_id=1, source_target_pairs={{0,16},{1,17},{2,18},{3,19},{4,20},{5,21},{6,22},{7,23},{8,24},{9,... | collective-permute-start | bytes 442376 | tf_op jit(solution)/shard_map/ppermute | solution.py:329
  75.8 7.8 %collective-permute-start.14 = (bf16[16,1152]{1,0:T(8,128)(2,1)S(1)}, bf16[16,1152]{1,0:T(8,128)(2,1)S(1)}, u32[]{:S(2)}, u32[]{:S(2)}) collective-permute-start(bf16[16,1152]{1,0:T(8,128)(2,1)S(1)} %get-tuple-element.37), channel_id=1, source_target_pairs={{0,2},{1,3},{2,0},{3,1},{4,6},{5,7},{6,4},{7,5},{8,10},{9,11},{10,... | collective-permute-start | bytes 110600 | tf_op jit(solution)/shard_map/ppermute | solution.py:329
  76.0 7.5 %collective-permute-start.16 = (bf16[16,1152]{1,0:T(8,128)(2,1)S(1)}, bf16[16,1152]{1,0:T(8,128)(2,1)S(1)}, u32[]{:S(2)}, u32[]{:S(2)}) collective-permute-start(bf16[16,1152]{1,0:T(8,128)(2,1)S(1)} %get-tuple-element.38), channel_id=1, source_target_pairs={{0,6},{1,7},{2,4},{3,5},{4,2},{5,3},{6,0},{7,1},{8,14},{9,15},{10,... | collective-permute-start | bytes 110600 | tf_op jit(solution)/shard_map/ppermute | solution.py:329
  79.3 4.9 %collective-permute-start.15 = (bf16[16,1152]{1,0:T(8,128)(2,1)S(1)}, bf16[16,1152]{1,0:T(8,128)(2,1)S(1)}, u32[]{:S(2)}, u32[]{:S(2)}) collective-permute-start(bf16[16,1152]{1,0:T(8,128)(2,1)S(1)} %get-tuple-element.39), channel_id=1, source_target_pairs={{0,4},{1,5},{2,6},{3,7},{4,0},{5,1},{6,2},{7,3},{8,12},{9,13},{10,... | collective-permute-start | bytes 110600 | tf_op jit(solution)/shard_map/ppermute | solution.py:329

commit v6 on v5

--- a/solution.py
+++ b/solution.py
@@ -108,10 +108,12 @@
     )(grads, weight, held, *more)
 
 
-def activate(half):
+def activate(half, exact):
     lift = 1.0 + jnp.tanh(half)
-    value = (half * lift).astype(BF16)
-    lift = lift.astype(BF16)
+    value = half * lift
+    if exact:
+        return value.astype(BF16), lift + value * (2.0 - lift)
+    value, lift = value.astype(BF16), lift.astype(BF16)
     return value, lift + value * (jnp.asarray(2, BF16) - lift)
 
 
@@ -200,20 +202,23 @@
         whole = pl.ds(0, size)
         spans = [pl.ds(k, min(PART, size - k)) for k in range(0, size, PART)]
         hidden, slope_a = zip(
-            *[activate(dot(x_ref[s, :], w_a[...]) + vec[0:1, :]) for s in spans]
+            *[activate(dot(x_ref[s, :], w_a[...]) + vec[0:1, :], True) for s in spans]
         )
+        slope_a = [v.astype(BF16) for v in slope_a]
         grads = []
         for s, h in zip(spans, hidden):
-            value, slope_b = activate(dot(h, w_b[...]) + vec[3:4, :])
+            value, slope_b = activate(dot(h, w_b[...]) + vec[3:4, :], True)
             out_ref[s, :] = value
             rows = [
                 jnp.broadcast_to(weight_ref[pl.ds(line + k, 1), :], (LANES, LANES))
                 for k in range(s.start // LANES, (s.start + s.size) // LANES)
             ]
-            weight = join([row.T.astype(BF16) for row in rows])
+            weight = join([row.T for row in rows])
             weight = jnp.concatenate([weight] * (width // LANES), axis=1)
-            grads.append((cot_ref[s, :] * weight) * slope_b)
-        grads_a = [dot(g, wt_b[...]).astype(BF16) * sa for g, sa in zip(grads, slope_a)]
+            grads.append(cot_ref[s, :] * (weight * slope_b).astype(BF16))
+        grads_a = [
+            (dot(g, wt_b[...]) * sa.astype(F32)).astype(BF16) for g, sa in zip(grads, slope_a)
+        ]
         for s, g in zip(spans, grads_a):
             grad_ref[s, :] = g
         ones = jnp.ones((SLOT, size), BF16)
@@ -356,8 +361,14 @@
         place, shape_points, shape_category, category_counts, held, rows, average
     )
     if fast:
-        extra = jnp.pad(small.T, ((0, 0), (0, LANES - 4)))
-        mine = jnp.concatenate([dir_a, dir_b, extra], axis=1)[None]
+        span = 2 * width + LANES
+        lane = lax.broadcasted_iota(jnp.int32, (share, span), 1)
+        mine = jnp.pad(dir_a, ((0, 0), (0, span - width)))
+        late = jnp.pad(dir_b, ((0, 0), (width, span - 2 * width)))
+        mine = jnp.where(lane < width, mine, late)
+        for k, vector in enumerate((gain_a, bias_a, gain_b, bias_b)):
+            mine = jnp.where(lane == 2 * width + k, vector[:, None], mine)
+        mine = mine[None]
         near = [mine] + [swap(mine, m, groups) for m in (2, 4, 6)]
         near = jnp.concatenate(near, axis=0)
         weights, same = weigh(near)

time: 85.7 us -> 84.7 us (0.988)
  transfers between devices with their start and end apart: 17 -> 17, of which waited for: 8 -> 8; matrix products, arithmetic and copies ran while one was open for 0% -> 0% of each run, Pallas kernels for 13% -> 14%
where the time goes in v6:
time: 84.7 us; the launch traced here: 84.5 us
  Pallas kernels  51.9 us (61%)
  starting transfers between devices  17.8 us (21%)
  waiting for transfers between devices  9.55 us (11%)
  local copies, waits for them, and re-layouts  3.19 us (4%)
  other arithmetic  1.22 us (1%)
    pallas_call x1, Pallas kernels, layers(): pl.pallas_call(functools.partial(layers_kernel, masks), in_specs=[pl.Bloc...  40.5 us
    ppermute x17, starting transfers between devices, swap(): return lax.ppermute(value, AXES, [(k, k ^ mask) for k in range(groups)])  17.8 us
    pallas_call x2, Pallas kernels, input_grads(): pl.pallas_call(input_grad_kernel, grid=(count,), in_specs=[by_row, pl.Blo...  10.4 us
    ppermute x17, waiting for transfers between devices, swap(): return lax.ppermute(value, AXES, [(k, k ^ mask) for k in range(groups)])  9.55 us
    unnamed x6, local copies, waits for them, and re-layouts  1.96 us
  transfers between devices with their start and end apart: 17, of which 8 were waited for; matrix products, arithmetic and copies ran while one was open for 0% of the time, Pallas kernels for 14%

profile of v6, /device:TPU:0, one launch (start us, length us, event | category | flops | bytes accessed | tf_op | source)
XLA Modules:
  0.0 84.5 jit_solution(17493864960453942922)
XLA Ops:
  0.7 0.8 %select_bitcast_fusion = bf16[1,16,1152]{2,1,0:T(8,128)(2,1)S(1)} fusion(bf16[16,512]{1,0:T(8,128)(2,1)} %param.19, bf16[16,512]{1,0:T(8,128)(2,1)} %param.16, pred[1152]{0:T(1024)(128)(4,1)S(1)} %get-tuple-element.46, pred[1152]{0:T(1024)(128)(4,1)S(1)} %get-tuple-element.47, pred[1152]{0:T(1024)(128)(4,1)S(1)} %get-tuple-element.48, ...), kind=kLoop, calls=%fused_computation.8 | loop fusion | flops 92160 | bytes 75520 | tf_op jit(solution)/shard_map/broadcast_in_dim | solution.py:371
  1.5 5.1 %collective-permute-start.2 = (bf16[1,16,1152]{2,1,0:T(8,128)(2,1)S(1)}, bf16[1,16,1152]{2,1,0:T(8,128)(2,1)S(1)}, u32[]{:S(2)}, u32[]{:S(2)}) collective-permute-start(bf16[1,16,1152]{2,1,0:T(8,128)(2,1)S(1)} %select_bitcast_fusion), channel_id=1, source_target_pairs={{0,6},{1,7},{2,4},{3,5},{4,2},{5,3},{6,0},{7,1},{8,14},{9,15},{10,... | collective-permute-start | bytes 110600 | tf_op jit(solution)/shard_map/ppermute | solution.py:334
  6.6 0.0 collective-permute-start.1
  6.6 0.6 collective-permute-start
  7.3 1.3 %collective-permute-done.2 = bf16[1,16,1152]{2,1,0:T(8,128)(2,1)S(1)} collective-permute-done((bf16[1,16,1152]{2,1,0:T(8,128)(2,1)S(1)}, bf16[1,16,1152]{2,1,0:T(8,128)(2,1)S(1)}, u32[]{:S(2)}, u32[]{:S(2)}) %collective-permute-start.2) | collective-permute-done | bytes 36896 | tf_op jit(solution)/shard_map/ppermute | solution.py:334
  8.6 2.9 %collective-permute-done.1 = bf16[1,16,1152]{2,1,0:T(8,128)(2,1)S(1)} collective-permute-done((bf16[1,16,1152]{2,1,0:T(8,128)(2,1)S(1)}, bf16[1,16,1152]{2,1,0:T(8,128)(2,1)S(1)}, u32[]{:S(2)}, u32[]{:S(2)}) %collective-permute-start.1) | collective-permute-done | bytes 36896 | tf_op jit(solution)/shard_map/ppermute | solution.py:334
  11.5 0.0 collective-permute-done
  11.5 2.5 %collective-permute-start.5 = (bf16[4,16,1152]{2,1,0:T(8,128)(2,1)S(1)}, bf16[4,16,1152]{2,1,0:T(8,128)(2,1)S(1)}, u32[]{:S(2)}, u32[]{:S(2)}) collective-permute-start(bf16[4,16,1152]{2,1,0:T(8,128)(2,1)S(1)} %pad_maximum_fusion.mine_ref), channel_id=1, source_target_pairs={{0,17},{1,16},{2,19},{3,18},{4,21},{5,20},{6,23},{7,22},{8,25},{9,... | collective-permute-start | bytes 442376 | tf_op jit(solution)/shard_map/ppermute | solution.py:334
  14.0 0.5 collective-permute-start.4
  14.6 0.5 collective-permute-start.3
  15.1 0.1 pad_add_fusion.place_ref.refs_0_
  15.2 0.0 copy-start
  15.2 0.7 copy-done
  15.8 0.7 copy-done.1
  16.5 0.7 copy-done.2
  17.1 1.0 %point_weight.1 = (f32[96,128]{1,0:T(8,128)S(1)}, bf16[4,16,1152]{2,1,0:T(8,128)(2,1)S(1)}) custom-call(s32[2]{0:T(128)S(1)} %pad_add_fusion.place_ref.refs_0_, s32[13]{0:T(128)S(1)} %copy-done, s32[64]{0:T(128)S(1)} %copy-done.1, s32[64]{0:T(128)S(1)} %copy-done.2, bf16[4,16,1152]{2,1,0:T(8,128)(2,1)S(1)} %pad_maximum_fusion.mine_ref), custom_call_target="tpu_custom_call" | custom-call | flops 75366400 | bytes 3014656 | tf_op jit(solution)/shard_map/point_weight/pallas_call | solution.py:58
  18.1 0.1 collective-permute-start.6
  18.2 0.0 collective-permute-done.5.refs_4_
  18.2 0.5 collective-permute-start.9
  18.7 1.2 %collective-permute-done.4.refs_3_ = bf16[4,16,1152]{2,1,0:T(8,128)(2,1)S(1)} collective-permute-done((bf16[4,16,1152]{2,1,0:T(8,128)(2,1)S(1)}, bf16[4,16,1152]{2,1,0:T(8,128)(2,1)S(1)}, u32[]{:S(2)}, u32[]{:S(2)}) %collective-permute-start.4) | collective-permute-done | bytes 147488 | tf_op jit(solution)/shard_map/ppermute | solution.py:334
  19.9 0.0 collective-permute-start.8
  19.9 0.0 collective-permute-done.3.refs_2_
  19.9 0.5 collective-permute-start.7
  20.4 0.0 collective-permute-done.6.refs_5_
  20.4 0.0 collective-permute-done.9.refs_8_
  20.4 0.9 %collective-permute-done.8.refs_7_ = bf16[4,16,1152]{2,1,0:T(8,128)(2,1)S(1)} collective-permute-done((bf16[4,16,1152]{2,1,0:T(8,128)(2,1)S(1)}, bf16[4,16,1152]{2,1,0:T(8,128)(2,1)S(1)}, u32[]{:S(2)}, u32[]{:S(2)}) %collective-permute-start.8) | collective-permute-done | bytes 147488 | tf_op jit(solution)/shard_map/ppermute | solution.py:334
  21.2 0.2 collective-permute-done.7.refs_6_
  21.5 40.5 %layers.1 = (bf16[11776,512]{1,0:T(8,128)(2,1)}, bf16[11776,512]{1,0:T(8,128)(2,1)S(1)}, bf16[512,512]{1,0:T(8,128)(2,1)S(1)}, f32[16,16,1152]{2,1,0:T(8,128)S(1)}, bf16[16,16,1152]{2,1,0:T(8,128)(2,1)S(1)}) custom-call(s32[2]{0:T(128)S(1)} %pad_add_fusion.place_ref.refs_0_, bf16[4,16,1152]{2,1,0:T(8,128)(2,1)S(1)} %get-tuple-element.19.refs_1_, ...), custom_call_target="tpu_custom_call" | custom-call | tf_op jit(solution)/shard_map/layers/pallas_call | solution.py:293
  62.0 0.4 collective-permute-start.10
  62.4 1.7 %collective-permute-done.10 = bf16[16,16,1152]{2,1,0:T(8,128)(2,1)S(1)} collective-permute-done((bf16[16,16,1152]{2,1,0:T(8,128)(2,1)S(1)}, bf16[16,16,1152]{2,1,0:T(8,128)(2,1)S(1)}, u32[]{:S(2)}, u32[]{:S(2)}) %collective-permute-start.10) | collective-permute-done | bytes 589856 | tf_op jit(solution)/shard_map/ppermute | solution.py:334
  64.1 0.2 fusion.1
  64.3 1.3 %collective-permute-start.11 = (bf16[4,16,1152]{2,1,0:T(8,128)(2,1)S(1)}, bf16[4,16,1152]{2,1,0:T(8,128)(2,1)S(1)}, u32[]{:S(2)}, u32[]{:S(2)}) collective-permute-start(bf16[4,16,1152]{2,1,0:T(8,128)(2,1)S(1)} %get-tuple-element.34), channel_id=1, source_target_pairs={{0,1},{1,0},{2,3},{3,2},{4,5},{5,4},{6,7},{7,6},{8,9},{9,8},{10,11... | collective-permute-start | bytes 442376 | tf_op jit(solution)/shard_map/ppermute | solution.py:334
  65.6 1.7 %collective-permute-start.13 = (bf16[4,16,1152]{2,1,0:T(8,128)(2,1)S(1)}, bf16[4,16,1152]{2,1,0:T(8,128)(2,1)S(1)}, u32[]{:S(2)}, u32[]{:S(2)}) collective-permute-start(bf16[4,16,1152]{2,1,0:T(8,128)(2,1)S(1)} %get-tuple-element.35), channel_id=1, source_target_pairs={{0,17},{1,16},{2,19},{3,18},{4,21},{5,20},{6,23},{7,22},{8,25},{9,... | collective-permute-start | bytes 442376 | tf_op jit(solution)/shard_map/ppermute | solution.py:334
  67.3 0.5 collective-permute-start.12
  67.8 6.3 %input_grad.2 = (bf16[11776,512]{1,0:T(8,128)(2,1)}, f32[4,16,1152]{2,1,0:T(8,128)S(1)}) custom-call(bf16[11776,512]{1,0:T(8,128)(2,1)S(1)} %get-tuple-element.22.grad_ref, bf16[512,512]{1,0:T(8,128)(2,1)S(1)} %get-tuple-element.23.w_ref, f32[4,16,1152]{2,1,0:T(8,128)S(1)} %slice.67.held_ref), custom_call_target="tpu_custom_call" | custom-call | flops 3858759680 | bytes 15073280 | tf_op jit(solution)/shard_map/input_grad/pallas_call | solution.py:90
  74.1 0.0 collective-permute-done.11
  74.1 0.0 collective-permute-done.13
  74.1 0.7 collective-permute-done.12
  74.8 0.1 fusion
  74.9 0.3 collective-permute-start.14
  75.1 3.3 %collective-permute-start.16 = (bf16[16,1152]{1,0:T(8,128)(2,1)S(1)}, bf16[16,1152]{1,0:T(8,128)(2,1)S(1)}, u32[]{:S(2)}, u32[]{:S(2)}) collective-permute-start(bf16[16,1152]{1,0:T(8,128)(2,1)S(1)} %get-tuple-element.38), channel_id=1, source_target_pairs={{0,6},{1,7},{2,4},{3,5},{4,2},{5,3},{6,0},{7,1},{8,14},{9,15},{10,... | collective-permute-start | bytes 110600 | tf_op jit(solution)/shard_map/ppermute | solution.py:334
  78.4 0.0 collective-permute-start.15
  78.4 4.2 %input_grad.3 = (bf16[11776,512]{1,0:T(8,128)(2,1)}, f32[16,1152]{1,0:T(8,128)S(1)}) custom-call(bf16[11776,512]{1,0:T(8,128)(2,1)S(1)} %get-tuple-element.22.grad_ref, bf16[512,512]{1,0:T(8,128)(2,1)S(1)} %get-tuple-element.23.w_ref, f32[16,1152]{1,0:T(8,128)S(1)} %slice_bitcast_fusion.held_ref, ...), custom_call_target="tpu_custom_call", output_to_operand_aliasing={{0}: (3, {})} | custom-call | flops 2315255808 | bytes 9043968 | tf_op jit(solution)/shard_map/input_grad/pallas_call | solution.py:90
  82.6 0.0 collective-permute-done.14
  82.6 0.0 collective-permute-done.16
  82.6 0.7 collective-permute-done.15
  83.3 0.5 slice_bitcast_fusion.4
  83.8 0.6 fusion.3
  (11 shorter events, 0.1 us)
Async XLA Ops:
  1.5 7.1 %collective-permute-start.2 = (bf16[1,16,1152]{2,1,0:T(8,128)(2,1)S(1)}, bf16[1,16,1152]{2,1,0:T(8,128)(2,1)S(1)}, u32[]{:S(2)}, u32[]{:S(2)}) collective-permute-start(bf16[1,16,1152]{2,1,0:T(8,128)(2,1)S(1)} %select_bitcast_fusion), channel_id=1, source_target_pairs={{0,6},{1,7},{2,4},{3,5},{4,2},{5,3},{6,0},{7,1},{8,14},{9,15},{10,... | collective-permute-start | bytes 110600 | tf_op jit(solution)/shard_map/ppermute | solution.py:334
  6.6 4.9 %collective-permute-start.1 = (bf16[1,16,1152]{2,1,0:T(8,128)(2,1)S(1)}, bf16[1,16,1152]{2,1,0:T(8,128)(2,1)S(1)}, u32[]{:S(2)}, u32[]{:S(2)}) collective-permute-start(bf16[1,16,1152]{2,1,0:T(8,128)(2,1)S(1)} %select_bitcast_fusion), channel_id=1, source_target_pairs={{0,4},{1,5},{2,6},{3,7},{4,0},{5,1},{6,2},{7,3},{8,12},{9,13},{10,... | collective-permute-start | bytes 110600 | tf_op jit(solution)/shard_map/ppermute | solution.py:334
  6.6 4.9 %collective-permute-start = (bf16[1,16,1152]{2,1,0:T(8,128)(2,1)S(1)}, bf16[1,16,1152]{2,1,0:T(8,128)(2,1)S(1)}, u32[]{:S(2)}, u32[]{:S(2)}) collective-permute-start(bf16[1,16,1152]{2,1,0:T(8,128)(2,1)S(1)} %select_bitcast_fusion), channel_id=1, source_target_pairs={{0,2},{1,3},{2,0},{3,1},{4,6},{5,7},{6,4},{7,5},{8,10},{9,11},{10,... | collective-permute-start | bytes 110600 | tf_op jit(solution)/shard_map/ppermute | solution.py:334
  11.5 6.7 %collective-permute-start.5 = (bf16[4,16,1152]{2,1,0:T(8,128)(2,1)S(1)}, bf16[4,16,1152]{2,1,0:T(8,128)(2,1)S(1)}, u32[]{:S(2)}, u32[]{:S(2)}) collective-permute-start(bf16[4,16,1152]{2,1,0:T(8,128)(2,1)S(1)} %pad_maximum_fusion.mine_ref), channel_id=1, source_target_pairs={{0,17},{1,16},{2,19},{3,18},{4,21},{5,20},{6,23},{7,22},{8,25},{9,... | collective-permute-start | bytes 442376 | tf_op jit(solution)/shard_map/ppermute | solution.py:334
  14.0 5.8 %collective-permute-start.4 = (bf16[4,16,1152]{2,1,0:T(8,128)(2,1)S(1)}, bf16[4,16,1152]{2,1,0:T(8,128)(2,1)S(1)}, u32[]{:S(2)}, u32[]{:S(2)}) collective-permute-start(bf16[4,16,1152]{2,1,0:T(8,128)(2,1)S(1)} %pad_maximum_fusion.mine_ref), channel_id=1, source_target_pairs={{0,16},{1,17},{2,18},{3,19},{4,20},{5,21},{6,22},{7,23},{8,24},{9,... | collective-permute-start | bytes 442376 | tf_op jit(solution)/shard_map/ppermute | solution.py:334
  14.6 5.3 %collective-permute-start.3 = (bf16[4,16,1152]{2,1,0:T(8,128)(2,1)S(1)}, bf16[4,16,1152]{2,1,0:T(8,128)(2,1)S(1)}, u32[]{:S(2)}, u32[]{:S(2)}) collective-permute-start(bf16[4,16,1152]{2,1,0:T(8,128)(2,1)S(1)} %pad_maximum_fusion.mine_ref), channel_id=1, source_target_pairs={{0,1},{1,0},{2,3},{3,2},{4,5},{5,4},{6,7},{7,6},{8,9},{9,8},{10,11... | collective-permute-start | bytes 442376 | tf_op jit(solution)/shard_map/ppermute | solution.py:334
  15.2 0.7 copy-start
  15.8 0.7 copy-start.1
  16.5 0.7 copy-start.2
  18.1 2.3 %collective-permute-start.6 = (bf16[4,16,1152]{2,1,0:T(8,128)(2,1)S(1)}, bf16[4,16,1152]{2,1,0:T(8,128)(2,1)S(1)}, u32[]{:S(2)}, u32[]{:S(2)}) collective-permute-start(bf16[4,16,1152]{2,1,0:T(8,128)(2,1)S(1)} %get-tuple-element.19.refs_1_), channel_id=1, source_target_pairs={{0,8},{1,9},{2,10},{3,11},{4,12},{5,13},{6,14},{7,15},{8,0},{9,1},... | collective-permute-start | bytes 442376 | tf_op jit(solution)/shard_map/ppermute | solution.py:334
  18.2 2.2 %collective-permute-start.9 = (bf16[4,16,1152]{2,1,0:T(8,128)(2,1)S(1)}, bf16[4,16,1152]{2,1,0:T(8,128)(2,1)S(1)}, u32[]{:S(2)}, u32[]{:S(2)}) collective-permute-start(bf16[4,16,1152]{2,1,0:T(8,128)(2,1)S(1)} %collective-permute-done.5.refs_4_), channel_id=1, source_target_pairs={{0,8},{1,9},{2,10},{3,11},{4,12},{5,13},{6,14},{7,15},{8,0},{9,1},... | collective-permute-start | bytes 442376 | tf_op jit(solution)/shard_map/ppermute | solution.py:334
  19.9 1.4 %collective-permute-start.8 = (bf16[4,16,1152]{2,1,0:T(8,128)(2,1)S(1)}, bf16[4,16,1152]{2,1,0:T(8,128)(2,1)S(1)}, u32[]{:S(2)}, u32[]{:S(2)}) collective-permute-start(bf16[4,16,1152]{2,1,0:T(8,128)(2,1)S(1)} %collective-permute-done.4.refs_3_), channel_id=1, source_target_pairs={{0,8},{1,9},{2,10},{3,11},{4,12},{5,13},{6,14},{7,15},{8,0},{9,1},... | collective-permute-start | bytes 442376 | tf_op jit(solution)/shard_map/ppermute | solution.py:334
  19.9 1.6 %collective-permute-start.7 = (bf16[4,16,1152]{2,1,0:T(8,128)(2,1)S(1)}, bf16[4,16,1152]{2,1,0:T(8,128)(2,1)S(1)}, u32[]{:S(2)}, u32[]{:S(2)}) collective-permute-start(bf16[4,16,1152]{2,1,0:T(8,128)(2,1)S(1)} %collective-permute-done.3.refs_2_), channel_id=1, source_target_pairs={{0,8},{1,9},{2,10},{3,11},{4,12},{5,13},{6,14},{7,15},{8,0},{9,1},... | collective-permute-start | bytes 442376 | tf_op jit(solution)/shard_map/ppermute | solution.py:334
  62.0 2.1 %collective-permute-start.10 = (bf16[16,16,1152]{2,1,0:T(8,128)(2,1)S(1)}, bf16[16,16,1152]{2,1,0:T(8,128)(2,1)S(1)}, u32[]{:S(2)}, u32[]{:S(2)}) collective-permute-start(bf16[16,16,1152]{2,1,0:T(8,128)(2,1)S(1)} %get-tuple-element.25), channel_id=1, source_target_pairs={{0,8},{1,9},{2,10},{3,11},{4,12},{5,13},{6,14},{7,15},{8,0},{9,1},... | collective-permute-start | bytes 1769480 | tf_op jit(solution)/shard_map/ppermute | solution.py:334
  64.3 9.8 %collective-permute-start.11 = (bf16[4,16,1152]{2,1,0:T(8,128)(2,1)S(1)}, bf16[4,16,1152]{2,1,0:T(8,128)(2,1)S(1)}, u32[]{:S(2)}, u32[]{:S(2)}) collective-permute-start(bf16[4,16,1152]{2,1,0:T(8,128)(2,1)S(1)} %get-tuple-element.34), channel_id=1, source_target_pairs={{0,1},{1,0},{2,3},{3,2},{4,5},{5,4},{6,7},{7,6},{8,9},{9,8},{10,11... | collective-permute-start | bytes 442376 | tf_op jit(solution)/shard_map/ppermute | solution.py:334
  65.6 8.5 %collective-permute-start.13 = (bf16[4,16,1152]{2,1,0:T(8,128)(2,1)S(1)}, bf16[4,16,1152]{2,1,0:T(8,128)(2,1)S(1)}, u32[]{:S(2)}, u32[]{:S(2)}) collective-permute-start(bf16[4,16,1152]{2,1,0:T(8,128)(2,1)S(1)} %get-tuple-element.35), channel_id=1, source_target_pairs={{0,17},{1,16},{2,19},{3,18},{4,21},{5,20},{6,23},{7,22},{8,25},{9,... | collective-permute-start | bytes 442376 | tf_op jit(solution)/shard_map/ppermute | solution.py:334
  67.3 7.5 %collective-permute-start.12 = (bf16[4,16,1152]{2,1,0:T(8,128)(2,1)S(1)}, bf16[4,16,1152]{2,1,0:T(8,128)(2,1)S(1)}, u32[]{:S(2)}, u32[]{:S(2)}) collective-permute-start(bf16[4,16,1152]{2,1,0:T(8,128)(2,1)S(1)} %get-tuple-element.36), channel_id=1, source_target_pairs={{0,16},{1,17},{2,18},{3,19},{4,20},{5,21},{6,22},{7,23},{8,24},{9,... | collective-permute-start | bytes 442376 | tf_op jit(solution)/shard_map/ppermute | solution.py:334
  74.9 7.8 %collective-permute-start.14 = (bf16[16,1152]{1,0:T(8,128)(2,1)S(1)}, bf16[16,1152]{1,0:T(8,128)(2,1)S(1)}, u32[]{:S(2)}, u32[]{:S(2)}) collective-permute-start(bf16[16,1152]{1,0:T(8,128)(2,1)S(1)} %get-tuple-element.37), channel_id=1, source_target_pairs={{0,2},{1,3},{2,0},{3,1},{4,6},{5,7},{6,4},{7,5},{8,10},{9,11},{10,... | collective-permute-start | bytes 110600 | tf_op jit(solution)/shard_map/ppermute | solution.py:334
  75.1 7.5 %collective-permute-start.16 = (bf16[16,1152]{1,0:T(8,128)(2,1)S(1)}, bf16[16,1152]{1,0:T(8,128)(2,1)S(1)}, u32[]{:S(2)}, u32[]{:S(2)}) collective-permute-start(bf16[16,1152]{1,0:T(8,128)(2,1)S(1)} %get-tuple-element.38), channel_id=1, source_target_pairs={{0,6},{1,7},{2,4},{3,5},{4,2},{5,3},{6,0},{7,1},{8,14},{9,15},{10,... | collective-permute-start | bytes 110600 | tf_op jit(solution)/shard_map/ppermute | solution.py:334
  78.4 4.9 %collective-permute-start.15 = (bf16[16,1152]{1,0:T(8,128)(2,1)S(1)}, bf16[16,1152]{1,0:T(8,128)(2,1)S(1)}, u32[]{:S(2)}, u32[]{:S(2)}) collective-permute-start(bf16[16,1152]{1,0:T(8,128)(2,1)S(1)} %get-tuple-element.39), channel_id=1, source_target_pairs={{0,4},{1,5},{2,6},{3,7},{4,0},{5,1},{6,2},{7,3},{8,12},{9,13},{10,... | collective-permute-start | bytes 110600 | tf_op jit(solution)/shard_map/ppermute | solution.py:334

commit v7 on v6

--- a/solution.py
+++ b/solution.py
@@ -17,6 +17,7 @@
 VMEM_BYTES = 36 << 20
 BIG_TILE = 1792
 PART = 256
+STRIP = 64
 GRAD_VMEM = 10 << 20
 
 
@@ -79,7 +80,9 @@
     def _():
         same_ref[...] = held_ref[...]
 
-    out_ref[...] = dot(grad_ref[...], w_ref[...]).astype(BF16)
+    out_ref[...] = lax.dot_general(
+        grad_ref[...], w_ref[...], (((1,), (1,)), ((), ())), preferred_element_type=F32
+    ).astype(BF16)
 
 
 def input_grads(grads, weight, held, whole, tile, first, count):
@@ -173,31 +176,32 @@
         copy.start()
     for copy in copies:
         copy.wait()
+    squares = [jnp.zeros((SLOT, width), F32)] * 2
     for slot in range(len(masks)):
         rows = pl.ds(pl.multiple_of(owner(slot) * SLOT, SLOT), SLOT)
-        block = landed[slot // 4, slot % 4]
-        dir_a[rows, :] = block[:, 0:width]
-        dir_b[rows, :] = block[:, width : 2 * width]
-        columns[rows, :] = block[:, 2 * width :].astype(F32)
+        for k, direction in enumerate((dir_a, dir_b)):
+            block = landed[slot // 4, slot % 4, :, k * width : (k + 1) * width]
+            direction[rows, :] = block
+            squares[k] = squares[k] + block.astype(F32) * block.astype(F32)
+        columns[rows, :] = landed[slot // 4, slot % 4, :, 2 * width :].astype(F32)
     small = columns[...].T
-    for k, (direction, w, wt) in enumerate(((dir_a, w_a, wt_a), (dir_b, w_b, wt_b))):
-        full = direction[...].astype(F32)
-        norm = lax.rsqrt(jnp.sum(full * full, axis=0, keepdims=True) + EPS)
+    for k, (direction, w) in enumerate(((dir_a, w_a), (dir_b, w_b))):
+        norm = lax.rsqrt(jnp.sum(squares[k], axis=0, keepdims=True) + EPS)
         scale = small[2 * k : 2 * k + 1] * norm
-        weight = (scale * full).astype(BF16)
-        half = weight * jnp.asarray(0.5, BF16)
-        w[...] = half
-        wt[...] = (weight if k == 0 else half).T
+        for row in range(0, width, STRIP):
+            strip = slice(row, row + STRIP)
+            weight = (scale * direction[strip, :].astype(F32)).astype(BF16)
+            w[strip, :] = weight * jnp.asarray(0.5, BF16)
+            if k == 0:
+                wt_a[strip, :] = weight
         vec[3 * k : 3 * k + 1, :] = 0.5 * small[2 * k + 1 : 2 * k + 2]
         vec[3 * k + 1 : 3 * k + 2, :] = scale
         vec[3 * k + 2 : 3 * k + 3, :] = norm
-    gw_a[...] = jnp.zeros_like(gw_a)
-    gw_b[...] = jnp.zeros_like(gw_b)
-    gsum[...] = jnp.zeros_like(gsum)
+    wt_b[...] = w_b[...].T
 
     join = lambda pieces: jnp.concatenate(pieces, axis=0)
 
-    def work(line, size, place):
+    def work(line, size, place, fresh):
         x_ref, cot_ref, out_ref, grad_ref = [ref.at[place] for ref in (*held, *leaving)]
         whole = pl.ds(0, size)
         spans = [pl.ds(k, min(PART, size - k)) for k in range(0, size, PART)]
@@ -222,17 +226,14 @@
         for s, g in zip(spans, grads_a):
             grad_ref[s, :] = g
         ones = jnp.ones((SLOT, size), BF16)
-        both = dot(join([join(hidden).T, ones]), join(grads))
-        gw_b[...] += both[:width]
-        gsum[8:16, :] += both[width : width + 8]
-        both = dot(join([x_ref[whole, :].T, ones]), grad_ref[whole, :])
-        gw_a[...] += both[:width]
-        gsum[0:8, :] += both[width : width + 8]
+        add = lambda ref, part: part if fresh else ref + part
+        gw_b[...] = add(gw_b[...], dot(join([join(hidden).T, ones]), join(grads)))
+        gw_a[...] = add(gw_a[...], dot(join([x_ref[whole, :].T, ones]), grad_ref[whole, :]))
 
     if count:
         begin(fetches(start_of(1), tile, 1))
     finish(fetches(0, first, 0))
-    work(0, first, 0)
+    work(0, first, 0, True)
     begin(leaves(0, first, 0))
 
     def turn(index, carry):
@@ -251,28 +252,34 @@
             finish(leaves(start_of(index - 2), tile, place))
 
         finish(fetches(start_of(index), tile, place))
-        work(start_of(index) // LANES, tile, place)
+        work(start_of(index) // LANES, tile, place, False)
         begin(leaves(start_of(index), tile, place))
         return carry
 
     lax.fori_loop(1, count + 1, turn, 0)
 
-    small = []
+    small, factors = [], []
     for k, (direction, gw) in enumerate(((dir_a, gw_a), (dir_b, gw_b))):
-        full = direction[...].astype(F32)
-        grad = gw[...]
+        inner = jnp.zeros((8, width), F32)
+        for row in range(0, width, STRIP):
+            product = gw[row : row + STRIP, :] * direction[row : row + STRIP, :].astype(F32)
+            inner = inner + jnp.sum(product.reshape(STRIP // 8, 8, width), axis=0)
+        inner = jnp.sum(inner, axis=0, keepdims=True)
         scale, norm = vec[3 * k + 1 : 3 * k + 2, :], vec[3 * k + 2 : 3 * k + 3, :]
-        inner = jnp.sum(grad * full, axis=0, keepdims=True)
-        gw[...] = scale * grad - (scale * norm * norm * inner) * full
-        small += [norm * inner, gsum[8 * k : 8 * k + 1, :]]
-    gsum[0:8, :] = jnp.concatenate(small + [jnp.zeros((4, width), F32)], axis=0)
+        small += [norm * inner, gw[width : width + 1, :]]
+        factors.append((scale, scale * norm * norm * inner))
+    gsum[...] = jnp.concatenate(small + [jnp.zeros((4, width), F32)], axis=0)
     for slot in range(len(masks)):
         home = owner(slot)
         rows = pl.ds(pl.multiple_of(home * SLOT, SLOT), SLOT)
         chunk = pl.ds(pl.multiple_of(home * SLOT // LANES * LANES, LANES), LANES)
-        extra = pltpu.roll(gsum[0:8, chunk], LANES - home * SLOT % LANES, 1)
-        extra = jnp.concatenate([extra, jnp.zeros((8, LANES), F32)], axis=0)
-        block = jnp.concatenate([gw_a[rows, :], gw_b[rows, :], extra], axis=1)
+        extra = pltpu.roll(gsum[:, chunk], LANES - home * SLOT % LANES, 1)
+        pieces = [
+            scale * gw[rows, :] - other * direction[rows, :].astype(F32)
+            for (scale, other), direction, gw in zip(factors, (dir_a, dir_b), (gw_a, gw_b))
+        ]
+        pieces.append(jnp.concatenate([extra, jnp.zeros((8, LANES), F32)], axis=0))
+        block = jnp.concatenate(pieces, axis=1)
         if slot < len(masks) // 2:
             keep_ref[slot] = block
         else:
@@ -311,10 +318,10 @@
             jax.ShapeDtypeStruct((half, SLOT, span), BF16),
         ],
         scratch_shapes=[square(BF16)] * 5
-        + [square(F32)] * 2
+        + [pltpu.VMEM((width + SLOT, width), F32)] * 2
         + [
             pltpu.VMEM((8, width), F32),
-            pltpu.VMEM((16, width), F32),
+            pltpu.VMEM((8, width), F32),
             pltpu.VMEM((8, 4, SLOT, span), BF16),
             pltpu.VMEM((width, LANES), F32),
             pltpu.SemaphoreType.DMA((8,)),

time: 84.7 us -> 84 us (level)
  no operation moved by 1% of the time
where the time goes in v7:
time: 84 us; the launch traced here: 83.8 us
  Pallas kernels  51.4 us (61%)
  starting transfers between devices  17.8 us (21%)
  waiting for transfers between devices  9.34 us (11%)
  local copies, waits for them, and re-layouts  3.19 us (4%)
  other arithmetic  1.22 us (1%)
    pallas_call x1, Pallas kernels, layers(): pl.pallas_call(functools.partial(layers_kernel, masks), in_specs=[pl.Bloc...  39.8 us
    ppermute x17, starting transfers between devices, swap(): return lax.ppermute(value, AXES, [(k, k ^ mask) for k in range(groups)])  17.8 us
    pallas_call x2, Pallas kernels, input_grads(): pl.pallas_call(input_grad_kernel, grid=(count,), in_specs=[by_row, pl.Blo...  10.6 us
    ppermute x17, waiting for transfers between devices, swap(): return lax.ppermute(value, AXES, [(k, k ^ mask) for k in range(groups)])  9.34 us
    unnamed x6, local copies, waits for them, and re-layouts  1.96 us
  transfers between devices with their start and end apart: 17, of which 8 were waited for; matrix products, arithmetic and copies ran while one was open for 0% of the time, Pallas kernels for 14%

profile of v7, /device:TPU:0, one launch (start us, length us, event | category | flops | bytes accessed | tf_op | source)
XLA Modules:
  0.0 83.8 jit_solution(14174978262701059559)
XLA Ops:
  0.7 0.8 %select_bitcast_fusion = bf16[1,16,1152]{2,1,0:T(8,128)(2,1)S(1)} fusion(bf16[16,512]{1,0:T(8,128)(2,1)} %param.19, bf16[16,512]{1,0:T(8,128)(2,1)} %param.16, pred[1152]{0:T(1024)(128)(4,1)S(1)} %get-tuple-element.46, pred[1152]{0:T(1024)(128)(4,1)S(1)} %get-tuple-element.47, pred[1152]{0:T(1024)(128)(4,1)S(1)} %get-tuple-element.48, ...), kind=kLoop, calls=%fused_computation.8 | loop fusion | flops 92160 | bytes 75520 | tf_op jit(solution)/shard_map/broadcast_in_dim | solution.py:378
  1.5 5.1 %collective-permute-start.2 = (bf16[1,16,1152]{2,1,0:T(8,128)(2,1)S(1)}, bf16[1,16,1152]{2,1,0:T(8,128)(2,1)S(1)}, u32[]{:S(2)}, u32[]{:S(2)}) collective-permute-start(bf16[1,16,1152]{2,1,0:T(8,128)(2,1)S(1)} %select_bitcast_fusion), channel_id=1, source_target_pairs={{0,6},{1,7},{2,4},{3,5},{4,2},{5,3},{6,0},{7,1},{8,14},{9,15},{10,... | collective-permute-start | bytes 110600 | tf_op jit(solution)/shard_map/ppermute | solution.py:341
  6.6 0.0 collective-permute-start.1
  6.6 0.6 collective-permute-start
  7.3 1.3 %collective-permute-done.2 = bf16[1,16,1152]{2,1,0:T(8,128)(2,1)S(1)} collective-permute-done((bf16[1,16,1152]{2,1,0:T(8,128)(2,1)S(1)}, bf16[1,16,1152]{2,1,0:T(8,128)(2,1)S(1)}, u32[]{:S(2)}, u32[]{:S(2)}) %collective-permute-start.2) | collective-permute-done | bytes 36896 | tf_op jit(solution)/shard_map/ppermute | solution.py:341
  8.6 2.9 %collective-permute-done.1 = bf16[1,16,1152]{2,1,0:T(8,128)(2,1)S(1)} collective-permute-done((bf16[1,16,1152]{2,1,0:T(8,128)(2,1)S(1)}, bf16[1,16,1152]{2,1,0:T(8,128)(2,1)S(1)}, u32[]{:S(2)}, u32[]{:S(2)}) %collective-permute-start.1) | collective-permute-done | bytes 36896 | tf_op jit(solution)/shard_map/ppermute | solution.py:341
  11.5 0.0 collective-permute-done
  11.5 2.5 %collective-permute-start.5 = (bf16[4,16,1152]{2,1,0:T(8,128)(2,1)S(1)}, bf16[4,16,1152]{2,1,0:T(8,128)(2,1)S(1)}, u32[]{:S(2)}, u32[]{:S(2)}) collective-permute-start(bf16[4,16,1152]{2,1,0:T(8,128)(2,1)S(1)} %pad_maximum_fusion.mine_ref), channel_id=1, source_target_pairs={{0,17},{1,16},{2,19},{3,18},{4,21},{5,20},{6,23},{7,22},{8,25},{9,... | collective-permute-start | bytes 442376 | tf_op jit(solution)/shard_map/ppermute | solution.py:341
  14.0 0.5 collective-permute-start.4
  14.6 0.5 collective-permute-start.3
  15.1 0.1 pad_add_fusion.place_ref.refs_0_
  15.2 0.0 copy-start
  15.2 0.7 copy-done
  15.8 0.7 copy-done.1
  16.5 0.7 copy-done.2
  17.1 1.0 %point_weight.1 = (f32[96,128]{1,0:T(8,128)S(1)}, bf16[4,16,1152]{2,1,0:T(8,128)(2,1)S(1)}) custom-call(s32[2]{0:T(128)S(1)} %pad_add_fusion.place_ref.refs_0_, s32[13]{0:T(128)S(1)} %copy-done, s32[64]{0:T(128)S(1)} %copy-done.1, s32[64]{0:T(128)S(1)} %copy-done.2, bf16[4,16,1152]{2,1,0:T(8,128)(2,1)S(1)} %pad_maximum_fusion.mine_ref), custom_call_target="tpu_custom_call" | custom-call | flops 75366400 | bytes 3014656 | tf_op jit(solution)/shard_map/point_weight/pallas_call | solution.py:59
  18.1 0.1 collective-permute-start.6
  18.2 0.0 collective-permute-done.5.refs_4_
  18.2 0.5 collective-permute-start.9
  18.7 1.2 %collective-permute-done.4.refs_3_ = bf16[4,16,1152]{2,1,0:T(8,128)(2,1)S(1)} collective-permute-done((bf16[4,16,1152]{2,1,0:T(8,128)(2,1)S(1)}, bf16[4,16,1152]{2,1,0:T(8,128)(2,1)S(1)}, u32[]{:S(2)}, u32[]{:S(2)}) %collective-permute-start.4) | collective-permute-done | bytes 147488 | tf_op jit(solution)/shard_map/ppermute | solution.py:341
  19.9 0.0 collective-permute-start.8
  19.9 0.0 collective-permute-done.3.refs_2_
  19.9 0.5 collective-permute-start.7
  20.4 0.0 collective-permute-done.6.refs_5_
  20.4 0.0 collective-permute-done.9.refs_8_
  20.4 0.9 %collective-permute-done.8.refs_7_ = bf16[4,16,1152]{2,1,0:T(8,128)(2,1)S(1)} collective-permute-done((bf16[4,16,1152]{2,1,0:T(8,128)(2,1)S(1)}, bf16[4,16,1152]{2,1,0:T(8,128)(2,1)S(1)}, u32[]{:S(2)}, u32[]{:S(2)}) %collective-permute-start.8) | collective-permute-done | bytes 147488 | tf_op jit(solution)/shard_map/ppermute | solution.py:341
  21.2 0.2 collective-permute-done.7.refs_6_
  21.5 39.8 %layers.1 = (bf16[11776,512]{1,0:T(8,128)(2,1)}, bf16[11776,512]{1,0:T(8,128)(2,1)S(1)}, bf16[512,512]{1,0:T(8,128)(2,1)S(1)}, f32[16,16,1152]{2,1,0:T(8,128)S(1)}, bf16[16,16,1152]{2,1,0:T(8,128)(2,1)S(1)}) custom-call(s32[2]{0:T(128)S(1)} %pad_add_fusion.place_ref.refs_0_, bf16[4,16,1152]{2,1,0:T(8,128)(2,1)S(1)} %get-tuple-element.19.refs_1_, ...), custom_call_target="tpu_custom_call" | custom-call | tf_op jit(solution)/shard_map/layers/pallas_call | solution.py:300
  61.3 0.4 collective-permute-start.10
  61.6 1.7 %collective-permute-done.10 = bf16[16,16,1152]{2,1,0:T(8,128)(2,1)S(1)} collective-permute-done((bf16[16,16,1152]{2,1,0:T(8,128)(2,1)S(1)}, bf16[16,16,1152]{2,1,0:T(8,128)(2,1)S(1)}, u32[]{:S(2)}, u32[]{:S(2)}) %collective-permute-start.10) | collective-permute-done | bytes 589856 | tf_op jit(solution)/shard_map/ppermute | solution.py:341
  63.3 0.2 fusion.1
  63.5 1.3 %collective-permute-start.11 = (bf16[4,16,1152]{2,1,0:T(8,128)(2,1)S(1)}, bf16[4,16,1152]{2,1,0:T(8,128)(2,1)S(1)}, u32[]{:S(2)}, u32[]{:S(2)}) collective-permute-start(bf16[4,16,1152]{2,1,0:T(8,128)(2,1)S(1)} %get-tuple-element.34), channel_id=1, source_target_pairs={{0,1},{1,0},{2,3},{3,2},{4,5},{5,4},{6,7},{7,6},{8,9},{9,8},{10,11... | collective-permute-start | bytes 442376 | tf_op jit(solution)/shard_map/ppermute | solution.py:341
  64.9 1.7 %collective-permute-start.13 = (bf16[4,16,1152]{2,1,0:T(8,128)(2,1)S(1)}, bf16[4,16,1152]{2,1,0:T(8,128)(2,1)S(1)}, u32[]{:S(2)}, u32[]{:S(2)}) collective-permute-start(bf16[4,16,1152]{2,1,0:T(8,128)(2,1)S(1)} %get-tuple-element.35), channel_id=1, source_target_pairs={{0,17},{1,16},{2,19},{3,18},{4,21},{5,20},{6,23},{7,22},{8,25},{9,... | collective-permute-start | bytes 442376 | tf_op jit(solution)/shard_map/ppermute | solution.py:341
  66.6 0.5 collective-permute-start.12
  67.1 6.4 %input_grad.2 = (bf16[11776,512]{1,0:T(8,128)(2,1)}, f32[4,16,1152]{2,1,0:T(8,128)S(1)}) custom-call(bf16[11776,512]{1,0:T(8,128)(2,1)S(1)} %get-tuple-element.22.grad_ref, bf16[512,512]{1,0:T(8,128)(2,1)S(1)} %get-tuple-element.23.w_ref, f32[4,16,1152]{2,1,0:T(8,128)S(1)} %slice.67.held_ref), custom_call_target="tpu_custom_call" | custom-call | flops 3858759680 | bytes 15073280 | tf_op jit(solution)/shard_map/input_grad/pallas_call | solution.py:93
  73.5 0.0 collective-permute-done.11
  73.5 0.0 collective-permute-done.13
  73.5 0.6 collective-permute-done.12
  74.1 0.1 fusion
  74.2 0.3 collective-permute-start.14
  74.4 3.3 %collective-permute-start.16 = (bf16[16,1152]{1,0:T(8,128)(2,1)S(1)}, bf16[16,1152]{1,0:T(8,128)(2,1)S(1)}, u32[]{:S(2)}, u32[]{:S(2)}) collective-permute-start(bf16[16,1152]{1,0:T(8,128)(2,1)S(1)} %get-tuple-element.38), channel_id=1, source_target_pairs={{0,6},{1,7},{2,4},{3,5},{4,2},{5,3},{6,0},{7,1},{8,14},{9,15},{10,... | collective-permute-start | bytes 110600 | tf_op jit(solution)/shard_map/ppermute | solution.py:341
  77.7 0.0 collective-permute-start.15
  77.7 4.3 %input_grad.3 = (bf16[11776,512]{1,0:T(8,128)(2,1)}, f32[16,1152]{1,0:T(8,128)S(1)}) custom-call(bf16[11776,512]{1,0:T(8,128)(2,1)S(1)} %get-tuple-element.22.grad_ref, bf16[512,512]{1,0:T(8,128)(2,1)S(1)} %get-tuple-element.23.w_ref, f32[16,1152]{1,0:T(8,128)S(1)} %slice_bitcast_fusion.held_ref, ...), custom_call_target="tpu_custom_call", output_to_operand_aliasing={{0}: (3, {})} | custom-call | flops 2315255808 | bytes 9043968 | tf_op jit(solution)/shard_map/input_grad/pallas_call | solution.py:93
  82.0 0.0 collective-permute-done.14
  82.0 0.0 collective-permute-done.16
  82.0 0.6 collective-permute-done.15
  82.6 0.5 slice_bitcast_fusion.4
  83.1 0.6 fusion.3
  (11 shorter events, 0.1 us)
Async XLA Ops:
  1.5 7.1 %collective-permute-start.2 = (bf16[1,16,1152]{2,1,0:T(8,128)(2,1)S(1)}, bf16[1,16,1152]{2,1,0:T(8,128)(2,1)S(1)}, u32[]{:S(2)}, u32[]{:S(2)}) collective-permute-start(bf16[1,16,1152]{2,1,0:T(8,128)(2,1)S(1)} %select_bitcast_fusion), channel_id=1, source_target_pairs={{0,6},{1,7},{2,4},{3,5},{4,2},{5,3},{6,0},{7,1},{8,14},{9,15},{10,... | collective-permute-start | bytes 110600 | tf_op jit(solution)/shard_map/ppermute | solution.py:341
  6.6 4.9 %collective-permute-start.1 = (bf16[1,16,1152]{2,1,0:T(8,128)(2,1)S(1)}, bf16[1,16,1152]{2,1,0:T(8,128)(2,1)S(1)}, u32[]{:S(2)}, u32[]{:S(2)}) collective-permute-start(bf16[1,16,1152]{2,1,0:T(8,128)(2,1)S(1)} %select_bitcast_fusion), channel_id=1, source_target_pairs={{0,4},{1,5},{2,6},{3,7},{4,0},{5,1},{6,2},{7,3},{8,12},{9,13},{10,... | collective-permute-start | bytes 110600 | tf_op jit(solution)/shard_map/ppermute | solution.py:341
  6.6 4.9 %collective-permute-start = (bf16[1,16,1152]{2,1,0:T(8,128)(2,1)S(1)}, bf16[1,16,1152]{2,1,0:T(8,128)(2,1)S(1)}, u32[]{:S(2)}, u32[]{:S(2)}) collective-permute-start(bf16[1,16,1152]{2,1,0:T(8,128)(2,1)S(1)} %select_bitcast_fusion), channel_id=1, source_target_pairs={{0,2},{1,3},{2,0},{3,1},{4,6},{5,7},{6,4},{7,5},{8,10},{9,11},{10,... | collective-permute-start | bytes 110600 | tf_op jit(solution)/shard_map/ppermute | solution.py:341
  11.5 6.7 %collective-permute-start.5 = (bf16[4,16,1152]{2,1,0:T(8,128)(2,1)S(1)}, bf16[4,16,1152]{2,1,0:T(8,128)(2,1)S(1)}, u32[]{:S(2)}, u32[]{:S(2)}) collective-permute-start(bf16[4,16,1152]{2,1,0:T(8,128)(2,1)S(1)} %pad_maximum_fusion.mine_ref), channel_id=1, source_target_pairs={{0,17},{1,16},{2,19},{3,18},{4,21},{5,20},{6,23},{7,22},{8,25},{9,... | collective-permute-start | bytes 442376 | tf_op jit(solution)/shard_map/ppermute | solution.py:341
  14.0 5.8 %collective-permute-start.4 = (bf16[4,16,1152]{2,1,0:T(8,128)(2,1)S(1)}, bf16[4,16,1152]{2,1,0:T(8,128)(2,1)S(1)}, u32[]{:S(2)}, u32[]{:S(2)}) collective-permute-start(bf16[4,16,1152]{2,1,0:T(8,128)(2,1)S(1)} %pad_maximum_fusion.mine_ref), channel_id=1, source_target_pairs={{0,16},{1,17},{2,18},{3,19},{4,20},{5,21},{6,22},{7,23},{8,24},{9,... | collective-permute-start | bytes 442376 | tf_op jit(solution)/shard_map/ppermute | solution.py:341
  14.6 5.3 %collective-permute-start.3 = (bf16[4,16,1152]{2,1,0:T(8,128)(2,1)S(1)}, bf16[4,16,1152]{2,1,0:T(8,128)(2,1)S(1)}, u32[]{:S(2)}, u32[]{:S(2)}) collective-permute-start(bf16[4,16,1152]{2,1,0:T(8,128)(2,1)S(1)} %pad_maximum_fusion.mine_ref), channel_id=1, source_target_pairs={{0,1},{1,0},{2,3},{3,2},{4,5},{5,4},{6,7},{7,6},{8,9},{9,8},{10,11... | collective-permute-start | bytes 442376 | tf_op jit(solution)/shard_map/ppermute | solution.py:341
  15.2 0.7 copy-start
  15.8 0.7 copy-start.1
  16.5 0.7 copy-start.2
  18.1 2.3 %collective-permute-start.6 = (bf16[4,16,1152]{2,1,0:T(8,128)(2,1)S(1)}, bf16[4,16,1152]{2,1,0:T(8,128)(2,1)S(1)}, u32[]{:S(2)}, u32[]{:S(2)}) collective-permute-start(bf16[4,16,1152]{2,1,0:T(8,128)(2,1)S(1)} %get-tuple-element.19.refs_1_), channel_id=1, source_target_pairs={{0,8},{1,9},{2,10},{3,11},{4,12},{5,13},{6,14},{7,15},{8,0},{9,1},... | collective-permute-start | bytes 442376 | tf_op jit(solution)/shard_map/ppermute | solution.py:341
  18.2 2.2 %collective-permute-start.9 = (bf16[4,16,1152]{2,1,0:T(8,128)(2,1)S(1)}, bf16[4,16,1152]{2,1,0:T(8,128)(2,1)S(1)}, u32[]{:S(2)}, u32[]{:S(2)}) collective-permute-start(bf16[4,16,1152]{2,1,0:T(8,128)(2,1)S(1)} %collective-permute-done.5.refs_4_), channel_id=1, source_target_pairs={{0,8},{1,9},{2,10},{3,11},{4,12},{5,13},{6,14},{7,15},{8,0},{9,1},... | collective-permute-start | bytes 442376 | tf_op jit(solution)/shard_map/ppermute | solution.py:341
  19.9 1.4 %collective-permute-start.8 = (bf16[4,16,1152]{2,1,0:T(8,128)(2,1)S(1)}, bf16[4,16,1152]{2,1,0:T(8,128)(2,1)S(1)}, u32[]{:S(2)}, u32[]{:S(2)}) collective-permute-start(bf16[4,16,1152]{2,1,0:T(8,128)(2,1)S(1)} %collective-permute-done.4.refs_3_), channel_id=1, source_target_pairs={{0,8},{1,9},{2,10},{3,11},{4,12},{5,13},{6,14},{7,15},{8,0},{9,1},... | collective-permute-start | bytes 442376 | tf_op jit(solution)/shard_map/ppermute | solution.py:341
  19.9 1.6 %collective-permute-start.7 = (bf16[4,16,1152]{2,1,0:T(8,128)(2,1)S(1)}, bf16[4,16,1152]{2,1,0:T(8,128)(2,1)S(1)}, u32[]{:S(2)}, u32[]{:S(2)}) collective-permute-start(bf16[4,16,1152]{2,1,0:T(8,128)(2,1)S(1)} %collective-permute-done.3.refs_2_), channel_id=1, source_target_pairs={{0,8},{1,9},{2,10},{3,11},{4,12},{5,13},{6,14},{7,15},{8,0},{9,1},... | collective-permute-start | bytes 442376 | tf_op jit(solution)/shard_map/ppermute | solution.py:341
  61.3 2.1 %collective-permute-start.10 = (bf16[16,16,1152]{2,1,0:T(8,128)(2,1)S(1)}, bf16[16,16,1152]{2,1,0:T(8,128)(2,1)S(1)}, u32[]{:S(2)}, u32[]{:S(2)}) collective-permute-start(bf16[16,16,1152]{2,1,0:T(8,128)(2,1)S(1)} %get-tuple-element.25), channel_id=1, source_target_pairs={{0,8},{1,9},{2,10},{3,11},{4,12},{5,13},{6,14},{7,15},{8,0},{9,1},... | collective-permute-start | bytes 1769480 | tf_op jit(solution)/shard_map/ppermute | solution.py:341
  63.5 10.0 %collective-permute-start.11 = (bf16[4,16,1152]{2,1,0:T(8,128)(2,1)S(1)}, bf16[4,16,1152]{2,1,0:T(8,128)(2,1)S(1)}, u32[]{:S(2)}, u32[]{:S(2)}) collective-permute-start(bf16[4,16,1152]{2,1,0:T(8,128)(2,1)S(1)} %get-tuple-element.34), channel_id=1, source_target_pairs={{0,1},{1,0},{2,3},{3,2},{4,5},{5,4},{6,7},{7,6},{8,9},{9,8},{10,11... | collective-permute-start | bytes 442376 | tf_op jit(solution)/shard_map/ppermute | solution.py:341
  64.9 8.6 %collective-permute-start.13 = (bf16[4,16,1152]{2,1,0:T(8,128)(2,1)S(1)}, bf16[4,16,1152]{2,1,0:T(8,128)(2,1)S(1)}, u32[]{:S(2)}, u32[]{:S(2)}) collective-permute-start(bf16[4,16,1152]{2,1,0:T(8,128)(2,1)S(1)} %get-tuple-element.35), channel_id=1, source_target_pairs={{0,17},{1,16},{2,19},{3,18},{4,21},{5,20},{6,23},{7,22},{8,25},{9,... | collective-permute-start | bytes 442376 | tf_op jit(solution)/shard_map/ppermute | solution.py:341
  66.6 7.5 %collective-permute-start.12 = (bf16[4,16,1152]{2,1,0:T(8,128)(2,1)S(1)}, bf16[4,16,1152]{2,1,0:T(8,128)(2,1)S(1)}, u32[]{:S(2)}, u32[]{:S(2)}) collective-permute-start(bf16[4,16,1152]{2,1,0:T(8,128)(2,1)S(1)} %get-tuple-element.36), channel_id=1, source_target_pairs={{0,16},{1,17},{2,18},{3,19},{4,20},{5,21},{6,22},{7,23},{8,24},{9,... | collective-permute-start | bytes 442376 | tf_op jit(solution)/shard_map/ppermute | solution.py:341
  74.2 7.8 %collective-permute-start.14 = (bf16[16,1152]{1,0:T(8,128)(2,1)S(1)}, bf16[16,1152]{1,0:T(8,128)(2,1)S(1)}, u32[]{:S(2)}, u32[]{:S(2)}) collective-permute-start(bf16[16,1152]{1,0:T(8,128)(2,1)S(1)} %get-tuple-element.37), channel_id=1, source_target_pairs={{0,2},{1,3},{2,0},{3,1},{4,6},{5,7},{6,4},{7,5},{8,10},{9,11},{10,... | collective-permute-start | bytes 110600 | tf_op jit(solution)/shard_map/ppermute | solution.py:341
  74.4 7.6 %collective-permute-start.16 = (bf16[16,1152]{1,0:T(8,128)(2,1)S(1)}, bf16[16,1152]{1,0:T(8,128)(2,1)S(1)}, u32[]{:S(2)}, u32[]{:S(2)}) collective-permute-start(bf16[16,1152]{1,0:T(8,128)(2,1)S(1)} %get-tuple-element.38), channel_id=1, source_target_pairs={{0,6},{1,7},{2,4},{3,5},{4,2},{5,3},{6,0},{7,1},{8,14},{9,15},{10,... | collective-permute-start | bytes 110600 | tf_op jit(solution)/shard_map/ppermute | solution.py:341
  77.7 4.9 %collective-permute-start.15 = (bf16[16,1152]{1,0:T(8,128)(2,1)S(1)}, bf16[16,1152]{1,0:T(8,128)(2,1)S(1)}, u32[]{:S(2)}, u32[]{:S(2)}) collective-permute-start(bf16[16,1152]{1,0:T(8,128)(2,1)S(1)} %get-tuple-element.39), channel_id=1, source_target_pairs={{0,4},{1,5},{2,6},{3,7},{4,0},{5,1},{6,2},{7,3},{8,12},{9,13},{10,... | collective-permute-start | bytes 110600 | tf_op jit(solution)/shard_map/ppermute | solution.py:341

commit v8 on v7

--- a/solution.py
+++ b/solution.py
@@ -335,6 +335,30 @@
         compiler_params=pltpu.CompilerParams(vmem_limit_bytes=VMEM_BYTES),
         name="layers",
     )(place, *gathered, layer_input, cotangent, weights)
+
+
+def last_kernel(*refs):
+    total = refs[0][...]
+    for ref in refs[1:4]:
+        total = total + ref[...].astype(F32)
+    width = refs[4].shape[1]
+    refs[4][...] = total[:, 0:width]
+    refs[5][...] = total[:, width : 2 * width]
+    for k, ref in enumerate(refs[6:]):
+        ref[...] = total[k, 2 * width : 2 * width + SLOT]
+
+
+def add_last(held, came, width):
+    square = jax.ShapeDtypeStruct((SLOT, width), F32)
+    vector = jax.ShapeDtypeStruct((SLOT,), F32)
+    return pl.pallas_call(
+        last_kernel,
+        in_specs=[pl.BlockSpec(memory_space=pltpu.VMEM)] * 4,
+        out_specs=[pl.BlockSpec(memory_space=pltpu.VMEM)] * 6,
+        out_shape=[square, square] + [vector] * 4,
+        compiler_params=pltpu.CompilerParams(vmem_limit_bytes=4 << 20),
+        name="last",
+    )(held, *came)
 
 
 def swap(value, mask, groups):
@@ -407,9 +431,7 @@
         input_grad, held = input_grads(
             grads, weight, total[0], input_grad, tile, first, tiles - first
         )
-        total = held + sum(v.astype(F32) for v in came)
-        vectors = total[0:4, 2 * width : 2 * width + SLOT]
-        grad_a, grad_b = total[:, :width], total[:, width : 2 * width]
+        grad_a, grad_b, *vectors = add_last(held, came, width)
     else:
         input_grad, _ = input_grads(grads, weight, keep[0], None, tile, 0, tiles)
         total = jnp.concatenate([keep, send.astype(F32)], axis=0)

time: 84 us -> 83.7 us (level)
  local copies, waits for them, and re-layouts: 3.19 us -> 2.04 us
  starting transfers between devices: 17.8 us -> 18.7 us
    ppermute x17, starting transfers between devices: 17.8 us -> 18.7 us  [swap(): return lax.ppermute(value, AXES, [(k, k ^ mask) for k in range(groups)])]
  transfers between devices with their start and end apart: 17 -> 17, of which waited for: 8 -> 7; matrix products, arithmetic and copies ran while one was open for 0% -> 0% of each run, Pallas kernels for 14% -> 14%
where the time goes in v8:
time: 83.7 us; the launch traced here: 83.5 us
  Pallas kernels  52.1 us (62%)
  starting transfers between devices  18.7 us (22%)
  waiting for transfers between devices  8.76 us (10%)
  local copies, waits for them, and re-layouts  2.04 us (2%)
  other arithmetic  1.2 us (1%)
    pallas_call x1, Pallas kernels, layers(): pl.pallas_call(functools.partial(layers_kernel, masks), in_specs=[pl.Bloc...  39.8 us
    ppermute x17, starting transfers between devices, swap(): return lax.ppermute(value, AXES, [(k, k ^ mask) for k in range(groups)])  18.7 us
    pallas_call x2, Pallas kernels, input_grads(): pl.pallas_call(input_grad_kernel, grid=(count,), in_specs=[by_row, pl.Blo...  10.6 us
    ppermute x17, waiting for transfers between devices, swap(): return lax.ppermute(value, AXES, [(k, k ^ mask) for k in range(groups)])  8.76 us
    unnamed x6, local copies, waits for them, and re-layouts  1.96 us
  transfers between devices with their start and end apart: 17, of which 7 were waited for; matrix products, arithmetic and copies ran while one was open for 0% of the time, Pallas kernels for 14%

profile of v8, /device:TPU:0, one launch (start us, length us, event | category | flops | bytes accessed | tf_op | source)
XLA Modules:
  0.0 83.5 jit_solution(15769579397379085875)
XLA Ops:
  0.7 0.8 %select_bitcast_fusion = bf16[1,16,1152]{2,1,0:T(8,128)(2,1)S(1)} fusion(bf16[16,512]{1,0:T(8,128)(2,1)} %param.19, bf16[16,512]{1,0:T(8,128)(2,1)} %param.16, pred[1152]{0:T(1024)(128)(4,1)S(1)} %get-tuple-element.52, pred[1152]{0:T(1024)(128)(4,1)S(1)} %get-tuple-element.53, pred[1152]{0:T(1024)(128)(4,1)S(1)} %get-tuple-element.54, ...), kind=kLoop, calls=%fused_computation.7 | loop fusion | flops 92160 | bytes 75520 | tf_op jit(solution)/shard_map/broadcast_in_dim | solution.py:402
  1.5 5.1 %collective-permute-start.2 = (bf16[1,16,1152]{2,1,0:T(8,128)(2,1)S(1)}, bf16[1,16,1152]{2,1,0:T(8,128)(2,1)S(1)}, u32[]{:S(2)}, u32[]{:S(2)}) collective-permute-start(bf16[1,16,1152]{2,1,0:T(8,128)(2,1)S(1)} %select_bitcast_fusion), channel_id=1, source_target_pairs={{0,6},{1,7},{2,4},{3,5},{4,2},{5,3},{6,0},{7,1},{8,14},{9,15},{10,... | collective-permute-start | bytes 110600 | tf_op jit(solution)/shard_map/ppermute | solution.py:365
  6.6 0.0 collective-permute-start.1
  6.6 0.6 collective-permute-start
  7.3 1.3 %collective-permute-done.2 = bf16[1,16,1152]{2,1,0:T(8,128)(2,1)S(1)} collective-permute-done((bf16[1,16,1152]{2,1,0:T(8,128)(2,1)S(1)}, bf16[1,16,1152]{2,1,0:T(8,128)(2,1)S(1)}, u32[]{:S(2)}, u32[]{:S(2)}) %collective-permute-start.2) | collective-permute-done | bytes 36896 | tf_op jit(solution)/shard_map/ppermute | solution.py:365
  8.6 2.9 %collective-permute-done.1 = bf16[1,16,1152]{2,1,0:T(8,128)(2,1)S(1)} collective-permute-done((bf16[1,16,1152]{2,1,0:T(8,128)(2,1)S(1)}, bf16[1,16,1152]{2,1,0:T(8,128)(2,1)S(1)}, u32[]{:S(2)}, u32[]{:S(2)}) %collective-permute-start.1) | collective-permute-done | bytes 36896 | tf_op jit(solution)/shard_map/ppermute | solution.py:365
  11.5 0.0 collective-permute-done
  11.5 2.5 %collective-permute-start.5 = (bf16[4,16,1152]{2,1,0:T(8,128)(2,1)S(1)}, bf16[4,16,1152]{2,1,0:T(8,128)(2,1)S(1)}, u32[]{:S(2)}, u32[]{:S(2)}) collective-permute-start(bf16[4,16,1152]{2,1,0:T(8,128)(2,1)S(1)} %pad_maximum_fusion.mine_ref), channel_id=1, source_target_pairs={{0,17},{1,16},{2,19},{3,18},{4,21},{5,20},{6,23},{7,22},{8,25},{9,... | collective-permute-start | bytes 442376 | tf_op jit(solution)/shard_map/ppermute | solution.py:365
  14.0 0.5 collective-permute-start.4
  14.6 0.5 collective-permute-start.3
  15.1 0.1 pad_add_fusion.place_ref.refs_0_
  15.2 0.0 copy-start
  15.2 0.7 copy-done
  15.8 0.0 copy-start.1
  15.8 0.7 copy-done.1
  16.5 0.7 copy-done.2
  17.1 1.0 %point_weight.1 = (f32[96,128]{1,0:T(8,128)S(1)}, bf16[4,16,1152]{2,1,0:T(8,128)(2,1)S(1)}) custom-call(s32[2]{0:T(128)S(1)} %pad_add_fusion.place_ref.refs_0_, s32[13]{0:T(128)S(1)} %copy-done, s32[64]{0:T(128)S(1)} %copy-done.1, s32[64]{0:T(128)S(1)} %copy-done.2, bf16[4,16,1152]{2,1,0:T(8,128)(2,1)S(1)} %pad_maximum_fusion.mine_ref), custom_call_target="tpu_custom_call" | custom-call | flops 75366400 | bytes 3014656 | tf_op jit(solution)/shard_map/point_weight/pallas_call | solution.py:59
  18.1 0.1 collective-permute-start.6
  18.2 0.0 collective-permute-done.5.refs_4_
  18.2 0.5 collective-permute-start.9
  18.7 1.2 %collective-permute-done.4.refs_3_ = bf16[4,16,1152]{2,1,0:T(8,128)(2,1)S(1)} collective-permute-done((bf16[4,16,1152]{2,1,0:T(8,128)(2,1)S(1)}, bf16[4,16,1152]{2,1,0:T(8,128)(2,1)S(1)}, u32[]{:S(2)}, u32[]{:S(2)}) %collective-permute-start.4) | collective-permute-done | bytes 147488 | tf_op jit(solution)/shard_map/ppermute | solution.py:365
  19.9 0.0 collective-permute-start.8
  19.9 0.0 collective-permute-done.3.refs_2_
  19.9 0.5 collective-permute-start.7
  20.4 0.0 collective-permute-done.6.refs_5_
  20.4 0.0 collective-permute-done.9.refs_8_
  20.4 0.9 %collective-permute-done.8.refs_7_ = bf16[4,16,1152]{2,1,0:T(8,128)(2,1)S(1)} collective-permute-done((bf16[4,16,1152]{2,1,0:T(8,128)(2,1)S(1)}, bf16[4,16,1152]{2,1,0:T(8,128)(2,1)S(1)}, u32[]{:S(2)}, u32[]{:S(2)}) %collective-permute-start.8) | collective-permute-done | bytes 147488 | tf_op jit(solution)/shard_map/ppermute | solution.py:365
  21.2 0.2 collective-permute-done.7.refs_6_
  21.5 39.8 %layers.1 = (bf16[11776,512]{1,0:T(8,128)(2,1)}, bf16[11776,512]{1,0:T(8,128)(2,1)S(1)}, bf16[512,512]{1,0:T(8,128)(2,1)S(1)}, f32[16,16,1152]{2,1,0:T(8,128)S(1)}, bf16[16,16,1152]{2,1,0:T(8,128)(2,1)S(1)}) custom-call(s32[2]{0:T(128)S(1)} %pad_add_fusion.place_ref.refs_0_, bf16[4,16,1152]{2,1,0:T(8,128)(2,1)S(1)} %get-tuple-element.25.refs_1_, ...), custom_call_target="tpu_custom_call" | custom-call | tf_op jit(solution)/shard_map/layers/pallas_call | solution.py:300
  61.3 0.4 collective-permute-start.10
  61.6 1.7 %collective-permute-done.10 = bf16[16,16,1152]{2,1,0:T(8,128)(2,1)S(1)} collective-permute-done((bf16[16,16,1152]{2,1,0:T(8,128)(2,1)S(1)}, bf16[16,16,1152]{2,1,0:T(8,128)(2,1)S(1)}, u32[]{:S(2)}, u32[]{:S(2)}) %collective-permute-start.10) | collective-permute-done | bytes 589856 | tf_op jit(solution)/shard_map/ppermute | solution.py:365
  63.3 0.2 fusion.1
  63.5 1.3 %collective-permute-start.11 = (bf16[4,16,1152]{2,1,0:T(8,128)(2,1)S(1)}, bf16[4,16,1152]{2,1,0:T(8,128)(2,1)S(1)}, u32[]{:S(2)}, u32[]{:S(2)}) collective-permute-start(bf16[4,16,1152]{2,1,0:T(8,128)(2,1)S(1)} %get-tuple-element.46), channel_id=1, source_target_pairs={{0,1},{1,0},{2,3},{3,2},{4,5},{5,4},{6,7},{7,6},{8,9},{9,8},{10,11... | collective-permute-start | bytes 442376 | tf_op jit(solution)/shard_map/ppermute | solution.py:365
  64.9 1.7 %collective-permute-start.13 = (bf16[4,16,1152]{2,1,0:T(8,128)(2,1)S(1)}, bf16[4,16,1152]{2,1,0:T(8,128)(2,1)S(1)}, u32[]{:S(2)}, u32[]{:S(2)}) collective-permute-start(bf16[4,16,1152]{2,1,0:T(8,128)(2,1)S(1)} %get-tuple-element.47), channel_id=1, source_target_pairs={{0,17},{1,16},{2,19},{3,18},{4,21},{5,20},{6,23},{7,22},{8,25},{9,... | collective-permute-start | bytes 442376 | tf_op jit(solution)/shard_map/ppermute | solution.py:365
  66.6 0.5 collective-permute-start.12
  67.1 6.4 %input_grad.2 = (bf16[11776,512]{1,0:T(8,128)(2,1)}, f32[4,16,1152]{2,1,0:T(8,128)S(1)}) custom-call(bf16[11776,512]{1,0:T(8,128)(2,1)S(1)} %get-tuple-element.28.grad_ref, bf16[512,512]{1,0:T(8,128)(2,1)S(1)} %get-tuple-element.29.w_ref, f32[4,16,1152]{2,1,0:T(8,128)S(1)} %slice.38.held_ref), custom_call_target="tpu_custom_call" | custom-call | flops 3858759680 | bytes 15073280 | tf_op jit(solution)/shard_map/input_grad/pallas_call | solution.py:93
  73.5 0.0 collective-permute-done.11
  73.5 0.0 collective-permute-done.13
  73.5 0.6 collective-permute-done.12
  74.1 0.1 fusion
  74.2 2.0 %collective-permute-start.16 = (bf16[16,1152]{1,0:T(8,128)(2,1)S(1)}, bf16[16,1152]{1,0:T(8,128)(2,1)S(1)}, u32[]{:S(2)}, u32[]{:S(2)}) collective-permute-start(bf16[16,1152]{1,0:T(8,128)(2,1)S(1)} %get-tuple-element.49), channel_id=1, source_target_pairs={{0,6},{1,7},{2,4},{3,5},{4,2},{5,3},{6,0},{7,1},{8,14},{9,15},{10,... | collective-permute-start | bytes 110600 | tf_op jit(solution)/shard_map/ppermute | solution.py:365
  76.1 0.2 collective-permute-start.15
  76.3 2.3 %collective-permute-start.14 = (bf16[16,1152]{1,0:T(8,128)(2,1)S(1)}, bf16[16,1152]{1,0:T(8,128)(2,1)S(1)}, u32[]{:S(2)}, u32[]{:S(2)}) collective-permute-start(bf16[16,1152]{1,0:T(8,128)(2,1)S(1)} %get-tuple-element.51), channel_id=1, source_target_pairs={{0,2},{1,3},{2,0},{3,1},{4,6},{5,7},{6,4},{7,5},{8,10},{9,11},{10,... | collective-permute-start | bytes 110600 | tf_op jit(solution)/shard_map/ppermute | solution.py:365
  78.6 4.2 %input_grad.3 = (bf16[11776,512]{1,0:T(8,128)(2,1)}, f32[16,1152]{1,0:T(8,128)S(1)}) custom-call(bf16[11776,512]{1,0:T(8,128)(2,1)S(1)} %get-tuple-element.28.grad_ref, bf16[512,512]{1,0:T(8,128)(2,1)S(1)} %get-tuple-element.29.w_ref, f32[16,1152]{1,0:T(8,128)S(1)} %slice_bitcast_fusion.held_ref, ...), custom_call_target="tpu_custom_call", output_to_operand_aliasing={{0}: (3, {})} | custom-call | flops 2315255808 | bytes 9043968 | tf_op jit(solution)/shard_map/input_grad/pallas_call | solution.py:93
  82.8 0.0 collective-permute-done.16.refs_3_
  82.8 0.0 collective-permute-done.15.refs_2_
  82.8 0.0 collective-permute-done.14.refs_1_
  82.9 0.7 last.1
  (9 shorter events, 0.1 us)
Async XLA Ops:
  1.5 7.1 %collective-permute-start.2 = (bf16[1,16,1152]{2,1,0:T(8,128)(2,1)S(1)}, bf16[1,16,1152]{2,1,0:T(8,128)(2,1)S(1)}, u32[]{:S(2)}, u32[]{:S(2)}) collective-permute-start(bf16[1,16,1152]{2,1,0:T(8,128)(2,1)S(1)} %select_bitcast_fusion), channel_id=1, source_target_pairs={{0,6},{1,7},{2,4},{3,5},{4,2},{5,3},{6,0},{7,1},{8,14},{9,15},{10,... | collective-permute-start | bytes 110600 | tf_op jit(solution)/shard_map/ppermute | solution.py:365
  6.6 4.9 %collective-permute-start.1 = (bf16[1,16,1152]{2,1,0:T(8,128)(2,1)S(1)}, bf16[1,16,1152]{2,1,0:T(8,128)(2,1)S(1)}, u32[]{:S(2)}, u32[]{:S(2)}) collective-permute-start(bf16[1,16,1152]{2,1,0:T(8,128)(2,1)S(1)} %select_bitcast_fusion), channel_id=1, source_target_pairs={{0,4},{1,5},{2,6},{3,7},{4,0},{5,1},{6,2},{7,3},{8,12},{9,13},{10,... | collective-permute-start | bytes 110600 | tf_op jit(solution)/shard_map/ppermute | solution.py:365
  6.6 4.9 %collective-permute-start = (bf16[1,16,1152]{2,1,0:T(8,128)(2,1)S(1)}, bf16[1,16,1152]{2,1,0:T(8,128)(2,1)S(1)}, u32[]{:S(2)}, u32[]{:S(2)}) collective-permute-start(bf16[1,16,1152]{2,1,0:T(8,128)(2,1)S(1)} %select_bitcast_fusion), channel_id=1, source_target_pairs={{0,2},{1,3},{2,0},{3,1},{4,6},{5,7},{6,4},{7,5},{8,10},{9,11},{10,... | collective-permute-start | bytes 110600 | tf_op jit(solution)/shard_map/ppermute | solution.py:365
  11.5 6.7 %collective-permute-start.5 = (bf16[4,16,1152]{2,1,0:T(8,128)(2,1)S(1)}, bf16[4,16,1152]{2,1,0:T(8,128)(2,1)S(1)}, u32[]{:S(2)}, u32[]{:S(2)}) collective-permute-start(bf16[4,16,1152]{2,1,0:T(8,128)(2,1)S(1)} %pad_maximum_fusion.mine_ref), channel_id=1, source_target_pairs={{0,17},{1,16},{2,19},{3,18},{4,21},{5,20},{6,23},{7,22},{8,25},{9,... | collective-permute-start | bytes 442376 | tf_op jit(solution)/shard_map/ppermute | solution.py:365
  14.0 5.8 %collective-permute-start.4 = (bf16[4,16,1152]{2,1,0:T(8,128)(2,1)S(1)}, bf16[4,16,1152]{2,1,0:T(8,128)(2,1)S(1)}, u32[]{:S(2)}, u32[]{:S(2)}) collective-permute-start(bf16[4,16,1152]{2,1,0:T(8,128)(2,1)S(1)} %pad_maximum_fusion.mine_ref), channel_id=1, source_target_pairs={{0,16},{1,17},{2,18},{3,19},{4,20},{5,21},{6,22},{7,23},{8,24},{9,... | collective-permute-start | bytes 442376 | tf_op jit(solution)/shard_map/ppermute | solution.py:365
  14.6 5.3 %collective-permute-start.3 = (bf16[4,16,1152]{2,1,0:T(8,128)(2,1)S(1)}, bf16[4,16,1152]{2,1,0:T(8,128)(2,1)S(1)}, u32[]{:S(2)}, u32[]{:S(2)}) collective-permute-start(bf16[4,16,1152]{2,1,0:T(8,128)(2,1)S(1)} %pad_maximum_fusion.mine_ref), channel_id=1, source_target_pairs={{0,1},{1,0},{2,3},{3,2},{4,5},{5,4},{6,7},{7,6},{8,9},{9,8},{10,11... | collective-permute-start | bytes 442376 | tf_op jit(solution)/shard_map/ppermute | solution.py:365
  15.2 0.7 copy-start
  15.8 0.7 copy-start.1
  16.5 0.7 copy-start.2
  18.1 2.3 %collective-permute-start.6 = (bf16[4,16,1152]{2,1,0:T(8,128)(2,1)S(1)}, bf16[4,16,1152]{2,1,0:T(8,128)(2,1)S(1)}, u32[]{:S(2)}, u32[]{:S(2)}) collective-permute-start(bf16[4,16,1152]{2,1,0:T(8,128)(2,1)S(1)} %get-tuple-element.25.refs_1_), channel_id=1, source_target_pairs={{0,8},{1,9},{2,10},{3,11},{4,12},{5,13},{6,14},{7,15},{8,0},{9,1},... | collective-permute-start | bytes 442376 | tf_op jit(solution)/shard_map/ppermute | solution.py:365
  18.2 2.2 %collective-permute-start.9 = (bf16[4,16,1152]{2,1,0:T(8,128)(2,1)S(1)}, bf16[4,16,1152]{2,1,0:T(8,128)(2,1)S(1)}, u32[]{:S(2)}, u32[]{:S(2)}) collective-permute-start(bf16[4,16,1152]{2,1,0:T(8,128)(2,1)S(1)} %collective-permute-done.5.refs_4_), channel_id=1, source_target_pairs={{0,8},{1,9},{2,10},{3,11},{4,12},{5,13},{6,14},{7,15},{8,0},{9,1},... | collective-permute-start | bytes 442376 | tf_op jit(solution)/shard_map/ppermute | solution.py:365
  19.9 1.4 %collective-permute-start.8 = (bf16[4,16,1152]{2,1,0:T(8,128)(2,1)S(1)}, bf16[4,16,1152]{2,1,0:T(8,128)(2,1)S(1)}, u32[]{:S(2)}, u32[]{:S(2)}) collective-permute-start(bf16[4,16,1152]{2,1,0:T(8,128)(2,1)S(1)} %collective-permute-done.4.refs_3_), channel_id=1, source_target_pairs={{0,8},{1,9},{2,10},{3,11},{4,12},{5,13},{6,14},{7,15},{8,0},{9,1},... | collective-permute-start | bytes 442376 | tf_op jit(solution)/shard_map/ppermute | solution.py:365
  19.9 1.6 %collective-permute-start.7 = (bf16[4,16,1152]{2,1,0:T(8,128)(2,1)S(1)}, bf16[4,16,1152]{2,1,0:T(8,128)(2,1)S(1)}, u32[]{:S(2)}, u32[]{:S(2)}) collective-permute-start(bf16[4,16,1152]{2,1,0:T(8,128)(2,1)S(1)} %collective-permute-done.3.refs_2_), channel_id=1, source_target_pairs={{0,8},{1,9},{2,10},{3,11},{4,12},{5,13},{6,14},{7,15},{8,0},{9,1},... | collective-permute-start | bytes 442376 | tf_op jit(solution)/shard_map/ppermute | solution.py:365
  61.3 2.1 %collective-permute-start.10 = (bf16[16,16,1152]{2,1,0:T(8,128)(2,1)S(1)}, bf16[16,16,1152]{2,1,0:T(8,128)(2,1)S(1)}, u32[]{:S(2)}, u32[]{:S(2)}) collective-permute-start(bf16[16,16,1152]{2,1,0:T(8,128)(2,1)S(1)} %get-tuple-element.31), channel_id=1, source_target_pairs={{0,8},{1,9},{2,10},{3,11},{4,12},{5,13},{6,14},{7,15},{8,0},{9,1},... | collective-permute-start | bytes 1769480 | tf_op jit(solution)/shard_map/ppermute | solution.py:365
  63.5 10.0 %collective-permute-start.11 = (bf16[4,16,1152]{2,1,0:T(8,128)(2,1)S(1)}, bf16[4,16,1152]{2,1,0:T(8,128)(2,1)S(1)}, u32[]{:S(2)}, u32[]{:S(2)}) collective-permute-start(bf16[4,16,1152]{2,1,0:T(8,128)(2,1)S(1)} %get-tuple-element.46), channel_id=1, source_target_pairs={{0,1},{1,0},{2,3},{3,2},{4,5},{5,4},{6,7},{7,6},{8,9},{9,8},{10,11... | collective-permute-start | bytes 442376 | tf_op jit(solution)/shard_map/ppermute | solution.py:365
  64.9 8.6 %collective-permute-start.13 = (bf16[4,16,1152]{2,1,0:T(8,128)(2,1)S(1)}, bf16[4,16,1152]{2,1,0:T(8,128)(2,1)S(1)}, u32[]{:S(2)}, u32[]{:S(2)}) collective-permute-start(bf16[4,16,1152]{2,1,0:T(8,128)(2,1)S(1)} %get-tuple-element.47), channel_id=1, source_target_pairs={{0,17},{1,16},{2,19},{3,18},{4,21},{5,20},{6,23},{7,22},{8,25},{9,... | collective-permute-start | bytes 442376 | tf_op jit(solution)/shard_map/ppermute | solution.py:365
  66.6 7.5 %collective-permute-start.12 = (bf16[4,16,1152]{2,1,0:T(8,128)(2,1)S(1)}, bf16[4,16,1152]{2,1,0:T(8,128)(2,1)S(1)}, u32[]{:S(2)}, u32[]{:S(2)}) collective-permute-start(bf16[4,16,1152]{2,1,0:T(8,128)(2,1)S(1)} %get-tuple-element.48), channel_id=1, source_target_pairs={{0,16},{1,17},{2,18},{3,19},{4,20},{5,21},{6,22},{7,23},{8,24},{9,... | collective-permute-start | bytes 442376 | tf_op jit(solution)/shard_map/ppermute | solution.py:365
  74.2 8.7 %collective-permute-start.16 = (bf16[16,1152]{1,0:T(8,128)(2,1)S(1)}, bf16[16,1152]{1,0:T(8,128)(2,1)S(1)}, u32[]{:S(2)}, u32[]{:S(2)}) collective-permute-start(bf16[16,1152]{1,0:T(8,128)(2,1)S(1)} %get-tuple-element.49), channel_id=1, source_target_pairs={{0,6},{1,7},{2,4},{3,5},{4,2},{5,3},{6,0},{7,1},{8,14},{9,15},{10,... | collective-permute-start | bytes 110600 | tf_op jit(solution)/shard_map/ppermute | solution.py:365
  76.1 6.7 %collective-permute-start.15 = (bf16[16,1152]{1,0:T(8,128)(2,1)S(1)}, bf16[16,1152]{1,0:T(8,128)(2,1)S(1)}, u32[]{:S(2)}, u32[]{:S(2)}) collective-permute-start(bf16[16,1152]{1,0:T(8,128)(2,1)S(1)} %get-tuple-element.50), channel_id=1, source_target_pairs={{0,4},{1,5},{2,6},{3,7},{4,0},{5,1},{6,2},{7,3},{8,12},{9,13},{10,... | collective-permute-start | bytes 110600 | tf_op jit(solution)/shard_map/ppermute | solution.py:365
  76.3 6.5 %collective-permute-start.14 = (bf16[16,1152]{1,0:T(8,128)(2,1)S(1)}, bf16[16,1152]{1,0:T(8,128)(2,1)S(1)}, u32[]{:S(2)}, u32[]{:S(2)}) collective-permute-start(bf16[16,1152]{1,0:T(8,128)(2,1)S(1)} %get-tuple-element.51), channel_id=1, source_target_pairs={{0,2},{1,3},{2,0},{3,1},{4,6},{5,7},{6,4},{7,5},{8,10},{9,11},{10,... | collective-permute-start | bytes 110600 | tf_op jit(solution)/shard_map/ppermute | solution.py:365
